TPU v7x, 256 devices: a whole 4x4x8 slice. The times are simulated.
256 devices in a mesh: group: 32 (over z, y), dom: 8 (over x, core).
Axes of the slice: x: 4, y: 4, z: 8, core: 2. Of those that a mesh axis runs over, the one named last changes fastest.
Arguments:
- blocks: bfloat16 [6656, 11, 128, 128], P(('group', 'dom')), may hold values from -0.5 to 0.5
- columns: int32 [6656, 11], P(('group', 'dom')), may hold values from 0 to 63, as said below
- sends: int32 [9728], P(('group', 'dom')), may hold values from 0 to 25, as said below
- active_row_count: int32 [256], P(('group', 'dom')), may hold values from 8 to 26, as said below
- degree: float32 [6656, 128], P(('group', 'dom')), may hold values from 1 to 16
- start: float32 [6656, 128, 128], P(('group', 'dom')), may hold values from -6 to 6
Outputs:
- basis: float32 [6656, 128, 128], P(('group', 'dom'))
- factor: float32 [128, 128], replicated
Inputs may be any that keep to these rules, and one draw needn't show every extreme that they name: `active_row_count`: some device holds exactly 26 live slots in every draw; slots from the count on are dead. `columns`: position 0 of a slot is the slot itself; a live slot's other positions name live own slots or halo entries of the extended list, and every halo entry is named by some live slot. `sends`: each names a live slot of the sending device.
All inputs are finite; a program needn't handle non-finite values.
Results may differ from a plain program's by a relative error of at most 0.004.
Values may be sent and summed in bfloat16 or wider, within the bound.
No kernel may reach another device: no remote copies, remote signals or barrier semaphores. Data moves between devices by JAX's collectives and lax.ppermute only.
A program may use at most 128 MiB of HBM per device.

v0:
```python
import jax
import jax.numpy as jnp
from jax import lax
from jax.sharding import PartitionSpec as P

ITERS = 2


def from_behind(shard, axis, by):
    size = lax.axis_size(axis)
    return lax.ppermute(shard, axis, [(i, (i + by) % size) for i in range(size)])


def from_behind_2(block, axis, distance):
    devices = range(lax.axis_size(axis))
    route = [(i - distance, i) for i in devices if i - distance in devices]
    return lax.ppermute(block, axis, route)


def halo_operand(operand, sends):
    width_slab = operand.shape[0] // 2
    width_part = operand.shape[0] // 4
    to_next = jnp.take(operand, sends[:width_slab], axis=0)
    to_prev = jnp.take(operand, sends[width_slab : 2 * width_slab], axis=0)
    to_right = jnp.take(operand, sends[2 * width_slab : 2 * width_slab + width_part], axis=0)
    to_left = jnp.take(operand, sends[2 * width_slab + width_part :], axis=0)
    from_below = from_behind(to_next, "group", 1)
    from_above = from_behind(to_prev, "group", -1)
    from_left = from_behind_2(to_right, "dom", 1)
    from_right = from_behind_2(to_left, "dom", -1)
    return jnp.concatenate([operand, from_below, from_above, from_left, from_right], axis=0)


def summed_gram(local):
    return lax.psum(local, ("group", "dom"))


def body(blocks, columns, sends, active_row_count, degree, start):
    highest = lax.Precision.HIGHEST
    slots = blocks.shape[0]
    nodes = blocks.shape[2]
    width = start.shape[2]
    denominator = jnp.float32(lax.axis_size("group") * lax.axis_size("dom") * slots * nodes)
    active_rows = (jnp.arange(slots, dtype=jnp.int32) < active_row_count[0])[:, None, None]
    scale = lax.rsqrt(degree)
    current = jnp.where(active_rows, start, jnp.float32(0.0))
    identity = jnp.eye(width, dtype=jnp.float32)
    factor = jnp.zeros((width, width), jnp.float32)
    for step in range(ITERS):
        operand = (scale[:, :, None] * current).astype(jnp.bfloat16)
        extended = halo_operand(operand, sends)
        gathered = jnp.take(extended, columns, axis=0)
        matrix_product = jnp.einsum(
            "skij,skjc->sic", blocks, gathered, preferred_element_type=jnp.float32
        )
        operator_image = jnp.where(
            active_rows, current + scale[:, :, None] * matrix_product, jnp.float32(0.0)
        )
        local = jnp.einsum("qhp,qhz->pz", operator_image, operator_image, precision=highest)
        gram_matrix = summed_gram(local) / denominator
        factor = jnp.linalg.cholesky(gram_matrix)
        inverse = jax.scipy.linalg.solve_triangular(factor, identity, lower=True)
        current = jnp.einsum("sic,dc->sid", operator_image, inverse, precision=highest)
    return (current, factor)


def solution(mesh):
    return jax.shard_map(
        body,
        mesh=mesh,
        in_specs=(
            P(("group", "dom"), None, None, None),
            P(("group", "dom"), None),
            P(("group", "dom")),
            P(("group", "dom")),
            P(("group", "dom"), None),
            P(("group", "dom"), None, None),
        ),
        out_specs=(P(("group", "dom"), None, None), P()),
        check_vma=False,
    )
```

profile of v0, /device:TPU:1, one launch (start us, length us, event | category | flops | bytes accessed | tf_op | source)
XLA Modules:
  0.0 643.1 jit_solution(8968248428599028099)
XLA Ops:
  8.6 2.7 copy.21
  11.4 1.7 constant_dynamic-update-slice_fusion.4
  14.7 2.1 collective-permute-start
  18.3 6.7 %collective-permute-start.1 = (bf16[13,128,128]{1,2,0:T(8,128)(2,1)}, bf16[13,128,128]{1,2,0:T(8,128)(2,1)}, u32[]{:S(2)}, u32[]{:S(2)}) collective-permute-start(bf16[13,128,128]{1,2,0:T(8,128)(2,1)} %broadcast_select_fusion.1), channel_id=1, source_target_pairs={{0,248},{8,0},{16,8},{24,16},{32,24},{40,32},{48,40},{56,48},{64,5... | collective-permute-start | bytes 1277960 | tf_op jit(solution)/shard_map/ppermute | solution.py:11
  25.8 4.0 collective-permute-start.2
  30.5 1.9 collective-permute-start.3
  33.4 1.1 constant_dynamic-update-slice_fusion.3
  34.4 1.1 constant_dynamic-update-slice_fusion.2
  37.5 10.3 %gather_fusion.4 = bf16[286,128,128]{1,2,0:T(8,128)(2,1)} fusion(bf16[64,128,128]{1,2,0:T(8,128)(2,1)S(1)} %constant_dynamic-update-slice_fusion, s32[1024]{0:T(1024)S(1)} %pad_clamp_fusion), kind=kCustom, calls=%fused_computation.2.clone | custom fusion | bytes 18744440 | tf_op jit(solution)/shard_map/jit(_take)/gather | solution.py:52
  47.8 9.7 %fusion.9 = f32[26,128,128]{1,2,0:T(8,128)S(1)} fusion(f32[26,128,128]{1,2,0:T(8,128)} %copy.21, bf16[26,11,128,128]{3,2,1,0:T(8,128)(2,1)} %param.15, bf16[26,11,128,128]{2,3,1,0:T(8,128)(2,1)} %bitcast.59, pred[26,11]{1,0:T(8,128)(4,1)S(1)} %copy.22, f32[26,128]{1,0:T(8,128)S(1)} %rsqrt.3, pred[26]{0:T(512)(128)(4,1)S(1)} %iota_compare_fusion.4), kind=kOutput, calls=%fused_computation.22 | convolution fusion | flops 1205960704 | bytes 22164792 | tf_op jit(solution)/shard_map/skij,skjc->sic/dot_general | solution.py:53
  57.6 2.1 convolution_bitcast_fusion.1
  60.0 237.4 %all-reduce.3.cloned.1.call-done = f32[128,128]{0,1:T(8,128)} async-done(((f32[128,128]{0,1:T(8,128)}), f32[128,128]{0,1:T(8,128)}) %all-reduce.3.cloned.1.call-update) | async-done | bytes 65552 | tf_op jit(solution)/shard_map/psum | solution.py:35
  299.2 11.7 %cholesky.44 = f32[128,128]{1,0:T(8,128)S(1)} custom-call(f32[128,128]{1,0:T(8,128)S(1)} %fusion.20), custom_call_target="Cholesky" | custom-call | tf_op jit(solution)/shard_map/jit(cholesky)/cholesky | solution.py:61
  312.3 9.8 %custom-call.6 = f32[1,128,128]{1,2,0:T(8,128)S(1)} custom-call(f32[1,128,128]{2,1,0:T(8,128)S(1)} %fusion.16), custom_call_target="InvertDiagBlocksLowerTriangular" | custom-call | tf_op jit(solution)/shard_map/jit(_solve_triangular)/triangular_solve | solution.py:62
  322.4 4.4 constant_dynamic-update-slice_fusion.9
  326.8 1.4 gather_fusion.5
  328.8 1.3 gather_fusion.7
  330.0 1.9 broadcast_select_fusion.2
  333.3 4.2 collective-permute-start.5
  339.2 3.1 collective-permute-start.6
  342.4 1.9 collective-permute-start.7
  344.3 2.8 collective-permute-done.4
  347.1 1.1 constant_dynamic-update-slice_fusion.8
  348.2 1.1 constant_dynamic-update-slice_fusion.7
  349.4 10.4 %gather_fusion.9 = bf16[286,128,128]{1,2,0:T(8,128)(2,1)} fusion(bf16[64,128,128]{1,2,0:T(8,128)(2,1)S(1)} %constant_dynamic-update-slice_fusion.5, s32[1024]{0:T(1024)S(1)} %pad_clamp_fusion), kind=kCustom, calls=%fused_computation.9.clone | custom fusion | bytes 18744440 | tf_op jit(solution)/shard_map/jit(_take)/gather | solution.py:52
  359.8 9.8 %fusion.8 = f32[26,128,128]{1,2,0:T(8,128)S(1)} fusion(f32[26,128,128]{1,2,0:T(8,128)} %get-tuple-element.25, bf16[26,11,128,128]{3,2,1,0:T(8,128)(2,1)} %param.15, bf16[26,11,128,128]{2,3,1,0:T(8,128)(2,1)} %bitcast.58, pred[26,11]{1,0:T(8,128)(4,1)S(1)} %copy.22, f32[26,128]{1,0:T(8,128)S(1)} %rsqrt.3, pred[26]{0:T(512)(128)(4,1)S(1)} %iota_compare_fusion.4), kind=kOutput, calls=%fused_computation.19 | convolution fusion | flops 1205534720 | bytes 22164792 | tf_op jit(solution)/shard_map/skij,skjc->sic/dot_general | solution.py:53
  369.5 2.1 convolution_bitcast_fusion
  371.7 235.0 %all-reduce.5.cloned.1.call-done = f32[128,128]{0,1:T(8,128)} async-done(((f32[128,128]{0,1:T(8,128)}), f32[128,128]{0,1:T(8,128)}) %all-reduce.5.cloned.1.call-update) | async-done | bytes 65552 | tf_op jit(solution)/shard_map/psum | solution.py:35
  608.5 11.7 %cholesky.55 = f32[128,128]{1,0:T(8,128)S(1)} custom-call(f32[128,128]{1,0:T(8,128)S(1)} %fusion.18), custom_call_target="Cholesky" | custom-call | tf_op jit(solution)/shard_map/jit(cholesky)/cholesky | solution.py:61
  620.9 1.3 select_bitcast_fusion
  622.2 9.8 %custom-call.7 = f32[1,128,128]{1,2,0:T(8,128)S(1)} custom-call(f32[1,128,128]{2,1,0:T(8,128)S(1)} %get-tuple-element.4), custom_call_target="InvertDiagBlocksLowerTriangular" | custom-call | tf_op jit(solution)/shard_map/jit(_solve_triangular)/triangular_solve | solution.py:62
  632.3 4.0 fusion.23
  (62 shorter events, 18.5 us)
Async XLA Ops:
  7.2 4.1 copy-start.2
  7.2 290.2 %all-reduce.3.cloned.1.call-start = ((), (), s32[]{:S(2)}) async-start(), calls=%async_computation | async-start | bytes 131072 | tf_op jit(solution)/shard_map/psum | solution.py:35
  13.8 18.6 %copy-start.1 = (s32[26,11]{0,1:T(8,128)S(1)}, s32[26,11]{0,1:T(8,128)}, u32[]{:S(2)}) copy-start(s32[26,11]{0,1:T(8,128)} %param.16) | copy-start | bytes 3436
  14.7 18.7 %collective-permute-start = (bf16[13,128,128]{1,2,0:T(8,128)(2,1)}, bf16[13,128,128]{1,2,0:T(8,128)(2,1)}, u32[]{:S(2)}, u32[]{:S(2)}) collective-permute-start(bf16[13,128,128]{1,2,0:T(8,128)(2,1)} %broadcast_select_fusion.3), channel_id=1, source_target_pairs={{0,8},{8,16},{16,24},{24,32},{32,40},{40,48},{48,56},{56,64},{64,7... | collective-permute-start | bytes 1277960 | tf_op jit(solution)/shard_map/ppermute | solution.py:11
  18.3 16.1 %collective-permute-start.1 = (bf16[13,128,128]{1,2,0:T(8,128)(2,1)}, bf16[13,128,128]{1,2,0:T(8,128)(2,1)}, u32[]{:S(2)}, u32[]{:S(2)}) collective-permute-start(bf16[13,128,128]{1,2,0:T(8,128)(2,1)} %broadcast_select_fusion.1), channel_id=1, source_target_pairs={{0,248},{8,0},{16,8},{24,16},{32,24},{40,32},{48,40},{56,48},{64,5... | collective-permute-start | bytes 1277960 | tf_op jit(solution)/shard_map/ppermute | solution.py:11
  25.8 9.7 %collective-permute-start.2 = (bf16[6,128,128]{1,2,0:T(8,128)(2,1)S(1)}, bf16[6,128,128]{1,2,0:T(8,128)(2,1)}, u32[]{:S(2)}, u32[]{:S(2)}) collective-permute-start(bf16[6,128,128]{1,2,0:T(8,128)(2,1)S(1)} %broadcast_select_fusion.7), channel_id=1, source_target_pairs={{0,1},{1,2},{2,3},{3,4},{4,5},{5,6},{6,7},{8,9},{9,10},{10,11},{11... | collective-permute-start | bytes 589832 | tf_op jit(solution)/shard_map/ppermute | solution.py:17
  30.5 7.0 %collective-permute-start.3 = (bf16[6,128,128]{1,2,0:T(8,128)(2,1)S(1)}, bf16[6,128,128]{1,2,0:T(8,128)(2,1)S(1)}, u32[]{:S(2)}, u32[]{:S(2)}) collective-permute-start(bf16[6,128,128]{1,2,0:T(8,128)(2,1)S(1)} %broadcast_select_fusion.5), channel_id=1, source_target_pairs={{1,0},{2,1},{3,2},{4,3},{5,4},{6,5},{7,6},{9,8},{10,9},{11,10},{12... | collective-permute-start | bytes 589832 | tf_op jit(solution)/shard_map/ppermute | solution.py:17
  57.6 254.7 %copy-start = (f32[26,128,128]{1,2,0:T(8,128)}, f32[26,128,128]{1,2,0:T(8,128)S(1)}, u32[]{:S(2)}) copy-start(f32[26,128,128]{1,2,0:T(8,128)S(1)} %fusion.9) | copy-start | bytes 5111812
  59.7 546.9 %all-reduce.5.cloned.1.call-start = ((), (), s32[]{:S(2)}) async-start(), calls=%async_computation.1 | async-start | bytes 131072 | tf_op jit(solution)/shard_map/psum | solution.py:35
  331.9 15.2 %collective-permute-start.4 = (bf16[13,128,128]{1,2,0:T(8,128)(2,1)}, bf16[13,128,128]{1,2,0:T(8,128)(2,1)}, u32[]{:S(2)}, u32[]{:S(2)}) collective-permute-start(bf16[13,128,128]{1,2,0:T(8,128)(2,1)} %broadcast_select_fusion.2), channel_id=1, source_target_pairs={{0,8},{8,16},{16,24},{24,32},{32,40},{40,48},{48,56},{56,64},{64,7... | collective-permute-start | bytes 1277960 | tf_op jit(solution)/shard_map/ppermute | solution.py:11
  333.3 14.8 %collective-permute-start.5 = (bf16[13,128,128]{1,2,0:T(8,128)(2,1)}, bf16[13,128,128]{1,2,0:T(8,128)(2,1)}, u32[]{:S(2)}, u32[]{:S(2)}) collective-permute-start(bf16[13,128,128]{1,2,0:T(8,128)(2,1)} %broadcast_select_fusion), channel_id=1, source_target_pairs={{0,248},{8,0},{16,8},{24,16},{32,24},{40,32},{48,40},{56,48},{64,5... | collective-permute-start | bytes 1277960 | tf_op jit(solution)/shard_map/ppermute | solution.py:11
  339.2 10.1 %collective-permute-start.6 = (bf16[6,128,128]{1,2,0:T(8,128)(2,1)S(1)}, bf16[6,128,128]{1,2,0:T(8,128)(2,1)S(1)}, u32[]{:S(2)}, u32[]{:S(2)}) collective-permute-start(bf16[6,128,128]{1,2,0:T(8,128)(2,1)S(1)} %broadcast_select_fusion.6), channel_id=1, source_target_pairs={{0,1},{1,2},{2,3},{3,4},{4,5},{5,6},{6,7},{8,9},{9,10},{10,11},{11... | collective-permute-start | bytes 589832 | tf_op jit(solution)/shard_map/ppermute | solution.py:17
  342.4 7.0 %collective-permute-start.7 = (bf16[6,128,128]{1,2,0:T(8,128)(2,1)S(1)}, bf16[6,128,128]{1,2,0:T(8,128)(2,1)S(1)}, u32[]{:S(2)}, u32[]{:S(2)}) collective-permute-start(bf16[6,128,128]{1,2,0:T(8,128)(2,1)S(1)} %broadcast_select_fusion.4), channel_id=1, source_target_pairs={{1,0},{2,1},{3,2},{4,3},{5,4},{6,5},{7,6},{9,8},{10,9},{11,10},{12... | collective-permute-start | bytes 589832 | tf_op jit(solution)/shard_map/ppermute | solution.py:17
Sparse Core Ops, SparseCore 0:
  59.9 237.5 all-reduce.2
  371.8 234.8 all-reduce.4
where the time goes:
time: 644 us; the launch traced here: 643 us
  waiting for transfers between devices  477 us (74%)
  other arithmetic  57.5 us (9%)
  local copies, waits for them, and re-layouts  36.2 us (6%)
  matrix products  32.7 us (5%)
  starting transfers between devices  24.8 us (4%)
  between operations  15 us (2%)
    psum x2, waiting for transfers between devices, summed_gram(): return lax.psum(local, ('group', 'dom'))  472 us
    another operation x6, other arithmetic, body(): factor = jnp.linalg.cholesky(gram_matrix)  24.8 us
    another operation x4, other arithmetic, body(): inverse = jax.scipy.linalg.solve_triangular(factor, identity, lower=True)  21.6 us
    gather x2, local copies, waits for them, and re-layouts, body(): gathered = jnp.take(extended, columns, axis=0)  20.7 us
    dot_general x2, matrix products, body(): jnp.einsum('skij,skjc->sic', blocks, gathered, preferred_element_type=jnp...  19.5 us
    ppermute x4, starting transfers between devices, from_behind(): lax.ppermute(shard, axis, [(i, (i + by) % size) for i in range(size)])  13.7 us
  transfers between devices with their start and end apart: 10, of which 6 were waited for; matrix products, arithmetic and copies ran while one was open for 2% of the time, Pallas kernels for 0%

commit v1 on v0

v1 whole, which is shorter than its diff:
```python
import functools
import jax
import jax.numpy as jnp
from jax import lax
from jax.experimental import pallas as pl
from jax.experimental.pallas import tpu as pltpu
from jax.sharding import PartitionSpec as P

AXES = ("group", "dom")
F32, BF16 = jnp.float32, jnp.bfloat16
VMEM_BYTES = 56 * 2**20
ANY = pl.BlockSpec(memory_space=pl.ANY)
SMEM = pl.BlockSpec(memory_space=pltpu.SMEM)
VMEM = pl.BlockSpec(memory_space=pltpu.VMEM)


def split3(x):
    high = x.astype(BF16)
    rest = x - high.astype(F32)
    mid = rest.astype(BF16)
    low = (rest - mid.astype(F32)).astype(BF16)
    return high, mid, low


def dot(a, b):
    return jnp.dot(a, b, preferred_element_type=F32)


def dot_rows(a, b):
    return lax.dot_general(a, b, (((0,), (0,)), ((), ())), preferred_element_type=F32)


def scale_columns(degree_ref, slot):
    row = lax.rsqrt(degree_ref[pl.ds(slot, 1), :])
    width = row.shape[1]
    return jnp.broadcast_to(row, (width, width)).T


def add_gram(image, wide_ref, side_ref):
    high, mid, low = split3(image)
    wide_ref[...] += dot_rows(high, jnp.concatenate([high, mid], axis=1))
    left = jnp.concatenate([high, mid * BF16(0.5)], axis=0)
    side_ref[...] += dot_rows(left, jnp.concatenate([low, mid], axis=0))


def finish_gram(wide_ref, side_ref):
    width = side_ref.shape[0]
    cross = wide_ref[:, width:] + side_ref[...]
    return wide_ref[:, :width] + (cross + cross.T)


def put_sends(out_refs, sends_ref, block_ref):
    base = 0
    for out_ref in out_refs:
        def put(j, carry, out_ref=out_ref, base=base):
            out_ref[j] = block_ref[sends_ref[base + j]]
            return carry
        lax.fori_loop(0, out_ref.shape[0], put, 0)
        base += out_ref.shape[0]


def prep_kernel(sends_ref, count_ref, degree_ref, start_ref, *refs):
    out_refs, operand_ref = refs[:4], refs[4]

    def scaled(s, carry):
        operand_ref[s] = (scale_columns(degree_ref, s) * start_ref[s]).astype(BF16)
        return carry
    lax.fori_loop(0, count_ref[0], scaled, 0)
    put_sends(out_refs, sends_ref, operand_ref)


def product_kernel(sending, columns_ref, sends_ref, count_ref, degree_ref, current_hbm,
                   blocks_hbm, halo0, halo1, halo2, halo3, image_ref, gram_ref, *refs):
    out_refs = refs[:4] if sending else ()
    (blocks_ref, ext_ref, current_ref, scale_ref, next_ref, wide_ref, side_ref,
     block_sems, halo_sems, current_sem) = refs[len(out_refs):]
    slots = image_ref.shape[0]
    per_row = blocks_ref.shape[1]
    count = count_ref[0]
    current_copy = pltpu.make_async_copy(current_hbm, current_ref, current_sem)
    current_copy.start()
    halo_copies, base = [], slots
    for i, halo in enumerate((halo0, halo1, halo2, halo3)):
        size = halo.shape[0]
        halo_copies.append(pltpu.make_async_copy(halo, ext_ref.at[pl.ds(base, size)], halo_sems.at[i]))
        halo_copies[-1].start()
        base += size

    def block_copy(s):
        return pltpu.make_async_copy(blocks_hbm.at[s], blocks_ref.at[s], block_sems.at[s])

    def begin(s, carry):
        block_copy(s).start()
        return carry
    lax.fori_loop(0, count, begin, 0)
    wide_ref[...] = jnp.zeros_like(wide_ref)
    side_ref[...] = jnp.zeros_like(side_ref)
    current_copy.wait()

    def own(s, carry):
        scale = scale_columns(degree_ref, s)
        scale_ref[s] = scale
        ext_ref[s] = (scale * current_ref[s]).astype(BF16)
        return carry
    lax.fori_loop(0, count, own, 0)
    for copy in halo_copies:
        copy.wait()

    def row(s, carry):
        block_copy(s).wait()
        left = jnp.concatenate([blocks_ref[s, k] for k in range(per_row)], axis=1)
        right = jnp.concatenate([ext_ref[columns_ref[s, k]] for k in range(per_row)], axis=0)
        scale = scale_ref[s]
        image = current_ref[s] + scale * dot(left, right)
        image_ref[s] = image
        add_gram(image, wide_ref, side_ref)
        if sending:
            next_ref[s] = (scale * image).astype(BF16)
        return carry
    lax.fori_loop(0, count, row, 0)

    def dead(s, carry):
        image_ref[s] = jnp.zeros(image_ref.shape[1:], F32)
        return carry
    lax.fori_loop(count, slots, dead, 0)
    gram_ref[...] = finish_gram(wide_ref, side_ref)
    if sending:
        put_sends(out_refs, sends_ref, next_ref)


def factorize(work_ref):
    size = work_ref.shape[0]
    step = 8
    sublane = lax.broadcasted_iota(jnp.int32, (step, size), 0)
    for top in range(0, size, step):
        rows = work_ref[top:top + step, :]
        main = [jnp.broadcast_to(rows[i:i + 1, :size], (step, size)) for i in range(step)]
        side = [jnp.broadcast_to(rows[i:i + 1, size:], (step, size)) for i in range(step)]
        entry = [[jnp.broadcast_to(main[i][:, top + k:top + k + 1], (step, size)) if k >= i else None
                  for k in range(step)] for i in range(step)]
        for j in range(step):
            inv = lax.rsqrt(entry[j][j])
            main[j] = main[j] * inv
            side[j] = side[j] * inv
            scaled = [entry[j][k] * inv if k > j else None for k in range(step)]
            for i in range(j + 1, step):
                for k in range(i, step):
                    entry[i][k] = entry[i][k] - scaled[i] * scaled[k]
                main[i] = main[i] - scaled[i] * main[j]
                side[i] = side[i] - scaled[i] * side[j]
        upper, inverse = main[0], side[0]
        for j in range(1, step):
            upper = jnp.where(sublane == j, main[j], upper)
            inverse = jnp.where(sublane == j, side[j], inverse)
        both = jnp.concatenate([upper, inverse], axis=1)
        work_ref[top:top + step, :] = both
        if top + step < size:
            h, m, l = split3(both)
            a, b, c = h[:, :size], m[:, :size], l[:, :size]
            left = jnp.concatenate([a, a, b, b, a, c], axis=0)
            right = jnp.concatenate([h, m, h, m, l, h], axis=0)
            update = dot_rows(left, right)
            work_ref[top + step:, :] -= update[top + step:, :]


def start_factor(gram, denominator, work_ref):
    size = work_ref.shape[0]
    rows = lax.broadcasted_iota(jnp.int32, (size, size), 0)
    columns = lax.broadcasted_iota(jnp.int32, (size, size), 1)
    work_ref[:, :size] = gram * F32(1.0 / denominator)
    work_ref[:, size:] = (rows == columns).astype(F32)
    factorize(work_ref)
    return rows, columns


def wide_weights(inverse, wide_ref):
    high, mid, _ = split3(inverse.T)
    half = jnp.concatenate([high, mid], axis=1)
    wide_ref[...] = jnp.concatenate([half, half], axis=0)


def times_weights(image, wide_ref):
    width = image.shape[1]
    high = image.astype(BF16)
    mid = (image - high.astype(F32)).astype(BF16)
    both = dot(jnp.concatenate([high, mid], axis=1), wide_ref[...])
    return both[:, :width] + both[:, width:]


def middle_kernel(denominator, parts, count_ref, *refs):
    gram_refs, image_hbm, image_ref, gram_ref = refs[:parts], refs[parts], refs[parts + 1], refs[parts + 2]
    work_ref, weights_ref, held_ref, wide_ref, side_ref, sem = refs[parts + 3:]
    count = count_ref[0]
    copy = pltpu.make_async_copy(image_hbm, held_ref, sem)
    copy.start()
    gram = functools.reduce(lambda a, b: a + b, [r[...] for r in gram_refs])
    start_factor(gram, denominator, work_ref)
    size = work_ref.shape[0]
    wide_weights(work_ref[:, size:], weights_ref)
    wide_ref[...] = jnp.zeros_like(wide_ref)
    side_ref[...] = jnp.zeros_like(side_ref)
    copy.wait()

    def row(s, carry):
        image = times_weights(held_ref[s], weights_ref)
        image_ref[s] = image
        add_gram(image, wide_ref, side_ref)
        return carry
    lax.fori_loop(0, count, row, 0)

    def dead(s, carry):
        image_ref[s] = jnp.zeros(image_ref.shape[1:], F32)
        return carry
    lax.fori_loop(count, image_ref.shape[0], dead, 0)
    gram_ref[...] = finish_gram(wide_ref, side_ref)


def last_kernel(denominator, parts, count_ref, *refs):
    gram_refs, image_hbm, basis_hbm, factor_ref = refs[:parts], refs[parts], refs[parts + 1], refs[parts + 2]
    work_ref, weights_ref, held_ref, basis_ref, sem, out_sems = refs[parts + 3:]
    slots = held_ref.shape[0]
    count = count_ref[0]
    copy = pltpu.make_async_copy(image_hbm, held_ref, sem)
    copy.start()
    gram = functools.reduce(lambda a, b: a + b, [r[...] for r in gram_refs])
    rows, columns = start_factor(gram, denominator, work_ref)
    size = work_ref.shape[0]
    wide_weights(work_ref[:, size:], weights_ref)
    copy.wait()

    def out_copy(s):
        return pltpu.make_async_copy(basis_ref.at[s], basis_hbm.at[s], out_sems.at[s])

    def row(s, carry):
        basis_ref[s] = times_weights(held_ref[s], weights_ref)
        out_copy(s).start()
        return carry
    lax.fori_loop(0, count, row, 0)

    def dead(s, carry):
        basis_ref[s] = jnp.zeros(basis_ref.shape[1:], F32)
        out_copy(s).start()
        return carry
    lax.fori_loop(count, slots, dead, 0)
    factor_ref[...] = jnp.where(rows <= columns, work_ref[:, :size], 0.0).T

    def finish(s, carry):
        out_copy(s).wait()
        return carry
    lax.fori_loop(0, slots, finish, 0)


def params():
    return pltpu.CompilerParams(vmem_limit_bytes=VMEM_BYTES)


def spread(shape_dtype):
    return jax.ShapeDtypeStruct(*shape_dtype)


def prep(sends, count, degree, start, sizes):
    slots, nodes, width = start.shape
    return pl.pallas_call(
        prep_kernel,
        out_shape=[spread(((n, nodes, width), BF16)) for n in sizes],
        in_specs=[SMEM, SMEM, VMEM, VMEM],
        out_specs=[VMEM] * 4,
        scratch_shapes=[pltpu.VMEM((slots, nodes, width), BF16)],
        compiler_params=params(),
        name="prep",
    )(sends, count, degree, start)


def product(columns, sends, count, degree, current, blocks, halos, sending):
    slots, nodes, width = current.shape
    sizes = [h.shape[0] for h in halos]
    out_shape = [spread((current.shape, F32)), spread(((width, width), F32))]
    if sending:
        out_shape += [spread(((n, nodes, width), BF16)) for n in sizes]
    return pl.pallas_call(
        functools.partial(product_kernel, sending),
        out_shape=out_shape,
        in_specs=[SMEM, SMEM, SMEM, VMEM] + [ANY] * 6,
        out_specs=[VMEM] * len(out_shape),
        scratch_shapes=[
            pltpu.VMEM(blocks.shape, BF16),
            pltpu.VMEM((slots + sum(sizes), nodes, width), BF16),
            pltpu.VMEM(current.shape, F32),
            pltpu.VMEM(current.shape, F32),
            pltpu.VMEM(current.shape, BF16),
            pltpu.VMEM((width, 2 * width), F32),
            pltpu.VMEM((width, width), F32),
            pltpu.SemaphoreType.DMA((slots,)),
            pltpu.SemaphoreType.DMA((4,)),
            pltpu.SemaphoreType.DMA(()),
        ],
        compiler_params=params(),
        name="product",
    )(columns, sends, count, degree, current, blocks, *halos)


def middle(parts, count, image, denominator):
    width = image.shape[2]
    return pl.pallas_call(
        functools.partial(middle_kernel, denominator, len(parts)),
        out_shape=[spread((image.shape, F32)), spread(((width, width), F32))],
        in_specs=[SMEM] + [VMEM] * len(parts) + [ANY],
        out_specs=[VMEM, VMEM],
        scratch_shapes=[
            pltpu.VMEM((width, 2 * width), F32),
            pltpu.VMEM((2 * width, 2 * width), BF16),
            pltpu.VMEM(image.shape, F32),
            pltpu.VMEM((width, 2 * width), F32),
            pltpu.VMEM((width, width), F32),
            pltpu.SemaphoreType.DMA(()),
        ],
        compiler_params=params(),
        name="middle",
    )(count, *parts, image)


def last(parts, count, image, denominator):
    width = image.shape[2]
    return pl.pallas_call(
        functools.partial(last_kernel, denominator, len(parts)),
        out_shape=[spread((image.shape, F32)), spread(((width, width), F32))],
        in_specs=[SMEM] + [VMEM] * len(parts) + [ANY],
        out_specs=[ANY, VMEM],
        scratch_shapes=[
            pltpu.VMEM((width, 2 * width), F32),
            pltpu.VMEM((2 * width, 2 * width), BF16),
            pltpu.VMEM(image.shape, F32),
            pltpu.VMEM(image.shape, F32),
            pltpu.SemaphoreType.DMA(()),
            pltpu.SemaphoreType.DMA((image.shape[0],)),
        ],
        compiler_params=params(),
        name="last",
    )(count, *parts, image)


def shift(shard, axis, by, wrap):
    size = lax.axis_size(axis)
    route = [(i, (i + by) % size) for i in range(size) if wrap or 0 <= i + by < size]
    return lax.ppermute(shard, axis, route)


def exchange(sent):
    to_next, to_prev, to_right, to_left = sent
    return (shift(to_next, "group", 1, True), shift(to_prev, "group", -1, True),
            shift(to_right, "dom", 1, False), shift(to_left, "dom", -1, False))


def swap(value, mask):
    size = lax.axis_size("group") * lax.axis_size("dom")
    return lax.ppermute(value, AXES, [(i, i ^ mask) for i in range(size)])


def sum_parts(value):
    size = lax.axis_size("group") * lax.axis_size("dom")
    masks = [1 << b for b in range(size.bit_length() - 1)]
    for mask in masks[:-1]:
        value = value + swap(value, mask)
    return [value, swap(value, masks[-1])]


def sum_gathered(gram):
    groups, parts = lax.axis_size("group"), lax.axis_size("dom")
    width = gram.shape[1]
    mine = lax.all_to_all(gram.reshape(parts, -1, width), "dom", 0, 0, tiled=True).sum(0)
    mine = lax.all_to_all(jnp.broadcast_to(mine, (groups,) + mine.shape), "group", 0, 0, tiled=True).sum(0)
    whole = lax.all_to_all(jnp.broadcast_to(mine, (parts,) + mine.shape), "dom", 0, 0, tiled=True)
    return [whole.reshape(gram.shape)]


def body(blocks, columns, sends, active_row_count, degree, start):
    slots, _, nodes, _ = blocks.shape
    denominator = lax.axis_size("group") * lax.axis_size("dom") * slots * nodes
    sizes = (slots // 2, slots // 2, slots // 4, slots // 4)
    halo = exchange(prep(sends, active_row_count, degree, start, sizes))
    image, gram, *sent = product(columns, sends, active_row_count, degree, start, blocks, halo, True)
    halo = exchange(sent)
    parts = sum_parts(gram)
    image, _ = product(columns, sends, active_row_count, degree, image, blocks, halo, False)
    image, gram = middle(parts, active_row_count, image, denominator)
    return tuple(last(sum_gathered(gram), active_row_count, image, denominator))


def solution(mesh):
    return jax.shard_map(
        body,
        mesh=mesh,
        in_specs=(
            P(AXES, None, None, None),
            P(AXES, None),
            P(AXES),
            P(AXES),
            P(AXES, None),
            P(AXES, None, None),
        ),
        out_specs=(P(AXES, None, None), P()),
        check_vma=False,
    )
```

time: 644 us -> 175 us (0.27)
  waiting for transfers between devices: 477 us -> 17.6 us
  other arithmetic: 57.5 us -> 0.95 us
  Pallas kernels: 0 us -> 53.7 us
  blocking collectives: 0 us -> 51.2 us
  matrix products: 32.7 us -> 0 us
  local copies, waits for them, and re-layouts: 36.2 us -> 3.94 us
  starting transfers between devices: 24.8 us -> 46.1 us
  between operations: 15 us -> 1.7 us
    psum x2 -> x0, waiting for transfers between devices: 472 us -> none  [summed_gram(): return lax.psum(local, ('group', 'dom'))]
    pallas_call x0 -> x5, Pallas kernels: none -> 53.7 us  [the longest x2 23.3 us: product(): pl.pallas_call(functools.partial(product_kernel, sending), out_shape=out_...]
    all_to_all x0 -> x3, blocking collectives: none -> 51.2 us  [the longest x1 25.1 us: sum_gathered(): lax.all_to_all(gram.reshape(parts, -1, width), 'dom', 0, 0, tiled=True)]
    another operation x10 -> x0, other arithmetic: 46.3 us -> none  [the longest x6 24.8 us: body(): factor = jnp.linalg.cholesky(gram_matrix)]
    dot_general x6 -> x0, matrix products: 32.1 us -> none  [the longest x2 19.5 us: body(): jnp.einsum('skij,skjc->sic', blocks, gathered, preferred_element_type=jnp...]
    gather x10 -> x0, local copies, waits for them, and re-layouts: 27 us -> none  [the longest x2 20.7 us: body(): gathered = jnp.take(extended, columns, axis=0)]
    ppermute x8 -> x16, starting transfers between devices: 24.6 us -> 46.1 us  [the longest x8 33 us: shift(): return lax.ppermute(shard, axis, route)]
    ppermute x8 -> x16, waiting for transfers between devices: 4.46 us -> 17.6 us  [the longest x8 13 us: swap(): return lax.ppermute(value, AXES, [(i, i ^ mask) for i in range(size)])]
  transfers between devices with their start and end apart: 10 -> 16, of which waited for: 6 -> 7; matrix products, arithmetic and copies ran while one was open for 2% -> 0% of each run, Pallas kernels for 0% -> 6%
where the time goes in v1:
time: 175 us
  Pallas kernels  53.7 us (31%)
  blocking collectives  51.2 us (29%)
  starting transfers between devices  46.1 us (26%)
  waiting for transfers between devices  17.6 us (10%)
  local copies, waits for them, and re-layouts  3.94 us (2%)
    ppermute x8, starting transfers between devices, shift(): return lax.ppermute(shard, axis, route)  33 us
    all_to_all x1, blocking collectives, sum_gathered(): lax.all_to_all(gram.reshape(parts, -1, width), 'dom', 0, 0, tiled=True)  25.1 us
    pallas_call x2, Pallas kernels, product(): pl.pallas_call(functools.partial(product_kernel, sending), out_shape=out_...  23.3 us
    all_to_all x1, blocking collectives, sum_gathered(): lax.all_to_all(jnp.broadcast_to(mine, (groups,) + mine.shape), 'group', 0...  15.9 us
    pallas_call x1, Pallas kernels, middle(): pl.pallas_call(functools.partial(middle_kernel, denominator, len(parts)),...  14.4 us
    ppermute x8, starting transfers between devices, swap(): return lax.ppermute(value, AXES, [(i, i ^ mask) for i in range(size)])  13.1 us
    ppermute x8, waiting for transfers between devices, swap(): return lax.ppermute(value, AXES, [(i, i ^ mask) for i in range(size)])  13 us
    pallas_call x1, Pallas kernels, last(): pl.pallas_call(functools.partial(last_kernel, denominator, len(parts)), o...  12 us
  transfers between devices with their start and end apart: 16, of which 7 were waited for; matrix products, arithmetic and copies ran while one was open for 0% of the time, Pallas kernels for 6%

profile of v1, /device:TPU:1, one launch (start us, length us, event | category | flops | bytes accessed | tf_op | source)
XLA Modules:
  0.0 175.2 jit_solution(3241667606248615116)
XLA Ops:
  1.3 4.1 %prep.1 = (bf16[13,128,128]{2,1,0:T(8,128)(2,1)}, bf16[13,128,128]{2,1,0:T(8,128)(2,1)}, bf16[6,128,128]{2,1,0:T(8,128)(2,1)}, bf16[6,128,128]{2,1,0:T(8,128)(2,1)}) custom-call(s32[38]{0:T(128)} %sends_ref.5, s32[1]{0:T(128)S(6)} %copy.12.count_ref, f32[26,128]{1,0:T(8,128)} %degree_ref.5, f32[26,128,128]{2,1,0:T(8,128)} %current_hbm.1), custom_call_target="tpu_custom_call" | custom-call | tf_op jit(solution)/shard_map/prep/pallas_call | solution.py:263
  5.4 1.8 %collective-permute-start = (bf16[13,128,128]{2,1,0:T(8,128)(2,1)}, bf16[13,128,128]{2,1,0:T(8,128)(2,1)S(1)}, u32[]{:S(2)}, u32[]{:S(2)}) collective-permute-start(bf16[13,128,128]{2,1,0:T(8,128)(2,1)} %get-tuple-element.15), channel_id=1, source_target_pairs={{0,8},{8,16},{16,24},{24,32},{32,40},{40,48},{48,56},{56,64},{64,7... | collective-permute-start | bytes 1277960 | tf_op jit(solution)/shard_map/ppermute | solution.py:345
  7.2 7.2 %collective-permute-start.1 = (bf16[13,128,128]{2,1,0:T(8,128)(2,1)}, bf16[13,128,128]{2,1,0:T(8,128)(2,1)S(1)}, u32[]{:S(2)}, u32[]{:S(2)}) collective-permute-start(bf16[13,128,128]{2,1,0:T(8,128)(2,1)} %get-tuple-element.16), channel_id=1, source_target_pairs={{0,248},{8,0},{16,8},{24,16},{32,24},{40,32},{48,40},{56,48},{64,5... | collective-permute-start | bytes 1277960 | tf_op jit(solution)/shard_map/ppermute | solution.py:345
  14.4 3.6 %collective-permute-start.2 = (bf16[6,128,128]{2,1,0:T(8,128)(2,1)}, bf16[6,128,128]{2,1,0:T(8,128)(2,1)S(1)}, u32[]{:S(2)}, u32[]{:S(2)}) collective-permute-start(bf16[6,128,128]{2,1,0:T(8,128)(2,1)} %get-tuple-element.17), channel_id=1, source_target_pairs={{0,1},{1,2},{2,3},{3,4},{4,5},{5,6},{6,7},{8,9},{9,10},{10,11},{11... | collective-permute-start | bytes 589832 | tf_op jit(solution)/shard_map/ppermute | solution.py:345
  18.0 1.9 %collective-permute-start.3 = (bf16[6,128,128]{2,1,0:T(8,128)(2,1)}, bf16[6,128,128]{2,1,0:T(8,128)(2,1)S(1)}, u32[]{:S(2)}, u32[]{:S(2)}) collective-permute-start(bf16[6,128,128]{2,1,0:T(8,128)(2,1)} %get-tuple-element.18), channel_id=1, source_target_pairs={{1,0},{2,1},{3,2},{4,3},{5,4},{6,5},{7,6},{9,8},{10,9},{11,10},{12... | collective-permute-start | bytes 589832 | tf_op jit(solution)/shard_map/ppermute | solution.py:345
  19.9 0.7 copy.10.columns_ref
  20.9 4.3 %collective-permute-done.3.halo3 = bf16[6,128,128]{2,1,0:T(8,128)(2,1)S(1)} collective-permute-done((bf16[6,128,128]{2,1,0:T(8,128)(2,1)}, bf16[6,128,128]{2,1,0:T(8,128)(2,1)S(1)}, u32[]{:S(2)}, u32[]{:S(2)}) %collective-permute-start.3) | collective-permute-done | bytes 196640 | tf_op jit(solution)/shard_map/ppermute | solution.py:345
  25.2 0.6 copy-done.8
  26.0 0.8 copy-done.3
  26.8 12.0 %product.2 = (f32[26,128,128]{2,1,0:T(8,128)}, f32[128,128]{1,0:T(8,128)}, bf16[13,128,128]{2,1,0:T(8,128)(2,1)}, bf16[13,128,128]{2,1,0:T(8,128)(2,1)}, bf16[6,...) custom-call(s32[26,11]{1,0:T(8,128)} %copy.10.columns_ref, s32[38]{0:T(128)} %sends_ref.5, s32[1]{0:T(128)S(6)} %copy.12.count_ref, ...), custom_call_target="tpu_custom_call" | custom-call | tf_op jit(solution)/shard_map/product/pallas_call | solution.py:280
  38.9 1.4 collective-permute-done.4
  40.3 0.9 add.21
  41.2 1.9 %collective-permute-start.5 = (f32[128,128]{1,0:T(8,128)S(1)}, f32[128,128]{1,0:T(8,128)S(1)}, u32[]{:S(2)}, u32[]{:S(2)}) collective-permute-start(f32[128,128]{1,0:T(8,128)S(1)} %add.21), channel_id=1, source_target_pairs={{0,2},{1,3},{2,0},{3,1},{4,6},{5,7},{6,4},{7,5},{8,10},{9,11},{10,... | collective-permute-start | bytes 196616 | tf_op jit(solution)/shard_map/ppermute | solution.py:356
  43.1 11.6 %collective-permute-start.13 = (bf16[13,128,128]{2,1,0:T(8,128)(2,1)}, bf16[13,128,128]{2,1,0:T(8,128)(2,1)S(1)}, u32[]{:S(2)}, u32[]{:S(2)}) collective-permute-start(bf16[13,128,128]{2,1,0:T(8,128)(2,1)} %get-tuple-element.22), channel_id=1, source_target_pairs={{0,248},{8,0},{16,8},{24,16},{32,24},{40,32},{48,40},{56,48},{64,5... | collective-permute-start | bytes 1277960 | tf_op jit(solution)/shard_map/ppermute | solution.py:345
  54.7 2.5 %collective-permute-start.6 = (f32[128,128]{1,0:T(8,128)S(1)}, f32[128,128]{1,0:T(8,128)S(1)}, u32[]{:S(2)}, u32[]{:S(2)}) collective-permute-start(f32[128,128]{1,0:T(8,128)S(1)} %add.22), channel_id=1, source_target_pairs={{0,4},{1,5},{2,6},{3,7},{4,0},{5,1},{6,2},{7,3},{8,12},{9,13},{10,... | collective-permute-start | bytes 196616 | tf_op jit(solution)/shard_map/ppermute | solution.py:356
  57.3 2.5 %collective-permute-done.6 = f32[128,128]{1,0:T(8,128)S(1)} collective-permute-done((f32[128,128]{1,0:T(8,128)S(1)}, f32[128,128]{1,0:T(8,128)S(1)}, u32[]{:S(2)}, u32[]{:S(2)}) %collective-permute-start.6) | collective-permute-done | bytes 65568 | tf_op jit(solution)/shard_map/ppermute | solution.py:356
  59.8 3.4 %collective-permute-done.7 = f32[128,128]{1,0:T(8,128)S(1)} collective-permute-done((f32[128,128]{1,0:T(8,128)S(1)}, f32[128,128]{1,0:T(8,128)S(1)}, u32[]{:S(2)}, u32[]{:S(2)}) %collective-permute-start.7) | collective-permute-done | bytes 65568 | tf_op jit(solution)/shard_map/ppermute | solution.py:356
  63.4 4.9 %collective-permute-start.14 = (bf16[6,128,128]{2,1,0:T(8,128)(2,1)}, bf16[6,128,128]{2,1,0:T(8,128)(2,1)S(1)}, u32[]{:S(2)}, u32[]{:S(2)}) collective-permute-start(bf16[6,128,128]{2,1,0:T(8,128)(2,1)} %get-tuple-element.23), channel_id=1, source_target_pairs={{0,1},{1,2},{2,3},{3,4},{4,5},{5,6},{6,7},{8,9},{9,10},{10,11},{11... | collective-permute-start | bytes 589832 | tf_op jit(solution)/shard_map/ppermute | solution.py:345
  68.3 1.9 %collective-permute-start.15 = (bf16[6,128,128]{2,1,0:T(8,128)(2,1)}, bf16[6,128,128]{2,1,0:T(8,128)(2,1)S(1)}, u32[]{:S(2)}, u32[]{:S(2)}) collective-permute-start(bf16[6,128,128]{2,1,0:T(8,128)(2,1)} %get-tuple-element.24), channel_id=1, source_target_pairs={{1,0},{2,1},{3,2},{4,3},{5,4},{6,5},{7,6},{9,8},{10,9},{11,10},{12... | collective-permute-start | bytes 589832 | tf_op jit(solution)/shard_map/ppermute | solution.py:345
  70.2 1.4 collective-permute-start.9
  71.6 1.8 %collective-permute-done.9 = f32[128,128]{1,0:T(8,128)S(1)} collective-permute-done((f32[128,128]{1,0:T(8,128)S(1)}, f32[128,128]{1,0:T(8,128)S(1)}, u32[]{:S(2)}, u32[]{:S(2)}) %collective-permute-start.9) | collective-permute-done | bytes 65568 | tf_op jit(solution)/shard_map/ppermute | solution.py:356
  73.4 5.7 %collective-permute-start.10 = (f32[128,128]{1,0:T(8,128)S(1)}, f32[128,128]{1,0:T(8,128)S(1)}, u32[]{:S(2)}, u32[]{:S(2)}) collective-permute-start(f32[128,128]{1,0:T(8,128)S(1)} %add.26), channel_id=1, source_target_pairs={{0,64},{1,65},{2,66},{3,67},{4,68},{5,69},{6,70},{7,71},{8,72},{9,... | collective-permute-start | bytes 196616 | tf_op jit(solution)/shard_map/ppermute | solution.py:356
  79.1 3.9 %collective-permute-done.10 = f32[128,128]{1,0:T(8,128)S(1)} collective-permute-done((f32[128,128]{1,0:T(8,128)S(1)}, f32[128,128]{1,0:T(8,128)S(1)}, u32[]{:S(2)}, u32[]{:S(2)}) %collective-permute-start.10) | collective-permute-done | bytes 65568 | tf_op jit(solution)/shard_map/ppermute | solution.py:356
  83.0 1.3 collective-permute-start.11
  84.4 0.6 copy-done.5
  85.4 11.3 %product.3 = (f32[26,128,128]{2,1,0:T(8,128)}, f32[128,128]{1,0:T(8,128)}) custom-call(s32[26,11]{1,0:T(8,128)} %copy.10.columns_ref, s32[38]{0:T(128)} %sends_ref.5, s32[1]{0:T(128)S(6)} %copy.12.count_ref, f32[26,128]{1,0:T(8,128)} %degree_ref.5, f32[26,128,128]{2,1,0:T(8,128)} %get-tuple-element.20.current_hbm, bf16[26,11,128,128]{3,2,1,0:T(8,128)(2,1)} %blocks_hbm.3, ...), custom_call_target="tpu_custom_call" | custom-call | tf_op jit(solution)/shard_map/product/pallas_call | solution.py:280
  96.7 0.6 copy-done.9
  97.3 14.4 %middle.1 = (f32[26,128,128]{2,1,0:T(8,128)}, f32[128,128]{1,0:T(8,128)}) custom-call(s32[1]{0:T(128)S(6)} %copy.12.count_ref, f32[128,128]{1,0:T(8,128)} %copy-done.4, f32[128,128]{1,0:T(8,128)} %copy-done.9, f32[26,128,128]{2,1,0:T(8,128)} %get-tuple-element.25.refs_2_), custom_call_target="tpu_custom_call" | custom-call | tf_op jit(solution)/shard_map/middle/pallas_call | solution.py:304
  111.7 25.1 %all_to_all.15 = f32[8,16,128]{2,1,0:T(8,128)S(1)} all-to-all(f32[8,16,128]{2,1,0:T(8,128)} %bitcast.3), channel_id=1, replica_groups=mesh['group'=32,'dom'=8] {'dom'}, dimensions={0} | all-to-all | bytes 131072 | tf_op jit(solution)/shard_map/all_to_all | solution.py:370
  136.8 15.9 %all_to_all.16 = f32[32,16,128]{2,1,0:T(8,128)S(1)} all-to-all(f32[32,16,128]{2,1,0:T(8,128)S(1)} %broadcast_in_dim.6), channel_id=1, replica_groups=mesh['group'=32,'dom'=8] {'group'}, dimensions={0} | all-to-all | bytes 524288 | tf_op jit(solution)/shard_map/all_to_all | solution.py:371
  152.7 10.3 %all_to_all.17 = f32[8,16,128]{2,1,0:T(8,128)} all-to-all(f32[8,16,128]{2,1,0:T(8,128)S(1)} %broadcast_in_dim.7), channel_id=1, replica_groups=mesh['group'=32,'dom'=8] {'dom'}, dimensions={0} | all-to-all | bytes 131072 | tf_op jit(solution)/shard_map/all_to_all | solution.py:372
  163.0 12.0 %last.1 = (f32[26,128,128]{2,1,0:T(8,128)}, f32[128,128]{1,0:T(8,128)}) custom-call(s32[1]{0:T(128)S(6)} %copy.12.count_ref, f32[128,128]{1,0:T(8,128)} %bitcast.2, f32[26,128,128]{2,1,0:T(8,128)} %get-tuple-element.27.refs_1_), custom_call_target="tpu_custom_call" | custom-call | tf_op jit(solution)/shard_map/last/pallas_call | solution.py:324
  (42 shorter events, 1.3 us)
Async XLA Ops:
  0.6 19.3 %copy-start.10 = (s32[26,11]{0,1:T(8,128)S(1)}, s32[26,11]{0,1:T(8,128)}, u32[]{:S(2)}) copy-start(s32[26,11]{0,1:T(8,128)} %param.7) | copy-start | bytes 3436
  5.4 19.8 %collective-permute-start = (bf16[13,128,128]{2,1,0:T(8,128)(2,1)}, bf16[13,128,128]{2,1,0:T(8,128)(2,1)S(1)}, u32[]{:S(2)}, u32[]{:S(2)}) collective-permute-start(bf16[13,128,128]{2,1,0:T(8,128)(2,1)} %get-tuple-element.15), channel_id=1, source_target_pairs={{0,8},{8,16},{16,24},{24,32},{32,40},{40,48},{48,56},{56,64},{64,7... | collective-permute-start | bytes 1277960 | tf_op jit(solution)/shard_map/ppermute | solution.py:345
  7.2 18.0 %collective-permute-start.1 = (bf16[13,128,128]{2,1,0:T(8,128)(2,1)}, bf16[13,128,128]{2,1,0:T(8,128)(2,1)S(1)}, u32[]{:S(2)}, u32[]{:S(2)}) collective-permute-start(bf16[13,128,128]{2,1,0:T(8,128)(2,1)} %get-tuple-element.16), channel_id=1, source_target_pairs={{0,248},{8,0},{16,8},{24,16},{32,24},{40,32},{48,40},{56,48},{64,5... | collective-permute-start | bytes 1277960 | tf_op jit(solution)/shard_map/ppermute | solution.py:345
  14.4 6.5 %collective-permute-start.2 = (bf16[6,128,128]{2,1,0:T(8,128)(2,1)}, bf16[6,128,128]{2,1,0:T(8,128)(2,1)S(1)}, u32[]{:S(2)}, u32[]{:S(2)}) collective-permute-start(bf16[6,128,128]{2,1,0:T(8,128)(2,1)} %get-tuple-element.17), channel_id=1, source_target_pairs={{0,1},{1,2},{2,3},{3,4},{4,5},{5,6},{6,7},{8,9},{9,10},{10,11},{11... | collective-permute-start | bytes 589832 | tf_op jit(solution)/shard_map/ppermute | solution.py:345
  18.0 7.2 %collective-permute-start.3 = (bf16[6,128,128]{2,1,0:T(8,128)(2,1)}, bf16[6,128,128]{2,1,0:T(8,128)(2,1)S(1)}, u32[]{:S(2)}, u32[]{:S(2)}) collective-permute-start(bf16[6,128,128]{2,1,0:T(8,128)(2,1)} %get-tuple-element.18), channel_id=1, source_target_pairs={{1,0},{2,1},{3,2},{4,3},{5,4},{6,5},{7,6},{9,8},{10,9},{11,10},{12... | collective-permute-start | bytes 589832 | tf_op jit(solution)/shard_map/ppermute | solution.py:345
  20.9 4.3 %copy-start.7 = (bf16[6,128,128]{2,1,0:T(8,128)(2,1)}, bf16[6,128,128]{2,1,0:T(8,128)(2,1)S(1)}, u32[]{:S(2)}) copy-start(bf16[6,128,128]{2,1,0:T(8,128)(2,1)S(1)} %collective-permute-done.2.halo2) | copy-start | bytes 589828
  25.2 0.7 copy-start.8
  25.2 0.9 copy-start.2
  26.0 0.8 copy-start.3
  38.8 1.6 collective-permute-start.4
  41.2 13.5 %collective-permute-start.5 = (f32[128,128]{1,0:T(8,128)S(1)}, f32[128,128]{1,0:T(8,128)S(1)}, u32[]{:S(2)}, u32[]{:S(2)}) collective-permute-start(f32[128,128]{1,0:T(8,128)S(1)} %add.21), channel_id=1, source_target_pairs={{0,2},{1,3},{2,0},{3,1},{4,6},{5,7},{6,4},{7,5},{8,10},{9,11},{10,... | collective-permute-start | bytes 196616 | tf_op jit(solution)/shard_map/ppermute | solution.py:356
  43.1 41.3 %collective-permute-start.12 = (bf16[13,128,128]{2,1,0:T(8,128)(2,1)}, bf16[13,128,128]{2,1,0:T(8,128)(2,1)S(1)}, u32[]{:S(2)}, u32[]{:S(2)}) collective-permute-start(bf16[13,128,128]{2,1,0:T(8,128)(2,1)} %get-tuple-element.21), channel_id=1, source_target_pairs={{0,8},{8,16},{16,24},{24,32},{32,40},{40,48},{48,56},{56,64},{64,7... | collective-permute-start | bytes 1277960 | tf_op jit(solution)/shard_map/ppermute | solution.py:345
  43.1 41.3 %collective-permute-start.13 = (bf16[13,128,128]{2,1,0:T(8,128)(2,1)}, bf16[13,128,128]{2,1,0:T(8,128)(2,1)S(1)}, u32[]{:S(2)}, u32[]{:S(2)}) collective-permute-start(bf16[13,128,128]{2,1,0:T(8,128)(2,1)} %get-tuple-element.22), channel_id=1, source_target_pairs={{0,248},{8,0},{16,8},{24,16},{32,24},{40,32},{48,40},{56,48},{64,5... | collective-permute-start | bytes 1277960 | tf_op jit(solution)/shard_map/ppermute | solution.py:345
  54.7 5.0 %collective-permute-start.6 = (f32[128,128]{1,0:T(8,128)S(1)}, f32[128,128]{1,0:T(8,128)S(1)}, u32[]{:S(2)}, u32[]{:S(2)}) collective-permute-start(f32[128,128]{1,0:T(8,128)S(1)} %add.22), channel_id=1, source_target_pairs={{0,4},{1,5},{2,6},{3,7},{4,0},{5,1},{6,2},{7,3},{8,12},{9,13},{10,... | collective-permute-start | bytes 196616 | tf_op jit(solution)/shard_map/ppermute | solution.py:356
  59.7 3.5 %collective-permute-start.7 = (f32[128,128]{1,0:T(8,128)S(1)}, f32[128,128]{1,0:T(8,128)S(1)}, u32[]{:S(2)}, u32[]{:S(2)}) collective-permute-start(f32[128,128]{1,0:T(8,128)S(1)} %add.23), channel_id=1, source_target_pairs={{0,8},{1,9},{2,10},{3,11},{4,12},{5,13},{6,14},{7,15},{8,0},{9,1},... | collective-permute-start | bytes 196616 | tf_op jit(solution)/shard_map/ppermute | solution.py:356
  63.3 6.9 %collective-permute-start.8 = (f32[128,128]{1,0:T(8,128)S(1)}, f32[128,128]{1,0:T(8,128)S(1)}, u32[]{:S(2)}, u32[]{:S(2)}) collective-permute-start(f32[128,128]{1,0:T(8,128)S(1)} %add.24), channel_id=1, source_target_pairs={{0,16},{1,17},{2,18},{3,19},{4,20},{5,21},{6,22},{7,23},{8,24},{9,... | collective-permute-start | bytes 196616 | tf_op jit(solution)/shard_map/ppermute | solution.py:356
  63.4 21.0 %collective-permute-start.14 = (bf16[6,128,128]{2,1,0:T(8,128)(2,1)}, bf16[6,128,128]{2,1,0:T(8,128)(2,1)S(1)}, u32[]{:S(2)}, u32[]{:S(2)}) collective-permute-start(bf16[6,128,128]{2,1,0:T(8,128)(2,1)} %get-tuple-element.23), channel_id=1, source_target_pairs={{0,1},{1,2},{2,3},{3,4},{4,5},{5,6},{6,7},{8,9},{9,10},{10,11},{11... | collective-permute-start | bytes 589832 | tf_op jit(solution)/shard_map/ppermute | solution.py:345
  68.3 16.1 %collective-permute-start.15 = (bf16[6,128,128]{2,1,0:T(8,128)(2,1)}, bf16[6,128,128]{2,1,0:T(8,128)(2,1)S(1)}, u32[]{:S(2)}, u32[]{:S(2)}) collective-permute-start(bf16[6,128,128]{2,1,0:T(8,128)(2,1)} %get-tuple-element.24), channel_id=1, source_target_pairs={{1,0},{2,1},{3,2},{4,3},{5,4},{6,5},{7,6},{9,8},{10,9},{11,10},{12... | collective-permute-start | bytes 589832 | tf_op jit(solution)/shard_map/ppermute | solution.py:345
  70.2 3.2 %collective-permute-start.9 = (f32[128,128]{1,0:T(8,128)S(1)}, f32[128,128]{1,0:T(8,128)S(1)}, u32[]{:S(2)}, u32[]{:S(2)}) collective-permute-start(f32[128,128]{1,0:T(8,128)S(1)} %add.25), channel_id=1, source_target_pairs={{0,32},{1,33},{2,34},{3,35},{4,36},{5,37},{6,38},{7,39},{8,40},{9,... | collective-permute-start | bytes 196616 | tf_op jit(solution)/shard_map/ppermute | solution.py:356
  73.4 9.6 %collective-permute-start.10 = (f32[128,128]{1,0:T(8,128)S(1)}, f32[128,128]{1,0:T(8,128)S(1)}, u32[]{:S(2)}, u32[]{:S(2)}) collective-permute-start(f32[128,128]{1,0:T(8,128)S(1)} %add.26), channel_id=1, source_target_pairs={{0,64},{1,65},{2,66},{3,67},{4,68},{5,69},{6,70},{7,71},{8,72},{9,... | collective-permute-start | bytes 196616 | tf_op jit(solution)/shard_map/ppermute | solution.py:356
  83.0 13.7 %copy-start.4 = (f32[128,128]{1,0:T(8,128)}, f32[128,128]{1,0:T(8,128)S(1)}, u32[]{:S(2)}) copy-start(f32[128,128]{1,0:T(8,128)S(1)} %add.27.refs_0_) | copy-start | bytes 196612
  83.0 13.7 %collective-permute-start.11 = (f32[128,128]{1,0:T(8,128)S(1)}, f32[128,128]{1,0:T(8,128)S(1)}, u32[]{:S(2)}, u32[]{:S(2)}) collective-permute-start(f32[128,128]{1,0:T(8,128)S(1)} %add.27.refs_0_), channel_id=1, source_target_pairs={{0,128},{1,129},{2,130},{3,131},{4,132},{5,133},{6,134},{7,135},{8... | collective-permute-start | bytes 196616 | tf_op jit(solution)/shard_map/ppermute | solution.py:356
  84.4 0.7 copy-start.5
  84.4 0.8 copy-start.6
  84.4 0.9 copy-start
  84.4 1.0 copy-start.1
  96.7 0.6 copy-start.9

commit v2 on v0

v2 whole, which is shorter than its diff:
```python
import functools
import jax
import jax.numpy as jnp
from jax import lax
from jax.experimental import pallas as pl
from jax.experimental.pallas import tpu as pltpu
from jax.sharding import PartitionSpec as P

AXES = ("group", "dom")
F32, BF16 = jnp.float32, jnp.bfloat16
PANEL = 16
ANY = pl.BlockSpec(memory_space=pl.ANY)
SMEM = pl.BlockSpec(memory_space=pltpu.SMEM)
VMEM = pl.BlockSpec(memory_space=pltpu.VMEM)


def split3(x):
    high = x.astype(BF16)
    rest = x - high.astype(F32)
    mid = rest.astype(BF16)
    low = (rest - mid.astype(F32)).astype(BF16)
    return high, mid, low


def dot(a, b):
    return jnp.dot(a, b, preferred_element_type=F32)


def dot_rows(a, b):
    return lax.dot_general(a, b, (((0,), (0,)), ((), ())), preferred_element_type=F32)


def scale_blocks(degree_ref):
    scale = lax.rsqrt(degree_ref[...])
    slots, nodes = scale.shape
    turned = jnp.concatenate([scale, jnp.zeros((nodes - slots, nodes), F32)], axis=0).T
    return [jnp.broadcast_to(turned[:, s:s + 1], (nodes, nodes)) for s in range(slots)]


def add_gram(parts, wide_ref, side_ref):
    high, mid, low = parts
    wide_ref[...] += dot_rows(high, jnp.concatenate([high, mid], axis=1))
    left = jnp.concatenate([high, mid * BF16(0.5)], axis=0)
    side_ref[...] += dot_rows(left, jnp.concatenate([low, mid], axis=0))


def finish_gram(wide_ref, side_ref):
    width = side_ref.shape[0]
    cross = wide_ref[:, width:] + side_ref[...]
    return wide_ref[:, :width] + (cross + cross.T)


def put_sends(out_refs, sends_ref, block_ref):
    base = 0
    for out_ref in out_refs:
        for j in range(out_ref.shape[0]):
            out_ref[j] = block_ref[sends_ref[base + j]]
        base += out_ref.shape[0]


def prep_kernel(sends_ref, degree_ref, start_ref, operand_ref, *out_refs):
    for s, scale in enumerate(scale_blocks(degree_ref)):
        operand_ref[s] = (scale * start_ref[s]).astype(BF16)
    put_sends(out_refs, sends_ref, operand_ref)


def load_kernel(blocks_hbm, after_ref, blocks_ref, sem):
    copy = pltpu.make_async_copy(blocks_hbm, blocks_ref, sem)
    copy.start()
    copy.wait()


def product_kernel(sending, columns_ref, sends_ref, count_ref, degree_ref, current_ref, operand_ref,
                   blocks_ref, halo0, halo1, halo2, halo3, image_ref, gram_ref, *refs):
    next_ref, out_refs = (refs[0], refs[1:5]) if sending else (None, ())
    ext_ref, scale_ref, parts_ref, wide_ref, side_ref = refs[1 + len(out_refs) if sending else 0:]
    slots, per_row = blocks_ref.shape[:2]
    group = parts_ref.shape[1] // image_ref.shape[1]
    count = count_ref[0]
    base = 0
    for piece in (operand_ref, halo0, halo1, halo2, halo3):
        size = piece.shape[0]
        ext_ref[base:base + size] = piece[...]
        base += size
    wide_ref[...] = jnp.zeros_like(wide_ref)
    side_ref[...] = jnp.zeros_like(side_ref)
    parts_ref[...] = jnp.zeros_like(parts_ref)
    for s, scale in enumerate(scale_blocks(degree_ref)):
        scale_ref[s] = scale

    def row(s):
        left = jnp.concatenate([blocks_ref[s, k] for k in range(per_row)], axis=1)
        right = jnp.concatenate([ext_ref[columns_ref[k, s]] for k in range(per_row)], axis=0)
        image = current_ref[s] + scale_ref[s] * dot(left, right)
        return jnp.where(s < count, image, 0.0)

    def rows(step, carry):
        add_gram([parts_ref[i] for i in range(3)], wide_ref, side_ref)
        first = step * group
        images = [row(first + i) for i in range(group)]
        for i, image in enumerate(images):
            image_ref[first + i] = image
            if sending:
                next_ref[first + i] = (scale_ref[first + i] * image).astype(BF16)
        for i, part in enumerate(split3(jnp.concatenate(images, axis=0))):
            parts_ref[i] = part
        return carry
    steps = (count + group - 1) // group
    lax.fori_loop(0, steps, rows, 0)
    add_gram([parts_ref[i] for i in range(3)], wide_ref, side_ref)

    def dead(s, carry):
        image_ref[s] = jnp.zeros(image_ref.shape[1:], F32)
        return carry
    lax.fori_loop(steps * group, slots, dead, 0)
    gram_ref[...] = finish_gram(wide_ref, side_ref)
    if sending:
        put_sends(out_refs, sends_ref, next_ref)


def gather_rows(rows, sublane):
    lanes = sublane.shape[0]
    pieces = []
    for first in range(0, len(rows), lanes):
        piece = rows[first]
        for j in range(1, lanes):
            piece = jnp.where(sublane == j, rows[first + j], piece)
        pieces.append(piece)
    return jnp.concatenate(pieces, axis=0)


def factorize(work_ref):
    size = work_ref.shape[0]
    step, lanes = PANEL, 8
    sublane = lax.broadcasted_iota(jnp.int32, (lanes, size), 0)
    for top in range(0, size, step):
        rows = work_ref[top:top + step, :]
        main = [jnp.broadcast_to(rows[i:i + 1, :size], (lanes, size)) for i in range(step)]
        side = [jnp.broadcast_to(rows[i:i + 1, size:], (lanes, size)) for i in range(step)]
        entry = [[jnp.broadcast_to(main[i][:, top + k:top + k + 1], (lanes, size)) if k >= i else None
                  for k in range(step)] for i in range(step)]
        for j in range(step):
            inv = lax.rsqrt(entry[j][j])
            main[j] = main[j] * inv
            side[j] = side[j] * inv
            scaled = [entry[j][k] * inv if k > j else None for k in range(step)]
            for i in range(j + 1, step):
                for k in range(i, step):
                    entry[i][k] = entry[i][k] - scaled[i] * scaled[k]
                main[i] = main[i] - scaled[i] * main[j]
                side[i] = side[i] - scaled[i] * side[j]
        both = jnp.concatenate([gather_rows(main, sublane), gather_rows(side, sublane)], axis=1)
        work_ref[top:top + step, :] = both
        if top + step < size:
            h, m, l = split3(both)
            a, b, c = h[:, :size], m[:, :size], l[:, :size]
            left = jnp.concatenate([a, a, b, b, a, c], axis=0)
            right = jnp.concatenate([h, m, h, m, l, h], axis=0)
            update = dot_rows(left, right)
            work_ref[top + step:, :] -= update[top + step:, :]


def start_factor(gram, denominator, work_ref):
    size = work_ref.shape[0]
    rows = lax.broadcasted_iota(jnp.int32, (size, size), 0)
    columns = lax.broadcasted_iota(jnp.int32, (size, size), 1)
    work_ref[:, :size] = gram * F32(1.0 / denominator)
    work_ref[:, size:] = (rows == columns).astype(F32)
    factorize(work_ref)
    return rows, columns


def dot_full(a, b):
    ah, am, al = split3(a)
    bh, bm, bl = split3(b)
    left = jnp.concatenate([ah, ah, am, ah, am, al], axis=1)
    right = jnp.concatenate([bh, bm, bh, bl, bm, bh], axis=0)
    return dot(left, right)


def wide_weights(weights, wide_ref):
    high, mid, _ = split3(weights)
    half = jnp.concatenate([high, mid], axis=1)
    wide_ref[...] = jnp.concatenate([half, half], axis=0)


def times_weights(image, wide_ref):
    width = image.shape[1]
    high = image.astype(BF16)
    mid = (image - high.astype(F32)).astype(BF16)
    both = dot(jnp.concatenate([high, mid], axis=1), wide_ref[...])
    return both[:, :width] + both[:, width:]


def last_kernel(denominator, grams_ref, image_ref, basis_hbm, factor_ref,
                work_ref, weights_ref, basis_ref, out_sems):
    slots, nodes, width = image_ref.shape
    start_factor(grams_ref[0], denominator, work_ref)
    first = work_ref[:, width:]
    turned = first.T
    rows, columns = start_factor(dot_full(dot_full(first, grams_ref[1]), turned), denominator, work_ref)
    wide_weights(dot_full(turned, work_ref[:, width:].T), weights_ref)
    half = slots // 2

    def out_copy(part):
        chunk = pl.ds(part * half, half)
        return pltpu.make_async_copy(basis_ref.at[chunk], basis_hbm.at[chunk], out_sems.at[part])

    def apply(s, carry):
        basis_ref[s] = times_weights(image_ref[s], weights_ref)
        return carry
    for part in range(2):
        lax.fori_loop(part * half, (part + 1) * half, apply, 0, unroll=half)
        out_copy(part).start()
    factor_ref[...] = jnp.where(rows <= columns, work_ref[:, :width], 0.0).T
    for part in range(2):
        out_copy(part).wait()


def params(limit):
    return pltpu.CompilerParams(vmem_limit_bytes=limit * 2**20)


def spread(shape, dtype):
    return jax.ShapeDtypeStruct(shape, dtype)


def prep(sends, degree, start, sizes):
    slots, nodes, width = start.shape
    return pl.pallas_call(
        prep_kernel,
        out_shape=[spread((n, nodes, width), BF16) for n in (slots,) + sizes],
        in_specs=[SMEM, VMEM, VMEM],
        out_specs=[VMEM] * 5,
        compiler_params=params(16),
        name="prep",
    )(sends, degree, start)


def load(blocks, after):
    size = blocks.size * blocks.dtype.itemsize
    return pl.pallas_call(
        load_kernel,
        out_shape=spread(blocks.shape, blocks.dtype),
        in_specs=[ANY, ANY],
        out_specs=VMEM,
        scratch_shapes=[pltpu.SemaphoreType.DMA(())],
        compiler_params=params(40),
        cost_estimate=pl.CostEstimate(flops=0, bytes_accessed=2 * size, transcendentals=0),
        name="load",
    )(blocks, after)


def product(columns, sends, count, degree, current, operand, blocks, halos, sending):
    slots, nodes, width = current.shape
    sizes = [h.shape[0] for h in halos]
    out_shape = [spread(current.shape, F32), spread((width, width), F32)]
    if sending:
        out_shape += [spread((n, nodes, width), BF16) for n in [slots] + sizes]
    group = 2
    return pl.pallas_call(
        functools.partial(product_kernel, sending),
        out_shape=out_shape,
        in_specs=[SMEM] * 3 + [VMEM] * 8,
        out_specs=[VMEM] * len(out_shape),
        scratch_shapes=[
            pltpu.VMEM((slots + sum(sizes), nodes, width), BF16),
            pltpu.VMEM(current.shape, F32),
            pltpu.VMEM((3, group * nodes, width), BF16),
            pltpu.VMEM((width, 2 * width), F32),
            pltpu.VMEM((width, width), F32),
        ],
        compiler_params=params(28),
        name="product",
    )(columns, sends, count, degree, current, operand, blocks, *halos)


def last(grams, image, denominator):
    slots, nodes, width = image.shape
    return pl.pallas_call(
        functools.partial(last_kernel, denominator),
        out_shape=[spread(image.shape, F32), spread((width, width), F32)],
        in_specs=[VMEM, VMEM],
        out_specs=[ANY, VMEM],
        scratch_shapes=[
            pltpu.VMEM((width, 2 * width), F32),
            pltpu.VMEM((2 * width, 2 * width), BF16),
            pltpu.VMEM(image.shape, F32),
            pltpu.SemaphoreType.DMA((2,)),
        ],
        compiler_params=params(16),
        name="last",
    )(grams, image)


def shift(shard, axis, by, wrap):
    size = lax.axis_size(axis)
    route = [(i, (i + by) % size) for i in range(size) if wrap or 0 <= i + by < size]
    return lax.ppermute(shard, axis, route)


def exchange(sent):
    to_next, to_prev, to_right, to_left = sent
    return (shift(to_next, "group", 1, True), shift(to_prev, "group", -1, True),
            shift(to_right, "dom", 1, False), shift(to_left, "dom", -1, False))


def collected(value, axis):
    size = lax.axis_size(axis)
    return lax.all_to_all(jnp.broadcast_to(value, (size,) + value.shape), axis, 0, 0, tiled=True)


def summed(grams):
    count, rows, width = grams.shape
    parts = lax.axis_size("dom")
    pieces = grams.reshape(count, parts, rows // parts, width).transpose(1, 0, 2, 3)
    mine = lax.all_to_all(pieces, "dom", 0, 0, tiled=True).sum(0)
    mine = collected(mine, "group").sum(0)
    whole = collected(mine, "dom")
    return whole.transpose(1, 0, 2, 3).reshape(grams.shape)


def body(blocks, columns, sends, active_row_count, degree, start):
    slots, _, nodes, _ = blocks.shape
    denominator = lax.axis_size("group") * lax.axis_size("dom") * slots * nodes
    sizes = (slots // 2, slots // 2, slots // 4, slots // 4)
    table = (columns.T, sends, active_row_count, degree)
    operand, *sent = prep(sends, degree, start, sizes)
    blocks = load(blocks, operand)
    image, first_gram, operand, *sent = product(*table, start, operand, blocks, exchange(sent), True)
    image, gram = product(*table, image, operand, blocks, exchange(sent), False)
    grams = summed(jnp.stack([first_gram, gram]))
    return last(grams, image, denominator)


def solution(mesh):
    return jax.shard_map(
        body,
        mesh=mesh,
        in_specs=(
            P(AXES, None, None, None),
            P(AXES, None),
            P(AXES),
            P(AXES),
            P(AXES, None),
            P(AXES, None, None),
        ),
        out_specs=(P(AXES, None, None), P()),
        check_vma=False,
    )
```

time: 644 us -> 107 us (0.17)
  waiting for transfers between devices: 477 us -> 5.63 us
  other arithmetic: 57.5 us -> 0.07 us
  blocking collectives: 0 us -> 45.6 us
  local copies, waits for them, and re-layouts: 36.2 us -> 2.92 us
  matrix products: 32.7 us -> 0 us
  Pallas kernels: 0 us -> 25.7 us
  between operations: 15 us -> 1.61 us
    psum x2 -> x0, waiting for transfers between devices: 472 us -> none  [summed_gram(): return lax.psum(local, ('group', 'dom'))]
    another operation x10 -> x0, other arithmetic: 46.3 us -> none  [the longest x6 24.8 us: body(): factor = jnp.linalg.cholesky(gram_matrix)]
    all_to_all x0 -> x3, blocking collectives: none -> 45.6 us  [the longest x2 30.5 us: collected(): lax.all_to_all(jnp.broadcast_to(value, (size,) + value.shape), axis, 0, 0...]
    dot_general x6 -> x0, matrix products: 32.1 us -> none  [the longest x2 19.5 us: body(): jnp.einsum('skij,skjc->sic', blocks, gathered, preferred_element_type=jnp...]
    gather x10 -> x0, local copies, waits for them, and re-layouts: 27 us -> none  [the longest x2 20.7 us: body(): gathered = jnp.take(extended, columns, axis=0)]
    pallas_call x0 -> x5, Pallas kernels: none -> 25.7 us  [the longest x1 12.6 us: last(): pl.pallas_call(functools.partial(last_kernel, denominator), out_shape=[sp...]
  transfers between devices with their start and end apart: 10 -> 8, of which waited for: 6 -> 3; matrix products, arithmetic and copies ran while one was open for 2% -> 0% of each run, Pallas kernels for 0% -> 4%
where the time goes in v2:
time: 107 us
  blocking collectives  45.6 us (43%)
  Pallas kernels  25.7 us (24%)
  starting transfers between devices  25.5 us (24%)
  waiting for transfers between devices  5.63 us (5%)
  local copies, waits for them, and re-layouts  2.92 us (3%)
  between operations  1.61 us (2%)
    all_to_all x2, blocking collectives, collected(): lax.all_to_all(jnp.broadcast_to(value, (size,) + value.shape), axis, 0, 0...  30.5 us
    ppermute x8, starting transfers between devices, shift(): return lax.ppermute(shard, axis, route)  25.5 us
    all_to_all x1, blocking collectives, summed(): mine = lax.all_to_all(pieces, 'dom', 0, 0, tiled=True).sum(0)  15.1 us
    pallas_call x1, Pallas kernels, last(): pl.pallas_call(functools.partial(last_kernel, denominator), out_shape=[sp...  12.6 us
    pallas_call x2, Pallas kernels, product(): pl.pallas_call(functools.partial(product_kernel, sending), out_shape=out_...  8.05 us
    ppermute x8, waiting for transfers between devices, shift(): return lax.ppermute(shard, axis, route)  5.63 us
    pallas_call x1, Pallas kernels, load(): pl.pallas_call(load_kernel, out_shape=spread(blocks.shape, blocks.dtype),...  3.79 us
    unnamed x14, local copies, waits for them, and re-layouts  2.85 us
  transfers between devices with their start and end apart: 8, of which 3 were waited for; matrix products, arithmetic and copies ran while one was open for 0% of the time, Pallas kernels for 4%

profile of v2, /device:TPU:1, one launch (start us, length us, event | category | flops | bytes accessed | tf_op | source)
XLA Modules:
  0.0 107.1 jit_solution(4537391591127748552)
XLA Ops:
  0.6 0.0 copy-start
  0.6 1.4 %copy-done = f32[26,128,128]{2,1,0:T(8,128)S(1)} copy-done((f32[26,128,128]{2,1,0:T(8,128)S(1)}, f32[26,128,128]{2,1,0:T(8,128)}, u32[]{:S(2)}) %copy-start) | copy-done | bytes 1703960
  2.1 0.7 copy-done.2
  2.8 0.7 copy-done.5
  3.5 1.3 %prep.1 = (bf16[26,128,128]{2,1,0:T(8,128)(2,1)S(1)}, bf16[13,128,128]{2,1,0:T(8,128)(2,1)S(1)}, bf16[13,128,128]{2,1,0:T(8,128)(2,1)S(1)}, bf16[6,128,128]{2,1,0:T(8,128)(2,1)S(1)}, bf16[6,128,128]{2,1,0:T(8,128)(2,1)S(1)}) custom-call(s32[38]{0:T(128)S(1)} %copy-done.5, f32[26,128]{1,0:T(8,128)S(1)} %copy-done.2, f32[26,128,128]{2,1,0:T(8,128)S(1)} %copy-done), custom_call_target="tpu_custom_call" | custom-call | tf_op jit(solution)/shard_map/prep/pallas_call | solution.py:230
  4.7 2.2 %collective-permute-start = (bf16[13,128,128]{2,1,0:T(8,128)(2,1)S(1)}, bf16[13,128,128]{2,1,0:T(8,128)(2,1)S(1)}, u32[]{:S(2)}, u32[]{:S(2)}) collective-permute-start(bf16[13,128,128]{2,1,0:T(8,128)(2,1)S(1)} %get-tuple-element.17), channel_id=1, source_target_pairs={{0,8},{8,16},{16,24},{24,32},{32,40},{40,48},{48,56},{56,64},{64,7... | collective-permute-start | bytes 1277960 | tf_op jit(solution)/shard_map/ppermute | solution.py:299
  7.0 6.8 %collective-permute-start.1 = (bf16[13,128,128]{2,1,0:T(8,128)(2,1)S(1)}, bf16[13,128,128]{2,1,0:T(8,128)(2,1)S(1)}, u32[]{:S(2)}, u32[]{:S(2)}) collective-permute-start(bf16[13,128,128]{2,1,0:T(8,128)(2,1)S(1)} %get-tuple-element.18), channel_id=1, source_target_pairs={{0,248},{8,0},{16,8},{24,16},{32,24},{40,32},{48,40},{56,48},{64,5... | collective-permute-start | bytes 1277960 | tf_op jit(solution)/shard_map/ppermute | solution.py:299
  13.8 3.9 %collective-permute-start.2 = (bf16[6,128,128]{2,1,0:T(8,128)(2,1)S(1)}, bf16[6,128,128]{2,1,0:T(8,128)(2,1)S(1)}, u32[]{:S(2)}, u32[]{:S(2)}) collective-permute-start(bf16[6,128,128]{2,1,0:T(8,128)(2,1)S(1)} %get-tuple-element.19), channel_id=1, source_target_pairs={{0,1},{1,2},{2,3},{3,4},{4,5},{5,6},{6,7},{8,9},{9,10},{10,11},{11... | collective-permute-start | bytes 589832 | tf_op jit(solution)/shard_map/ppermute | solution.py:299
  17.7 1.9 %collective-permute-start.3 = (bf16[6,128,128]{2,1,0:T(8,128)(2,1)S(1)}, bf16[6,128,128]{2,1,0:T(8,128)(2,1)S(1)}, u32[]{:S(2)}, u32[]{:S(2)}) collective-permute-start(bf16[6,128,128]{2,1,0:T(8,128)(2,1)S(1)} %get-tuple-element.20), channel_id=1, source_target_pairs={{1,0},{2,1},{3,2},{4,3},{5,4},{6,5},{7,6},{9,8},{10,9},{11,10},{12... | collective-permute-start | bytes 589832 | tf_op jit(solution)/shard_map/ppermute | solution.py:299
  20.3 0.0 copy-start.1
  20.3 0.0 copy-start.3
  20.3 0.0 copy-start.4
  20.3 0.0 copy-start.6
  20.4 3.8 %load.1.blocks_ref = bf16[26,11,128,128]{3,2,1,0:T(8,128)(2,1)S(1)} custom-call(bf16[26,11,128,128]{3,2,1,0:T(8,128)(2,1)} %blocks_hbm.1, bf16[26,128,128]{2,1,0:T(8,128)(2,1)S(1)} %get-tuple-element.16.after_ref.operand_ref), custom_call_target="tpu_custom_call" | custom-call | bytes 18743296 | tf_op jit(solution)/shard_map/load/pallas_call | solution.py:242
  24.1 0.0 collective-permute-done.2.halo2
  24.2 0.6 collective-permute-done.3.halo3
  24.7 0.0 collective-permute-done.halo0
  24.7 0.0 collective-permute-done.1.halo1
  24.8 4.0 %product.2 = (f32[26,128,128]{2,1,0:T(8,128)S(1)}, f32[128,128]{1,0:T(8,128)S(1)}, bf16[26,128,128]{2,1,0:T(8,128)(2,1)S(1)}, bf16[13,128,128]{2,1,0:T(8,128)(2,...) custom-call(s32[11,26]{1,0:T(8,128)S(1)} %bitcast.14, ...), custom_call_target="tpu_custom_call" | custom-call | tf_op jit(solution)/shard_map/product/pallas_call | solution.py:261
  28.8 0.1 collective-permute-start.4
  28.9 4.8 %collective-permute-start.5 = (bf16[13,128,128]{2,1,0:T(8,128)(2,1)S(1)}, bf16[13,128,128]{2,1,0:T(8,128)(2,1)S(1)}, u32[]{:S(2)}, u32[]{:S(2)}) collective-permute-start(bf16[13,128,128]{2,1,0:T(8,128)(2,1)S(1)} %get-tuple-element.25), channel_id=1, source_target_pairs={{0,248},{8,0},{16,8},{24,16},{32,24},{40,32},{48,40},{56,48},{64,5... | collective-permute-start | bytes 1277960 | tf_op jit(solution)/shard_map/ppermute | solution.py:299
  33.7 3.9 %collective-permute-start.6 = (bf16[6,128,128]{2,1,0:T(8,128)(2,1)S(1)}, bf16[6,128,128]{2,1,0:T(8,128)(2,1)S(1)}, u32[]{:S(2)}, u32[]{:S(2)}) collective-permute-start(bf16[6,128,128]{2,1,0:T(8,128)(2,1)S(1)} %get-tuple-element.26), channel_id=1, source_target_pairs={{0,1},{1,2},{2,3},{3,4},{4,5},{5,6},{6,7},{8,9},{9,10},{10,11},{11... | collective-permute-start | bytes 589832 | tf_op jit(solution)/shard_map/ppermute | solution.py:299
  37.5 1.9 %collective-permute-start.7 = (bf16[6,128,128]{2,1,0:T(8,128)(2,1)S(1)}, bf16[6,128,128]{2,1,0:T(8,128)(2,1)S(1)}, u32[]{:S(2)}, u32[]{:S(2)}) collective-permute-start(bf16[6,128,128]{2,1,0:T(8,128)(2,1)S(1)} %get-tuple-element.27), channel_id=1, source_target_pairs={{1,0},{2,1},{3,2},{4,3},{5,4},{6,5},{7,6},{9,8},{10,9},{11,10},{12... | collective-permute-start | bytes 589832 | tf_op jit(solution)/shard_map/ppermute | solution.py:299
  39.5 0.7 collective-permute-done.6.halo2
  40.1 4.4 %collective-permute-done.7.halo3 = bf16[6,128,128]{2,1,0:T(8,128)(2,1)S(1)} collective-permute-done((bf16[6,128,128]{2,1,0:T(8,128)(2,1)S(1)}, bf16[6,128,128]{2,1,0:T(8,128)(2,1)S(1)}, u32[]{:S(2)}, u32[]{:S(2)}) %collective-permute-start.7) | collective-permute-done | bytes 196640 | tf_op jit(solution)/shard_map/ppermute | solution.py:299
  44.5 0.0 collective-permute-done.5.halo1
  44.5 4.0 %product.3 = (f32[26,128,128]{2,1,0:T(8,128)S(1)}, f32[128,128]{1,0:T(8,128)S(1)}) custom-call(s32[11,26]{1,0:T(8,128)S(1)} %bitcast.15, s32[38]{0:T(128)S(1)} %copy-done.6, s32[1]{0:T(128)S(6)} %copy.14.count_ref, f32[26,128]{1,0:T(8,128)S(1)} %copy-done.3, f32[26,128,128]{2,1,0:T(8,128)S(1)} %get-tuple-element.22.current_ref, ...), custom_call_target="tpu_custom_call" | custom-call | tf_op jit(solution)/shard_map/product/pallas_call | solution.py:261
  48.6 15.1 %all_to_all.15 = f32[8,2,16,128]{3,2,1,0:T(8,128)S(1)} all-to-all(f32[8,2,16,128]{3,2,1,0:T(8,128)S(1)} %maximum_bitcast_fusion), channel_id=1, replica_groups=mesh['group'=32,'dom'=8] {'dom'}, dimensions={0} | all-to-all | bytes 262144 | tf_op jit(solution)/shard_map/all_to_all | solution.py:317
  63.7 0.1 broadcast_in_dim.6
  63.8 19.6 %all_to_all.16 = f32[32,2,16,128]{3,2,1,0:T(8,128)S(1)} all-to-all(f32[32,2,16,128]{3,2,1,0:T(8,128)S(1)} %broadcast_in_dim.6), channel_id=1, replica_groups=mesh['group'=32,'dom'=8] {'group'}, dimensions={0} | all-to-all | bytes 1048576 | tf_op jit(solution)/shard_map/all_to_all | solution.py:310
  83.4 10.9 %all_to_all.17 = f32[8,2,16,128]{3,2,1,0:T(8,128)S(1)} all-to-all(f32[8,2,16,128]{3,2,1,0:T(8,128)S(1)} %broadcast_in_dim.7), channel_id=1, replica_groups=mesh['group'=32,'dom'=8] {'dom'}, dimensions={0} | all-to-all | bytes 262144 | tf_op jit(solution)/shard_map/all_to_all | solution.py:310
  94.4 12.6 %last.1 = (f32[26,128,128]{2,1,0:T(8,128)}, f32[128,128]{1,0:T(8,128)}) custom-call(f32[2,128,128]{2,1,0:T(8,128)S(1)} %bitcast.11, f32[26,128,128]{2,1,0:T(8,128)S(1)} %get-tuple-element.29.image_ref), custom_call_target="tpu_custom_call" | custom-call | tf_op jit(solution)/shard_map/last/pallas_call | solution.py:280
  (12 shorter events, 0.1 us)
Async XLA Ops:
  0.6 1.5 %copy-start = (f32[26,128,128]{2,1,0:T(8,128)S(1)}, f32[26,128,128]{2,1,0:T(8,128)}, u32[]{:S(2)}) copy-start(f32[26,128,128]{2,1,0:T(8,128)} %current_ref.1) | copy-start | bytes 5111812
  2.1 0.7 copy-start.2
  2.8 0.7 copy-start.5
  4.7 20.0 %collective-permute-start = (bf16[13,128,128]{2,1,0:T(8,128)(2,1)S(1)}, bf16[13,128,128]{2,1,0:T(8,128)(2,1)S(1)}, u32[]{:S(2)}, u32[]{:S(2)}) collective-permute-start(bf16[13,128,128]{2,1,0:T(8,128)(2,1)S(1)} %get-tuple-element.17), channel_id=1, source_target_pairs={{0,8},{8,16},{16,24},{24,32},{32,40},{40,48},{48,56},{56,64},{64,7... | collective-permute-start | bytes 1277960 | tf_op jit(solution)/shard_map/ppermute | solution.py:299
  7.0 17.8 %collective-permute-start.1 = (bf16[13,128,128]{2,1,0:T(8,128)(2,1)S(1)}, bf16[13,128,128]{2,1,0:T(8,128)(2,1)S(1)}, u32[]{:S(2)}, u32[]{:S(2)}) collective-permute-start(bf16[13,128,128]{2,1,0:T(8,128)(2,1)S(1)} %get-tuple-element.18), channel_id=1, source_target_pairs={{0,248},{8,0},{16,8},{24,16},{32,24},{40,32},{48,40},{56,48},{64,5... | collective-permute-start | bytes 1277960 | tf_op jit(solution)/shard_map/ppermute | solution.py:299
  13.8 10.4 %collective-permute-start.2 = (bf16[6,128,128]{2,1,0:T(8,128)(2,1)S(1)}, bf16[6,128,128]{2,1,0:T(8,128)(2,1)S(1)}, u32[]{:S(2)}, u32[]{:S(2)}) collective-permute-start(bf16[6,128,128]{2,1,0:T(8,128)(2,1)S(1)} %get-tuple-element.19), channel_id=1, source_target_pairs={{0,1},{1,2},{2,3},{3,4},{4,5},{5,6},{6,7},{8,9},{9,10},{10,11},{11... | collective-permute-start | bytes 589832 | tf_op jit(solution)/shard_map/ppermute | solution.py:299
  17.7 7.0 %collective-permute-start.3 = (bf16[6,128,128]{2,1,0:T(8,128)(2,1)S(1)}, bf16[6,128,128]{2,1,0:T(8,128)(2,1)S(1)}, u32[]{:S(2)}, u32[]{:S(2)}) collective-permute-start(bf16[6,128,128]{2,1,0:T(8,128)(2,1)S(1)} %get-tuple-element.20), channel_id=1, source_target_pairs={{1,0},{2,1},{3,2},{4,3},{5,4},{6,5},{7,6},{9,8},{10,9},{11,10},{12... | collective-permute-start | bytes 589832 | tf_op jit(solution)/shard_map/ppermute | solution.py:299
  20.3 4.4 %copy-start.1 = (f32[26,128,128]{2,1,0:T(8,128)S(1)}, f32[26,128,128]{2,1,0:T(8,128)}, u32[]{:S(2)}) copy-start(f32[26,128,128]{2,1,0:T(8,128)} %current_ref.1) | copy-start | bytes 5111812
  20.3 4.4 %copy-start.3 = (f32[26,128]{1,0:T(8,128)S(1)}, f32[26,128]{1,0:T(8,128)}, u32[]{:S(2)}) copy-start(f32[26,128]{1,0:T(8,128)} %degree_ref.5) | copy-start | bytes 39940
  20.3 4.4 %copy-start.4 = (s32[26,11]{0,1:T(8,128)S(1)}, s32[26,11]{0,1:T(8,128)}, u32[]{:S(2)}) copy-start(s32[26,11]{0,1:T(8,128)} %param.7) | copy-start | bytes 3436
  20.3 4.4 %copy-start.6 = (s32[38]{0:T(128)S(1)}, s32[38]{0:T(128)}, u32[]{:S(2)}) copy-start(s32[38]{0:T(128)} %sends_ref.5) | copy-start | bytes 460
  28.8 15.7 %collective-permute-start.4 = (bf16[13,128,128]{2,1,0:T(8,128)(2,1)S(1)}, bf16[13,128,128]{2,1,0:T(8,128)(2,1)S(1)}, u32[]{:S(2)}, u32[]{:S(2)}) collective-permute-start(bf16[13,128,128]{2,1,0:T(8,128)(2,1)S(1)} %get-tuple-element.24), channel_id=1, source_target_pairs={{0,8},{8,16},{16,24},{24,32},{32,40},{40,48},{48,56},{56,64},{64,7... | collective-permute-start | bytes 1277960 | tf_op jit(solution)/shard_map/ppermute | solution.py:299
  28.9 15.6 %collective-permute-start.5 = (bf16[13,128,128]{2,1,0:T(8,128)(2,1)S(1)}, bf16[13,128,128]{2,1,0:T(8,128)(2,1)S(1)}, u32[]{:S(2)}, u32[]{:S(2)}) collective-permute-start(bf16[13,128,128]{2,1,0:T(8,128)(2,1)S(1)} %get-tuple-element.25), channel_id=1, source_target_pairs={{0,248},{8,0},{16,8},{24,16},{32,24},{40,32},{48,40},{56,48},{64,5... | collective-permute-start | bytes 1277960 | tf_op jit(solution)/shard_map/ppermute | solution.py:299
  33.7 6.5 %collective-permute-start.6 = (bf16[6,128,128]{2,1,0:T(8,128)(2,1)S(1)}, bf16[6,128,128]{2,1,0:T(8,128)(2,1)S(1)}, u32[]{:S(2)}, u32[]{:S(2)}) collective-permute-start(bf16[6,128,128]{2,1,0:T(8,128)(2,1)S(1)} %get-tuple-element.26), channel_id=1, source_target_pairs={{0,1},{1,2},{2,3},{3,4},{4,5},{5,6},{6,7},{8,9},{9,10},{10,11},{11... | collective-permute-start | bytes 589832 | tf_op jit(solution)/shard_map/ppermute | solution.py:299
  37.5 7.0 %collective-permute-start.7 = (bf16[6,128,128]{2,1,0:T(8,128)(2,1)S(1)}, bf16[6,128,128]{2,1,0:T(8,128)(2,1)S(1)}, u32[]{:S(2)}, u32[]{:S(2)}) collective-permute-start(bf16[6,128,128]{2,1,0:T(8,128)(2,1)S(1)} %get-tuple-element.27), channel_id=1, source_target_pairs={{1,0},{2,1},{3,2},{4,3},{5,4},{6,5},{7,6},{9,8},{10,9},{11,10},{12... | collective-permute-start | bytes 589832 | tf_op jit(solution)/shard_map/ppermute | solution.py:299

commit v3 on v2

--- a/solution.py
+++ b/solution.py
@@ -50,6 +50,27 @@
     return wide_ref[:, :width] + (cross + cross.T)
 
 
+def pack_gram(gram):
+    half, quarter = gram.shape[0] // 2, gram.shape[0] // 4
+    left = lax.broadcasted_iota(jnp.int32, (half, gram.shape[1]), 1) < half
+    low = gram[half:]
+    blocks = jnp.where(left, gram[:half], low)
+    corner = jnp.where(left[:quarter], low[:quarter], pltpu.roll(low[quarter:], half, 1))
+    return jnp.concatenate([blocks, corner], axis=0)
+
+
+def unpack_gram(packed):
+    size = packed.shape[1]
+    half = size // 2
+    left = lax.broadcasted_iota(jnp.int32, (half, size), 1) < half
+    corner = jnp.concatenate([packed[half:], pltpu.roll(packed[half:], half, 1)], axis=0)
+    low = jnp.where(left, corner, packed[:half])
+    full = jnp.concatenate([packed[:half], low], axis=0)
+    rows = lax.broadcasted_iota(jnp.int32, (size, size), 0)
+    columns = lax.broadcasted_iota(jnp.int32, (size, size), 1)
+    return jnp.where(rows > columns, full, 0.0) + jnp.where(rows >= columns, full, 0.0).T
+
+
 def put_sends(out_refs, sends_ref, block_ref):
     base = 0
     for out_ref in out_refs:
@@ -58,9 +79,24 @@
         base += out_ref.shape[0]
 
 
-def prep_kernel(sends_ref, degree_ref, start_ref, operand_ref, *out_refs):
+def prep_kernel(sends_hbm, degree_hbm, start_hbm, token_ref, operand_ref, *refs):
+    out_refs = refs[:4]
+    sends_ref, degree_ref, start_ref, sems = refs[4:]
+    half = start_ref.shape[0] // 2
+    halves = [pl.ds(0, half), pl.ds(half, half)]
+    copies = [pltpu.make_async_copy(degree_hbm, degree_ref, sems.at[0])]
+    copies += [pltpu.make_async_copy(start_hbm.at[part], start_ref.at[part], sems.at[1 + i])
+               for i, part in enumerate(halves)]
+    copies += [pltpu.make_async_copy(sends_hbm, sends_ref, sems.at[3])]
+    for copy in copies:
+        copy.start()
+    token_ref[...] = jnp.zeros_like(token_ref)
+    copies[0].wait()
     for s, scale in enumerate(scale_blocks(degree_ref)):
+        if s % half == 0:
+            copies[1 + s // half].wait()
         operand_ref[s] = (scale * start_ref[s]).astype(BF16)
+    copies[3].wait()
     put_sends(out_refs, sends_ref, operand_ref)
 
 
@@ -71,7 +107,7 @@
 
 
 def product_kernel(sending, columns_ref, sends_ref, count_ref, degree_ref, current_ref, operand_ref,
-                   blocks_ref, halo0, halo1, halo2, halo3, image_ref, gram_ref, *refs):
+                   blocks_ref, halo0, halo1, halo2, halo3, other_ref, image_ref, gram_ref, *refs):
     next_ref, out_refs = (refs[0], refs[1:5]) if sending else (None, ())
     ext_ref, scale_ref, parts_ref, wide_ref, side_ref = refs[1 + len(out_refs) if sending else 0:]
     slots, per_row = blocks_ref.shape[:2]
@@ -113,7 +149,8 @@
         image_ref[s] = jnp.zeros(image_ref.shape[1:], F32)
         return carry
     lax.fori_loop(steps * group, slots, dead, 0)
-    gram_ref[...] = finish_gram(wide_ref, side_ref)
+    gram = pack_gram(finish_gram(wide_ref, side_ref))
+    gram_ref[...] = gram if sending else jnp.concatenate([other_ref[...], gram], axis=0)
     if sending:
         put_sends(out_refs, sends_ref, next_ref)
 
@@ -195,10 +232,12 @@
 def last_kernel(denominator, grams_ref, image_ref, basis_hbm, factor_ref,
                 work_ref, weights_ref, basis_ref, out_sems):
     slots, nodes, width = image_ref.shape
-    start_factor(grams_ref[0], denominator, work_ref)
+    half_rows = grams_ref.shape[0] // 2
+    start_factor(unpack_gram(grams_ref[:half_rows]), denominator, work_ref)
     first = work_ref[:, width:]
     turned = first.T
-    rows, columns = start_factor(dot_full(dot_full(first, grams_ref[1]), turned), denominator, work_ref)
+    second = dot_full(dot_full(first, unpack_gram(grams_ref[half_rows:])), turned)
+    rows, columns = start_factor(second, denominator, work_ref)
     wide_weights(dot_full(turned, work_ref[:, width:].T), weights_ref)
     half = slots // 2
 
@@ -229,10 +268,16 @@
     slots, nodes, width = start.shape
     return pl.pallas_call(
         prep_kernel,
-        out_shape=[spread((n, nodes, width), BF16) for n in (slots,) + sizes],
-        in_specs=[SMEM, VMEM, VMEM],
-        out_specs=[VMEM] * 5,
-        compiler_params=params(16),
+        out_shape=[spread((8, width), F32)] + [spread((n, nodes, width), BF16) for n in (slots,) + sizes],
+        in_specs=[ANY] * 3,
+        out_specs=[VMEM] * 6,
+        scratch_shapes=[
+            pltpu.SMEM(sends.shape, sends.dtype),
+            pltpu.VMEM(degree.shape, F32),
+            pltpu.VMEM(start.shape, F32),
+            pltpu.SemaphoreType.DMA((4,)),
+        ],
+        compiler_params=params(58),
         name="prep",
     )(sends, degree, start)
 
@@ -251,17 +296,19 @@
     )(blocks, after)
 
 
-def product(columns, sends, count, degree, current, operand, blocks, halos, sending):
+def product(columns, sends, count, degree, current, operand, blocks, halos, other):
     slots, nodes, width = current.shape
     sizes = [h.shape[0] for h in halos]
-    out_shape = [spread(current.shape, F32), spread((width, width), F32)]
+    sending = other is None
+    rows = 3 * width // 4
+    out_shape = [spread(current.shape, F32), spread((rows if sending else 2 * rows, width), F32)]
     if sending:
         out_shape += [spread((n, nodes, width), BF16) for n in [slots] + sizes]
     group = 2
     return pl.pallas_call(
         functools.partial(product_kernel, sending),
         out_shape=out_shape,
-        in_specs=[SMEM] * 3 + [VMEM] * 8,
+        in_specs=[SMEM] * 3 + [VMEM] * 9,
         out_specs=[VMEM] * len(out_shape),
         scratch_shapes=[
             pltpu.VMEM((slots + sum(sizes), nodes, width), BF16),
@@ -272,7 +319,7 @@
         ],
         compiler_params=params(28),
         name="product",
-    )(columns, sends, count, degree, current, operand, blocks, *halos)
+    )(columns, sends, count, degree, current, operand, blocks, *halos, degree if sending else other)
 
 
 def last(grams, image, denominator):
@@ -311,13 +358,10 @@
 
 
 def summed(grams):
-    count, rows, width = grams.shape
-    parts = lax.axis_size("dom")
-    pieces = grams.reshape(count, parts, rows // parts, width).transpose(1, 0, 2, 3)
+    pieces = grams.reshape(lax.axis_size("dom"), -1, grams.shape[1])
     mine = lax.all_to_all(pieces, "dom", 0, 0, tiled=True).sum(0)
     mine = collected(mine, "group").sum(0)
-    whole = collected(mine, "dom")
-    return whole.transpose(1, 0, 2, 3).reshape(grams.shape)
+    return collected(mine, "dom").reshape(grams.shape)
 
 
 def body(blocks, columns, sends, active_row_count, degree, start):
@@ -325,12 +369,11 @@
     denominator = lax.axis_size("group") * lax.axis_size("dom") * slots * nodes
     sizes = (slots // 2, slots // 2, slots // 4, slots // 4)
     table = (columns.T, sends, active_row_count, degree)
-    operand, *sent = prep(sends, degree, start, sizes)
-    blocks = load(blocks, operand)
-    image, first_gram, operand, *sent = product(*table, start, operand, blocks, exchange(sent), True)
-    image, gram = product(*table, image, operand, blocks, exchange(sent), False)
-    grams = summed(jnp.stack([first_gram, gram]))
-    return last(grams, image, denominator)
+    token, operand, *sent = prep(sends, degree, start, sizes)
+    blocks = load(blocks, token)
+    image, first_gram, operand, *sent = product(*table, start, operand, blocks, exchange(sent), None)
+    image, grams = product(*table, image, operand, blocks, exchange(sent), first_gram)
+    return last(summed(grams), image, denominator)
 
 
 def solution(mesh):

time: 107 us -> 105 us (0.981)
  Pallas kernels: 25.7 us -> 28.6 us
  blocking collectives: 45.6 us -> 43.5 us
  local copies, waits for them, and re-layouts: 2.92 us -> 1.13 us
    all_to_all x1, blocking collectives: 15.1 us -> 9.98 us  [summed(): mine = lax.all_to_all(pieces, 'dom', 0, 0, tiled=True).sum(0)]
    all_to_all x2, blocking collectives: 30.5 us -> 33.5 us  [collected(): lax.all_to_all(jnp.broadcast_to(value, (size,) + value.shape), axis, 0, 0...]
    unnamed x14 -> x12, local copies, waits for them, and re-layouts: 2.85 us -> 1.09 us
    pallas_call x1, Pallas kernels: 1.28 us -> 2.95 us  [prep(): pl.pallas_call(prep_kernel, out_shape=[spread((8, width), F32)] + [spread...]
where the time goes in v3:
time: 105 us; the launch traced here: 106 us
  blocking collectives  43.5 us (41%)
  Pallas kernels  28.6 us (27%)
  starting transfers between devices  26 us (25%)
  waiting for transfers between devices  5.04 us (5%)
  between operations  1.56 us (1%)
  local copies, waits for them, and re-layouts  1.13 us (1%)
    all_to_all x2, blocking collectives, collected(): lax.all_to_all(jnp.broadcast_to(value, (size,) + value.shape), axis, 0, 0...  33.5 us
    ppermute x8, starting transfers between devices, shift(): return lax.ppermute(shard, axis, route)  26 us
    pallas_call x1, Pallas kernels, last(): pl.pallas_call(functools.partial(last_kernel, denominator), out_shape=[sp...  12.8 us
    all_to_all x1, blocking collectives, summed(): mine = lax.all_to_all(pieces, 'dom', 0, 0, tiled=True).sum(0)  9.98 us
    pallas_call x2, Pallas kernels, product(): pl.pallas_call(functools.partial(product_kernel, sending), out_shape=out_...  9.06 us
    ppermute x8, waiting for transfers between devices, shift(): return lax.ppermute(shard, axis, route)  5.04 us
    pallas_call x1, Pallas kernels, load(): pl.pallas_call(load_kernel, out_shape=spread(blocks.shape, blocks.dtype),...  3.82 us
    pallas_call x1, Pallas kernels, prep(): pl.pallas_call(prep_kernel, out_shape=[spread((8, width), F32)] + [spread...  2.95 us
  transfers between devices with their start and end apart: 8, of which 3 were waited for; matrix products, arithmetic and copies ran while one was open for 0% of the time, Pallas kernels for 4%

profile of v3, /device:TPU:1, one launch (start us, length us, event | category | flops | bytes accessed | tf_op | source)
XLA Modules:
  0.0 105.8 jit_solution(3621203444557211786)
XLA Ops:
  0.6 2.9 %prep.1 = (f32[8,128]{1,0:T(8,128)}, bf16[26,128,128]{2,1,0:T(8,128)(2,1)}, bf16[13,128,128]{2,1,0:T(8,128)(2,1)}, bf16[13,128,128]{2,1,0:T(8,128)(2,1)}, bf16[6...) custom-call(s32[38]{0:T(128)} %sends_ref.3, f32[26,128]{1,0:T(8,128)} %degree_ref.3, f32[26,128,128]{2,1,0:T(8,128)} %current_ref.1), custom_call_target="tpu_custom_call" | custom-call | tf_op jit(solution)/shard_map/prep/pallas_call | solution.py:269
  3.6 2.2 %collective-permute-start = (bf16[13,128,128]{2,1,0:T(8,128)(2,1)}, bf16[13,128,128]{2,1,0:T(8,128)(2,1)S(1)}, u32[]{:S(2)}, u32[]{:S(2)}) collective-permute-start(bf16[13,128,128]{2,1,0:T(8,128)(2,1)} %get-tuple-element.19), channel_id=1, source_target_pairs={{0,8},{8,16},{16,24},{24,32},{32,40},{40,48},{48,56},{56,64},{64,7... | collective-permute-start | bytes 1277960 | tf_op jit(solution)/shard_map/ppermute | solution.py:346
  5.8 6.8 %collective-permute-start.1 = (bf16[13,128,128]{2,1,0:T(8,128)(2,1)}, bf16[13,128,128]{2,1,0:T(8,128)(2,1)S(1)}, u32[]{:S(2)}, u32[]{:S(2)}) collective-permute-start(bf16[13,128,128]{2,1,0:T(8,128)(2,1)} %get-tuple-element.20), channel_id=1, source_target_pairs={{0,248},{8,0},{16,8},{24,16},{32,24},{40,32},{48,40},{56,48},{64,5... | collective-permute-start | bytes 1277960 | tf_op jit(solution)/shard_map/ppermute | solution.py:346
  12.6 3.9 %collective-permute-start.2 = (bf16[6,128,128]{2,1,0:T(8,128)(2,1)}, bf16[6,128,128]{2,1,0:T(8,128)(2,1)S(1)}, u32[]{:S(2)}, u32[]{:S(2)}) collective-permute-start(bf16[6,128,128]{2,1,0:T(8,128)(2,1)} %get-tuple-element.21), channel_id=1, source_target_pairs={{0,1},{1,2},{2,3},{3,4},{4,5},{5,6},{6,7},{8,9},{9,10},{10,11},{11... | collective-permute-start | bytes 589832 | tf_op jit(solution)/shard_map/ppermute | solution.py:346
  16.6 1.9 %collective-permute-start.3 = (bf16[6,128,128]{2,1,0:T(8,128)(2,1)}, bf16[6,128,128]{2,1,0:T(8,128)(2,1)S(1)}, u32[]{:S(2)}, u32[]{:S(2)}) collective-permute-start(bf16[6,128,128]{2,1,0:T(8,128)(2,1)} %get-tuple-element.22), channel_id=1, source_target_pairs={{1,0},{2,1},{3,2},{4,3},{5,4},{6,5},{7,6},{9,8},{10,9},{11,10},{12... | collective-permute-start | bytes 589832 | tf_op jit(solution)/shard_map/ppermute | solution.py:346
  19.1 0.0 copy-start.5
  19.1 0.7 copy-done.5
  19.8 0.0 copy-start.4
  19.8 3.8 %load.1.blocks_ref = bf16[26,11,128,128]{3,2,1,0:T(8,128)(2,1)S(1)} custom-call(bf16[26,11,128,128]{3,2,1,0:T(8,128)(2,1)} %blocks_hbm.1, f32[8,128]{1,0:T(8,128)S(1)} %copy-done.5), custom_call_target="tpu_custom_call" | custom-call | bytes 18743296 | tf_op jit(solution)/shard_map/load/pallas_call | solution.py:287
  23.7 0.0 collective-permute-done.2.halo2
  23.7 0.1 collective-permute-done.3.halo3
  23.8 0.0 collective-permute-done.halo0
  23.8 0.0 collective-permute-done.1.halo1
  23.8 0.2 copy-done
  23.9 0.2 copy-done.1
  24.2 0.0 copy-done.2
  24.2 0.0 copy-done.3
  24.2 0.0 copy-done.4
  24.2 4.5 %product.2 = (f32[26,128,128]{2,1,0:T(8,128)S(1)}, f32[96,128]{1,0:T(8,128)S(1)}, bf16[26,128,128]{2,1,0:T(8,128)(2,1)S(1)}, bf16[13,128,128]{2,1,0:T(8,128)(2,1...) custom-call(s32[11,26]{1,0:T(8,128)S(1)} %bitcast.5, ...), custom_call_target="tpu_custom_call" | custom-call | tf_op jit(solution)/shard_map/product/pallas_call | solution.py:308
  28.7 0.1 collective-permute-start.4
  28.8 4.8 %collective-permute-start.5 = (bf16[13,128,128]{2,1,0:T(8,128)(2,1)S(1)}, bf16[13,128,128]{2,1,0:T(8,128)(2,1)S(1)}, u32[]{:S(2)}, u32[]{:S(2)}) collective-permute-start(bf16[13,128,128]{2,1,0:T(8,128)(2,1)S(1)} %get-tuple-element.26), channel_id=1, source_target_pairs={{0,248},{8,0},{16,8},{24,16},{32,24},{40,32},{48,40},{56,48},{64,5... | collective-permute-start | bytes 1277960 | tf_op jit(solution)/shard_map/ppermute | solution.py:346
  33.6 4.2 %collective-permute-start.6 = (bf16[6,128,128]{2,1,0:T(8,128)(2,1)S(1)}, bf16[6,128,128]{2,1,0:T(8,128)(2,1)S(1)}, u32[]{:S(2)}, u32[]{:S(2)}) collective-permute-start(bf16[6,128,128]{2,1,0:T(8,128)(2,1)S(1)} %get-tuple-element.27), channel_id=1, source_target_pairs={{0,1},{1,2},{2,3},{3,4},{4,5},{5,6},{6,7},{8,9},{9,10},{10,11},{11... | collective-permute-start | bytes 589832 | tf_op jit(solution)/shard_map/ppermute | solution.py:346
  37.8 2.0 %collective-permute-start.7 = (bf16[6,128,128]{2,1,0:T(8,128)(2,1)S(1)}, bf16[6,128,128]{2,1,0:T(8,128)(2,1)S(1)}, u32[]{:S(2)}, u32[]{:S(2)}) collective-permute-start(bf16[6,128,128]{2,1,0:T(8,128)(2,1)S(1)} %get-tuple-element.28), channel_id=1, source_target_pairs={{1,0},{2,1},{3,2},{4,3},{5,4},{6,5},{7,6},{9,8},{10,9},{11,10},{12... | collective-permute-start | bytes 589832 | tf_op jit(solution)/shard_map/ppermute | solution.py:346
  39.8 0.6 collective-permute-done.6.halo2
  40.4 4.4 %collective-permute-done.7.halo3 = bf16[6,128,128]{2,1,0:T(8,128)(2,1)S(1)} collective-permute-done((bf16[6,128,128]{2,1,0:T(8,128)(2,1)S(1)}, bf16[6,128,128]{2,1,0:T(8,128)(2,1)S(1)}, u32[]{:S(2)}, u32[]{:S(2)}) %collective-permute-start.7) | collective-permute-done | bytes 196640 | tf_op jit(solution)/shard_map/ppermute | solution.py:346
  44.8 0.0 collective-permute-done.4.halo0
  44.8 0.0 collective-permute-done.5.halo1
  44.8 4.5 %product.3 = (f32[26,128,128]{2,1,0:T(8,128)S(1)}, f32[192,128]{1,0:T(8,128)S(1)}) custom-call(s32[11,26]{1,0:T(8,128)S(1)} %bitcast.6, s32[38]{0:T(128)S(1)} %copy-done.4, s32[1]{0:T(128)S(6)} %copy.8.count_ref, f32[26,128]{1,0:T(8,128)S(1)} %copy-done.2, f32[26,128,128]{2,1,0:T(8,128)S(1)} %get-tuple-element.23.current_ref, ...), custom_call_target="tpu_custom_call" | custom-call | tf_op jit(solution)/shard_map/product/pallas_call | solution.py:308
  49.3 10.0 %all_to_all.15 = f32[8,24,128]{2,1,0:T(8,128)S(1)} all-to-all(f32[8,24,128]{2,1,0:T(8,128)S(1)} %bitcast.4), channel_id=1, replica_groups=mesh['group'=32,'dom'=8] {'dom'}, dimensions={0} | all-to-all | bytes 196608 | tf_op jit(solution)/shard_map/all_to_all | solution.py:362
  59.3 23.7 %all_to_all.16 = f32[32,24,128]{2,1,0:T(8,128)S(1)} all-to-all(f32[32,24,128]{2,1,0:T(8,128)S(1)} %broadcast_in_dim.6), channel_id=1, replica_groups=mesh['group'=32,'dom'=8] {'group'}, dimensions={0} | all-to-all | bytes 786432 | tf_op jit(solution)/shard_map/all_to_all | solution.py:357
  83.1 9.8 %all_to_all.17 = f32[8,24,128]{2,1,0:T(8,128)S(1)} all-to-all(f32[8,24,128]{2,1,0:T(8,128)S(1)} %broadcast_in_dim.7), channel_id=1, replica_groups=mesh['group'=32,'dom'=8] {'dom'}, dimensions={0} | all-to-all | bytes 196608 | tf_op jit(solution)/shard_map/all_to_all | solution.py:357
  92.9 12.8 %last.1 = (f32[26,128,128]{2,1,0:T(8,128)}, f32[128,128]{1,0:T(8,128)}) custom-call(f32[192,128]{1,0:T(8,128)S(1)} %bitcast.3, f32[26,128,128]{2,1,0:T(8,128)S(1)} %get-tuple-element.31.image_ref), custom_call_target="tpu_custom_call" | custom-call | tf_op jit(solution)/shard_map/last/pallas_call | solution.py:327
  (8 shorter events, 0.1 us)
Async XLA Ops:
  3.6 20.2 %collective-permute-start = (bf16[13,128,128]{2,1,0:T(8,128)(2,1)}, bf16[13,128,128]{2,1,0:T(8,128)(2,1)S(1)}, u32[]{:S(2)}, u32[]{:S(2)}) collective-permute-start(bf16[13,128,128]{2,1,0:T(8,128)(2,1)} %get-tuple-element.19), channel_id=1, source_target_pairs={{0,8},{8,16},{16,24},{24,32},{32,40},{40,48},{48,56},{56,64},{64,7... | collective-permute-start | bytes 1277960 | tf_op jit(solution)/shard_map/ppermute | solution.py:346
  5.8 18.0 %collective-permute-start.1 = (bf16[13,128,128]{2,1,0:T(8,128)(2,1)}, bf16[13,128,128]{2,1,0:T(8,128)(2,1)S(1)}, u32[]{:S(2)}, u32[]{:S(2)}) collective-permute-start(bf16[13,128,128]{2,1,0:T(8,128)(2,1)} %get-tuple-element.20), channel_id=1, source_target_pairs={{0,248},{8,0},{16,8},{24,16},{32,24},{40,32},{48,40},{56,48},{64,5... | collective-permute-start | bytes 1277960 | tf_op jit(solution)/shard_map/ppermute | solution.py:346
  12.6 11.1 %collective-permute-start.2 = (bf16[6,128,128]{2,1,0:T(8,128)(2,1)}, bf16[6,128,128]{2,1,0:T(8,128)(2,1)S(1)}, u32[]{:S(2)}, u32[]{:S(2)}) collective-permute-start(bf16[6,128,128]{2,1,0:T(8,128)(2,1)} %get-tuple-element.21), channel_id=1, source_target_pairs={{0,1},{1,2},{2,3},{3,4},{4,5},{5,6},{6,7},{8,9},{9,10},{10,11},{11... | collective-permute-start | bytes 589832 | tf_op jit(solution)/shard_map/ppermute | solution.py:346
  16.6 7.2 %collective-permute-start.3 = (bf16[6,128,128]{2,1,0:T(8,128)(2,1)}, bf16[6,128,128]{2,1,0:T(8,128)(2,1)S(1)}, u32[]{:S(2)}, u32[]{:S(2)}) collective-permute-start(bf16[6,128,128]{2,1,0:T(8,128)(2,1)} %get-tuple-element.22), channel_id=1, source_target_pairs={{1,0},{2,1},{3,2},{4,3},{5,4},{6,5},{7,6},{9,8},{10,9},{11,10},{12... | collective-permute-start | bytes 589832 | tf_op jit(solution)/shard_map/ppermute | solution.py:346
  19.1 0.7 copy-start.5
  19.8 4.1 %copy-start = (f32[26,128,128]{2,1,0:T(8,128)S(1)}, f32[26,128,128]{2,1,0:T(8,128)}, u32[]{:S(2)}) copy-start(f32[26,128,128]{2,1,0:T(8,128)} %current_ref.1) | copy-start | bytes 5111812
  19.8 4.3 %copy-start.1 = (bf16[26,128,128]{2,1,0:T(8,128)(2,1)S(1)}, bf16[26,128,128]{2,1,0:T(8,128)(2,1)}, u32[]{:S(2)}) copy-start(bf16[26,128,128]{2,1,0:T(8,128)(2,1)} %get-tuple-element.17.operand_ref) | copy-start | bytes 2555908
  19.8 4.3 %copy-start.2 = (f32[26,128]{1,0:T(8,128)S(1)}, f32[26,128]{1,0:T(8,128)}, u32[]{:S(2)}) copy-start(f32[26,128]{1,0:T(8,128)} %degree_ref.3) | copy-start | bytes 39940
  19.8 4.3 %copy-start.3 = (s32[26,11]{0,1:T(8,128)S(1)}, s32[26,11]{0,1:T(8,128)}, u32[]{:S(2)}) copy-start(s32[26,11]{0,1:T(8,128)} %param.7) | copy-start | bytes 3436
  19.8 4.3 %copy-start.4 = (s32[38]{0:T(128)S(1)}, s32[38]{0:T(128)}, u32[]{:S(2)}) copy-start(s32[38]{0:T(128)} %sends_ref.3) | copy-start | bytes 460
  28.7 16.1 %collective-permute-start.4 = (bf16[13,128,128]{2,1,0:T(8,128)(2,1)S(1)}, bf16[13,128,128]{2,1,0:T(8,128)(2,1)S(1)}, u32[]{:S(2)}, u32[]{:S(2)}) collective-permute-start(bf16[13,128,128]{2,1,0:T(8,128)(2,1)S(1)} %get-tuple-element.25), channel_id=1, source_target_pairs={{0,8},{8,16},{16,24},{24,32},{32,40},{40,48},{48,56},{56,64},{64,7... | collective-permute-start | bytes 1277960 | tf_op jit(solution)/shard_map/ppermute | solution.py:346
  28.8 16.0 %collective-permute-start.5 = (bf16[13,128,128]{2,1,0:T(8,128)(2,1)S(1)}, bf16[13,128,128]{2,1,0:T(8,128)(2,1)S(1)}, u32[]{:S(2)}, u32[]{:S(2)}) collective-permute-start(bf16[13,128,128]{2,1,0:T(8,128)(2,1)S(1)} %get-tuple-element.26), channel_id=1, source_target_pairs={{0,248},{8,0},{16,8},{24,16},{32,24},{40,32},{48,40},{56,48},{64,5... | collective-permute-start | bytes 1277960 | tf_op jit(solution)/shard_map/ppermute | solution.py:346
  33.6 6.8 %collective-permute-start.6 = (bf16[6,128,128]{2,1,0:T(8,128)(2,1)S(1)}, bf16[6,128,128]{2,1,0:T(8,128)(2,1)S(1)}, u32[]{:S(2)}, u32[]{:S(2)}) collective-permute-start(bf16[6,128,128]{2,1,0:T(8,128)(2,1)S(1)} %get-tuple-element.27), channel_id=1, source_target_pairs={{0,1},{1,2},{2,3},{3,4},{4,5},{5,6},{6,7},{8,9},{9,10},{10,11},{11... | collective-permute-start | bytes 589832 | tf_op jit(solution)/shard_map/ppermute | solution.py:346
  37.8 7.0 %collective-permute-start.7 = (bf16[6,128,128]{2,1,0:T(8,128)(2,1)S(1)}, bf16[6,128,128]{2,1,0:T(8,128)(2,1)S(1)}, u32[]{:S(2)}, u32[]{:S(2)}) collective-permute-start(bf16[6,128,128]{2,1,0:T(8,128)(2,1)S(1)} %get-tuple-element.28), channel_id=1, source_target_pairs={{1,0},{2,1},{3,2},{4,3},{5,4},{6,5},{7,6},{9,8},{10,9},{11,10},{12... | collective-permute-start | bytes 589832 | tf_op jit(solution)/shard_map/ppermute | solution.py:346

commit v4 on v3

--- a/solution.py
+++ b/solution.py
@@ -1,4 +1,5 @@
 import functools
+import math
 import jax
 import jax.numpy as jnp
 from jax import lax
@@ -9,6 +10,7 @@
 AXES = ("group", "dom")
 F32, BF16 = jnp.float32, jnp.bfloat16
 PANEL = 16
+LIMIT1 = 36
 ANY = pl.BlockSpec(memory_space=pl.ANY)
 SMEM = pl.BlockSpec(memory_space=pltpu.SMEM)
 VMEM = pl.BlockSpec(memory_space=pltpu.VMEM)
@@ -79,9 +81,9 @@
         base += out_ref.shape[0]
 
 
-def prep_kernel(sends_hbm, degree_hbm, start_hbm, token_ref, operand_ref, *refs):
+def prep_kernel(sends_hbm, degree_hbm, start_hbm, *refs):
     out_refs = refs[:4]
-    sends_ref, degree_ref, start_ref, sems = refs[4:]
+    operand_ref, sends_ref, degree_ref, start_ref, sems = refs[4:]
     half = start_ref.shape[0] // 2
     halves = [pl.ds(0, half), pl.ds(half, half)]
     copies = [pltpu.make_async_copy(degree_hbm, degree_ref, sems.at[0])]
@@ -90,7 +92,6 @@
     copies += [pltpu.make_async_copy(sends_hbm, sends_ref, sems.at[3])]
     for copy in copies:
         copy.start()
-    token_ref[...] = jnp.zeros_like(token_ref)
     copies[0].wait()
     for s, scale in enumerate(scale_blocks(degree_ref)):
         if s % half == 0:
@@ -100,29 +101,40 @@
     put_sends(out_refs, sends_ref, operand_ref)
 
 
-def load_kernel(blocks_hbm, after_ref, blocks_ref, sem):
-    copy = pltpu.make_async_copy(blocks_hbm, blocks_ref, sem)
-    copy.start()
-    copy.wait()
-
-
-def product_kernel(sending, columns_ref, sends_ref, count_ref, degree_ref, current_ref, operand_ref,
-                   blocks_ref, halo0, halo1, halo2, halo3, other_ref, image_ref, gram_ref, *refs):
-    next_ref, out_refs = (refs[0], refs[1:5]) if sending else (None, ())
-    ext_ref, scale_ref, parts_ref, wide_ref, side_ref = refs[1 + len(out_refs) if sending else 0:]
+def chunk_bounds(slots, group):
+    steps = slots // group
+    return sorted({0, steps // 6, steps // 3, 2 * steps // 3, steps})
+
+
+def product_kernel(sending, columns_ref, sends_ref, count_ref, core_ref, degree_ref, current_ref,
+                   blocks_hbm, halo0, halo1, halo2, halo3, *refs):
+    ext_ref, scale_ref, next_ref, parts_ref, wide_ref, side_ref, sems = refs[-7:]
+    if sending:
+        image_ref, gram_ref, blocks_ref, *out_refs = refs[:-7]
+    else:
+        other_ref, image_ref, mine_ref, yours_ref = refs[:-7]
+        blocks_ref = blocks_hbm
     slots, per_row = blocks_ref.shape[:2]
     group = parts_ref.shape[1] // image_ref.shape[1]
     count = count_ref[0]
-    base = 0
-    for piece in (operand_ref, halo0, halo1, halo2, halo3):
+    bounds = chunk_bounds(slots, group)
+    copies = []
+    if sending:
+        for i, (low, high) in enumerate(zip(bounds, bounds[1:])):
+            chunk = pl.ds(low * group, (high - low) * group)
+            copies.append(pltpu.make_async_copy(blocks_hbm.at[chunk], blocks_ref.at[chunk], sems.at[i]))
+            copies[-1].start()
+    for s, scale in enumerate(scale_blocks(degree_ref)):
+        scale_ref[s] = scale
+        ext_ref[s] = (scale * current_ref[s]).astype(BF16)
+    base = slots
+    for piece in (halo0, halo1, halo2, halo3):
         size = piece.shape[0]
         ext_ref[base:base + size] = piece[...]
         base += size
     wide_ref[...] = jnp.zeros_like(wide_ref)
     side_ref[...] = jnp.zeros_like(side_ref)
     parts_ref[...] = jnp.zeros_like(parts_ref)
-    for s, scale in enumerate(scale_blocks(degree_ref)):
-        scale_ref[s] = scale
 
     def row(s):
         left = jnp.concatenate([blocks_ref[s, k] for k in range(per_row)], axis=1)
@@ -142,7 +154,10 @@
             parts_ref[i] = part
         return carry
     steps = (count + group - 1) // group
-    lax.fori_loop(0, steps, rows, 0)
+    for i, (low, high) in enumerate(zip(bounds, bounds[1:])):
+        if sending:
+            copies[i].wait()
+        lax.fori_loop(low, jnp.minimum(high, steps), rows, 0)
     add_gram([parts_ref[i] for i in range(3)], wide_ref, side_ref)
 
     def dead(s, carry):
@@ -150,9 +165,13 @@
         return carry
     lax.fori_loop(steps * group, slots, dead, 0)
     gram = pack_gram(finish_gram(wide_ref, side_ref))
-    gram_ref[...] = gram if sending else jnp.concatenate([other_ref[...], gram], axis=0)
     if sending:
+        gram_ref[...] = gram
         put_sends(out_refs, sends_ref, next_ref)
+    else:
+        other, low_core = other_ref[...], core_ref[0] == 0
+        mine_ref[...] = jnp.where(low_core, other, gram)
+        yours_ref[...] = jnp.where(low_core, gram, other)
 
 
 def gather_rows(rows, sublane):
@@ -229,14 +248,15 @@
     return both[:, :width] + both[:, width:]
 
 
-def last_kernel(denominator, grams_ref, image_ref, basis_hbm, factor_ref,
+def last_kernel(denominator, core_ref, mine_ref, yours_ref, image_ref, basis_hbm, factor_ref,
                 work_ref, weights_ref, basis_ref, out_sems):
     slots, nodes, width = image_ref.shape
-    half_rows = grams_ref.shape[0] // 2
-    start_factor(unpack_gram(grams_ref[:half_rows]), denominator, work_ref)
+    low_core = core_ref[0] == 0
+    mine, yours = mine_ref[...], yours_ref[...]
+    start_factor(unpack_gram(jnp.where(low_core, mine, yours)), denominator, work_ref)
     first = work_ref[:, width:]
     turned = first.T
-    second = dot_full(dot_full(first, unpack_gram(grams_ref[half_rows:])), turned)
+    second = dot_full(dot_full(first, unpack_gram(jnp.where(low_core, yours, mine))), turned)
     rows, columns = start_factor(second, denominator, work_ref)
     wide_weights(dot_full(turned, work_ref[:, width:].T), weights_ref)
     half = slots // 2
@@ -268,10 +288,11 @@
     slots, nodes, width = start.shape
     return pl.pallas_call(
         prep_kernel,
-        out_shape=[spread((8, width), F32)] + [spread((n, nodes, width), BF16) for n in (slots,) + sizes],
+        out_shape=[spread((n, nodes, width), BF16) for n in sizes],
         in_specs=[ANY] * 3,
-        out_specs=[VMEM] * 6,
+        out_specs=[VMEM] * 4,
         scratch_shapes=[
+            pltpu.VMEM(start.shape, BF16),
             pltpu.SMEM(sends.shape, sends.dtype),
             pltpu.VMEM(degree.shape, F32),
             pltpu.VMEM(start.shape, F32),
@@ -282,52 +303,43 @@
     )(sends, degree, start)
 
 
-def load(blocks, after):
-    size = blocks.size * blocks.dtype.itemsize
-    return pl.pallas_call(
-        load_kernel,
-        out_shape=spread(blocks.shape, blocks.dtype),
-        in_specs=[ANY, ANY],
-        out_specs=VMEM,
-        scratch_shapes=[pltpu.SemaphoreType.DMA(())],
-        compiler_params=params(40),
-        cost_estimate=pl.CostEstimate(flops=0, bytes_accessed=2 * size, transcendentals=0),
-        name="load",
-    )(blocks, after)
-
-
-def product(columns, sends, count, degree, current, operand, blocks, halos, other):
+def product(columns, sends, count, core, degree, current, blocks, halos, other):
     slots, nodes, width = current.shape
     sizes = [h.shape[0] for h in halos]
     sending = other is None
-    rows = 3 * width // 4
-    out_shape = [spread(current.shape, F32), spread((rows if sending else 2 * rows, width), F32)]
+    group = 2
+    packed = spread((3 * width // 4, width), F32)
+    out_shape = [spread(current.shape, F32), packed]
     if sending:
-        out_shape += [spread((n, nodes, width), BF16) for n in [slots] + sizes]
-    group = 2
+        out_shape += [spread(blocks.shape, BF16)]
+        out_shape += [spread(h.shape, BF16) for h in halos]
+    else:
+        out_shape += [packed]
     return pl.pallas_call(
         functools.partial(product_kernel, sending),
         out_shape=out_shape,
-        in_specs=[SMEM] * 3 + [VMEM] * 9,
+        in_specs=[SMEM] * 4 + [VMEM] * 2 + [ANY if sending else VMEM] + [VMEM] * (4 if sending else 5),
         out_specs=[VMEM] * len(out_shape),
         scratch_shapes=[
             pltpu.VMEM((slots + sum(sizes), nodes, width), BF16),
             pltpu.VMEM(current.shape, F32),
+            pltpu.VMEM(current.shape if sending else (1, 16, width), BF16),
             pltpu.VMEM((3, group * nodes, width), BF16),
             pltpu.VMEM((width, 2 * width), F32),
             pltpu.VMEM((width, width), F32),
+            pltpu.SemaphoreType.DMA((len(chunk_bounds(slots, group)),)),
         ],
-        compiler_params=params(28),
+        compiler_params=params(LIMIT1 if sending else 28),
         name="product",
-    )(columns, sends, count, degree, current, operand, blocks, *halos, degree if sending else other)
-
-
-def last(grams, image, denominator):
+    )(columns, sends, count, core, degree, current, blocks, *halos, *([] if sending else [other]))
+
+
+def last(core, mine, yours, image, denominator):
     slots, nodes, width = image.shape
     return pl.pallas_call(
         functools.partial(last_kernel, denominator),
         out_shape=[spread(image.shape, F32), spread((width, width), F32)],
-        in_specs=[VMEM, VMEM],
+        in_specs=[SMEM, VMEM, VMEM, VMEM],
         out_specs=[ANY, VMEM],
         scratch_shapes=[
             pltpu.VMEM((width, 2 * width), F32),
@@ -337,7 +349,7 @@
         ],
         compiler_params=params(16),
         name="last",
-    )(grams, image)
+    )(core, mine, yours, image)
 
 
 def shift(shard, axis, by, wrap):
@@ -352,28 +364,59 @@
             shift(to_right, "dom", 1, False), shift(to_left, "dom", -1, False))
 
 
-def collected(value, axis):
-    size = lax.axis_size(axis)
-    return lax.all_to_all(jnp.broadcast_to(value, (size,) + value.shape), axis, 0, 0, tiled=True)
-
-
-def summed(grams):
-    pieces = grams.reshape(lax.axis_size("dom"), -1, grams.shape[1])
-    mine = lax.all_to_all(pieces, "dom", 0, 0, tiled=True).sum(0)
-    mine = collected(mine, "group").sum(0)
-    return collected(mine, "dom").reshape(grams.shape)
+def place():
+    groups, parts = lax.axis_size("group"), lax.axis_size("dom")
+    y = min(groups, 4)
+    return groups // y, y, parts // 2, 2
+
+
+def neighbours(value, dim, by):
+    extents = place()
+    size = math.prod(extents)
+    stride = math.prod(extents[dim + 1:])
+    route = []
+    for i in range(size):
+        at = i // stride % extents[dim]
+        route.append((i, i + ((at + by) % extents[dim] - at) * stride))
+    return lax.ppermute(value, AXES, route)
+
+
+def sum_ring(value, dim):
+    extent = place()[dim]
+    order = sorted(range(1, extent), key=lambda k: min(k, extent - k))
+    for piece in [neighbours(value, dim, k) for k in order]:
+        value = value + piece
+    return value
+
+
+def sum_far(value):
+    extents = place()
+    depth, stride = extents[0], math.prod(extents[1:])
+    if depth == 1:
+        return value
+    groups = [[z * stride + i for z in range(depth)] for i in range(stride)]
+    copies = jnp.broadcast_to(value, (depth,) + value.shape)
+    return lax.all_to_all(copies, AXES, 0, 0, axis_index_groups=groups, tiled=True).sum(0)
+
+
+def summed(mine, yours):
+    value = mine + neighbours(yours, 3, 1)
+    value = sum_ring(value, 2)
+    value = sum_ring(value, 1)
+    value = sum_far(value)
+    return value, neighbours(value, 3, 1)
 
 
 def body(blocks, columns, sends, active_row_count, degree, start):
     slots, _, nodes, _ = blocks.shape
     denominator = lax.axis_size("group") * lax.axis_size("dom") * slots * nodes
     sizes = (slots // 2, slots // 2, slots // 4, slots // 4)
-    table = (columns.T, sends, active_row_count, degree)
-    token, operand, *sent = prep(sends, degree, start, sizes)
-    blocks = load(blocks, token)
-    image, first_gram, operand, *sent = product(*table, start, operand, blocks, exchange(sent), None)
-    image, grams = product(*table, image, operand, blocks, exchange(sent), first_gram)
-    return last(summed(grams), image, denominator)
+    core = lax.rem(lax.axis_index("dom"), 2).reshape(1)
+    table = (columns.T, sends, active_row_count, core, degree)
+    sent = prep(sends, degree, start, sizes)
+    image, first_gram, blocks, *sent = product(*table, start, blocks, exchange(sent), None)
+    image, mine, yours = product(*table, image, blocks, exchange(sent), first_gram)
+    return last(core, *summed(mine, yours), image, denominator)
 
 
 def solution(mesh):

time: 105 us -> 103 us (0.981); the launches traced: 106 us -> 102 us
  blocking collectives: 43.5 us -> 17.5 us
  starting transfers between devices: 26 us -> 41.2 us
  waiting for transfers between devices: 5.04 us -> 17.2 us
  Pallas kernels: 28.6 us -> 24.7 us
  local copies, waits for them, and re-layouts: 1.13 us -> 0.04 us
    all_to_all x3 -> x1, blocking collectives: 43.5 us -> 17.5 us  [sum_far(): lax.all_to_all(copies, AXES, 0, 0, axis_index_groups=groups, tiled=True)]
    ppermute x0 -> x8, starting transfers between devices: none -> 15.5 us  [neighbours(): return lax.ppermute(value, AXES, route)]
    ppermute x0 -> x8, waiting for transfers between devices: none -> 8.02 us  [neighbours(): return lax.ppermute(value, AXES, route)]
    ppermute x8, waiting for transfers between devices: 5.04 us -> 9.2 us  [shift(): return lax.ppermute(shard, axis, route)]
    pallas_call x2 -> x1, Pallas kernels: 6.77 us -> 2.8 us  [prep(): pl.pallas_call(prep_kernel, out_shape=[spread((n, nodes, width), BF16) fo...]
    unnamed x12 -> x8, local copies, waits for them, and re-layouts: 1.09 us -> 0.02 us
  transfers between devices with their start and end apart: 8 -> 16, of which waited for: 3 -> 10; matrix products, arithmetic and copies ran while one was open for 0% -> 0% of each run, Pallas kernels for 4% -> 0%
where the time goes in v4:
time: 103 us; the launch traced here: 102 us
  starting transfers between devices  41.2 us (40%)
  Pallas kernels  24.7 us (24%)
  blocking collectives  17.5 us (17%)
  waiting for transfers between devices  17.2 us (17%)
  between operations  1.62 us (2%)
    ppermute x8, starting transfers between devices, shift(): return lax.ppermute(shard, axis, route)  25.7 us
    all_to_all x1, blocking collectives, sum_far(): lax.all_to_all(copies, AXES, 0, 0, axis_index_groups=groups, tiled=True)  17.5 us
    ppermute x8, starting transfers between devices, neighbours(): return lax.ppermute(value, AXES, route)  15.5 us
    pallas_call x1, Pallas kernels, last(): pl.pallas_call(functools.partial(last_kernel, denominator), out_shape=[sp...  12.8 us
    ppermute x8, waiting for transfers between devices, shift(): return lax.ppermute(shard, axis, route)  9.2 us
    pallas_call x2, Pallas kernels, product(): pl.pallas_call(functools.partial(product_kernel, sending), out_shape=out_...  9.09 us
    ppermute x8, waiting for transfers between devices, neighbours(): return lax.ppermute(value, AXES, route)  8.02 us
    pallas_call x1, Pallas kernels, prep(): pl.pallas_call(prep_kernel, out_shape=[spread((n, nodes, width), BF16) fo...  2.8 us
  transfers between devices with their start and end apart: 16, of which 10 were waited for; matrix products, arithmetic and copies ran while one was open for 0% of the time, Pallas kernels for 0%

profile of v4, /device:TPU:1, one launch (start us, length us, event | category | flops | bytes accessed | tf_op | source)
XLA Modules:
  0.0 102.3 jit_solution(4304482395328800899)
XLA Ops:
  0.7 2.8 %prep.1 = (bf16[13,128,128]{2,1,0:T(8,128)(2,1)}, bf16[13,128,128]{2,1,0:T(8,128)(2,1)}, bf16[6,128,128]{2,1,0:T(8,128)(2,1)}, bf16[6,128,128]{2,1,0:T(8,128)(2,1)}) custom-call(s32[38]{0:T(128)} %sends_ref.3, f32[26,128]{1,0:T(8,128)} %degree_ref.3, f32[26,128,128]{2,1,0:T(8,128)} %current_ref.1), custom_call_target="tpu_custom_call" | custom-call | tf_op jit(solution)/shard_map/prep/pallas_call | solution.py:289
  3.5 2.2 %collective-permute-start = (bf16[13,128,128]{2,1,0:T(8,128)(2,1)}, bf16[13,128,128]{2,1,0:T(8,128)(2,1)S(1)}, u32[]{:S(2)}, u32[]{:S(2)}) collective-permute-start(bf16[13,128,128]{2,1,0:T(8,128)(2,1)} %get-tuple-element.16), channel_id=1, source_target_pairs={{0,8},{8,16},{16,24},{24,32},{32,40},{40,48},{48,56},{56,64},{64,7... | collective-permute-start | bytes 1277960 | tf_op jit(solution)/shard_map/ppermute | solution.py:358
  5.7 6.8 %collective-permute-start.1 = (bf16[13,128,128]{2,1,0:T(8,128)(2,1)}, bf16[13,128,128]{2,1,0:T(8,128)(2,1)S(1)}, u32[]{:S(2)}, u32[]{:S(2)}) collective-permute-start(bf16[13,128,128]{2,1,0:T(8,128)(2,1)} %get-tuple-element.17), channel_id=1, source_target_pairs={{0,248},{8,0},{16,8},{24,16},{32,24},{40,32},{48,40},{56,48},{64,5... | collective-permute-start | bytes 1277960 | tf_op jit(solution)/shard_map/ppermute | solution.py:358
  12.5 3.9 %collective-permute-start.2 = (bf16[6,128,128]{2,1,0:T(8,128)(2,1)}, bf16[6,128,128]{2,1,0:T(8,128)(2,1)S(1)}, u32[]{:S(2)}, u32[]{:S(2)}) collective-permute-start(bf16[6,128,128]{2,1,0:T(8,128)(2,1)} %get-tuple-element.18), channel_id=1, source_target_pairs={{0,1},{1,2},{2,3},{3,4},{4,5},{5,6},{6,7},{8,9},{9,10},{10,11},{11... | collective-permute-start | bytes 589832 | tf_op jit(solution)/shard_map/ppermute | solution.py:358
  16.5 1.9 %collective-permute-start.3 = (bf16[6,128,128]{2,1,0:T(8,128)(2,1)}, bf16[6,128,128]{2,1,0:T(8,128)(2,1)S(1)}, u32[]{:S(2)}, u32[]{:S(2)}) collective-permute-start(bf16[6,128,128]{2,1,0:T(8,128)(2,1)} %get-tuple-element.19), channel_id=1, source_target_pairs={{1,0},{2,1},{3,2},{4,3},{5,4},{6,5},{7,6},{9,8},{10,9},{11,10},{12... | collective-permute-start | bytes 589832 | tf_op jit(solution)/shard_map/ppermute | solution.py:358
  19.0 0.3 collective-permute-done.2.halo2
  19.4 4.3 %collective-permute-done.3.halo3 = bf16[6,128,128]{2,1,0:T(8,128)(2,1)S(1)} collective-permute-done((bf16[6,128,128]{2,1,0:T(8,128)(2,1)}, bf16[6,128,128]{2,1,0:T(8,128)(2,1)S(1)}, u32[]{:S(2)}, u32[]{:S(2)}) %collective-permute-start.3) | collective-permute-done | bytes 196640 | tf_op jit(solution)/shard_map/ppermute | solution.py:358
  23.7 0.0 collective-permute-done.halo0
  23.7 5.0 %product.2 = (f32[26,128,128]{2,1,0:T(8,128)S(1)}, f32[96,128]{1,0:T(8,128)S(1)}, bf16[26,11,128,128]{3,2,1,0:T(8,128)(2,1)S(1)}, bf16[13,128,128]{2,1,0:T(8,128...) custom-call(s32[11,26]{1,0:T(8,128)S(1)} %bitcast.2, ...), custom_call_target="tpu_custom_call" | custom-call | tf_op jit(solution)/shard_map/product/pallas_call | solution.py:318
  28.7 0.1 collective-permute-start.4
  28.8 6.4 %collective-permute-start.5 = (bf16[13,128,128]{2,1,0:T(8,128)(2,1)S(1)}, bf16[13,128,128]{2,1,0:T(8,128)(2,1)S(1)}, u32[]{:S(2)}, u32[]{:S(2)}) collective-permute-start(bf16[13,128,128]{2,1,0:T(8,128)(2,1)S(1)} %get-tuple-element.23), channel_id=1, source_target_pairs={{0,248},{8,0},{16,8},{24,16},{32,24},{40,32},{48,40},{56,48},{64,5... | collective-permute-start | bytes 1277960 | tf_op jit(solution)/shard_map/ppermute | solution.py:358
  35.2 1.9 %collective-permute-start.6 = (bf16[6,128,128]{2,1,0:T(8,128)(2,1)S(1)}, bf16[6,128,128]{2,1,0:T(8,128)(2,1)S(1)}, u32[]{:S(2)}, u32[]{:S(2)}) collective-permute-start(bf16[6,128,128]{2,1,0:T(8,128)(2,1)S(1)} %get-tuple-element.24), channel_id=1, source_target_pairs={{0,1},{1,2},{2,3},{3,4},{4,5},{5,6},{6,7},{8,9},{9,10},{10,11},{11... | collective-permute-start | bytes 589832 | tf_op jit(solution)/shard_map/ppermute | solution.py:358
  37.1 2.4 %collective-permute-start.7 = (bf16[6,128,128]{2,1,0:T(8,128)(2,1)S(1)}, bf16[6,128,128]{2,1,0:T(8,128)(2,1)S(1)}, u32[]{:S(2)}, u32[]{:S(2)}) collective-permute-start(bf16[6,128,128]{2,1,0:T(8,128)(2,1)S(1)} %get-tuple-element.25), channel_id=1, source_target_pairs={{1,0},{2,1},{3,2},{4,3},{5,4},{6,5},{7,6},{9,8},{10,9},{11,10},{12... | collective-permute-start | bytes 589832 | tf_op jit(solution)/shard_map/ppermute | solution.py:358
  39.5 0.2 collective-permute-done.6.halo2
  39.7 4.4 %collective-permute-done.7.halo3 = bf16[6,128,128]{2,1,0:T(8,128)(2,1)S(1)} collective-permute-done((bf16[6,128,128]{2,1,0:T(8,128)(2,1)S(1)}, bf16[6,128,128]{2,1,0:T(8,128)(2,1)S(1)}, u32[]{:S(2)}, u32[]{:S(2)}) %collective-permute-start.7) | collective-permute-done | bytes 196640 | tf_op jit(solution)/shard_map/ppermute | solution.py:358
  44.1 4.1 %product.3 = (f32[26,128,128]{2,1,0:T(8,128)S(1)}, f32[96,128]{1,0:T(8,128)S(1)}, f32[96,128]{1,0:T(8,128)S(1)}) custom-call(s32[11,26]{1,0:T(8,128)S(1)} %bitcast.3, s32[38]{0:T(128)S(1)} %copy-done.3, s32[1]{0:T(128)S(6)} %copy.8.count_ref, s32[1]{0:T(128)} %bitcast.core_ref, f32[26,128]{1,0:T(8,128)S(1)} %copy-done.1, ...), custom_call_target="tpu_custom_call" | custom-call | tf_op jit(solution)/shard_map/product/pallas_call | solution.py:318
  48.2 0.1 collective-permute-start.8
  48.3 1.2 %collective-permute-done.8 = f32[96,128]{1,0:T(8,128)S(1)} collective-permute-done((f32[96,128]{1,0:T(8,128)S(1)}, f32[96,128]{1,0:T(8,128)S(1)}, u32[]{:S(2)}, u32[]{:S(2)}) %collective-permute-start.8) | collective-permute-done | bytes 49184 | tf_op jit(solution)/shard_map/ppermute | solution.py:381
  49.5 7.6 %collective-permute-start.11 = (f32[96,128]{1,0:T(8,128)S(1)}, f32[96,128]{1,0:T(8,128)S(1)}, u32[]{:S(2)}, u32[]{:S(2)}) collective-permute-start(f32[96,128]{1,0:T(8,128)S(1)} %add.21), channel_id=1, source_target_pairs={{0,4},{1,5},{2,6},{3,7},{4,0},{5,1},{6,2},{7,3},{8,12},{9,13},{10,... | collective-permute-start | bytes 147464 | tf_op jit(solution)/shard_map/ppermute | solution.py:381
  57.2 1.5 %collective-permute-start.9 = (f32[96,128]{1,0:T(8,128)S(1)}, f32[96,128]{1,0:T(8,128)S(1)}, u32[]{:S(2)}, u32[]{:S(2)}) collective-permute-start(f32[96,128]{1,0:T(8,128)S(1)} %add.21), channel_id=1, source_target_pairs={{0,2},{1,3},{2,4},{3,5},{4,6},{5,7},{6,0},{7,1},{8,10},{9,11},{10,... | collective-permute-start | bytes 147464 | tf_op jit(solution)/shard_map/ppermute | solution.py:381
  58.6 0.0 collective-permute-done.11
  58.6 1.5 %collective-permute-done.10 = f32[96,128]{1,0:T(8,128)S(1)} collective-permute-done((f32[96,128]{1,0:T(8,128)S(1)}, f32[96,128]{1,0:T(8,128)S(1)}, u32[]{:S(2)}, u32[]{:S(2)}) %collective-permute-start.10) | collective-permute-done | bytes 49184 | tf_op jit(solution)/shard_map/ppermute | solution.py:381
  60.1 1.2 %collective-permute-done.9 = f32[96,128]{1,0:T(8,128)S(1)} collective-permute-done((f32[96,128]{1,0:T(8,128)S(1)}, f32[96,128]{1,0:T(8,128)S(1)}, u32[]{:S(2)}, u32[]{:S(2)}) %collective-permute-start.9) | collective-permute-done | bytes 49184 | tf_op jit(solution)/shard_map/ppermute | solution.py:381
  61.3 0.1 collective-permute-start.14
  61.4 0.3 collective-permute-start.13
  61.7 1.5 %collective-permute-start.12 = (f32[96,128]{1,0:T(8,128)S(1)}, f32[96,128]{1,0:T(8,128)S(1)}, u32[]{:S(2)}, u32[]{:S(2)}) collective-permute-start(f32[96,128]{1,0:T(8,128)S(1)} %add_add_fusion.1), channel_id=1, source_target_pairs={{0,8},{1,9},{2,10},{3,11},{4,12},{5,13},{6,14},{7,15},{8,16},{9,17... | collective-permute-start | bytes 147464 | tf_op jit(solution)/shard_map/ppermute | solution.py:381
  63.2 2.7 %collective-permute-done.14 = f32[96,128]{1,0:T(8,128)S(1)} collective-permute-done((f32[96,128]{1,0:T(8,128)S(1)}, f32[96,128]{1,0:T(8,128)S(1)}, u32[]{:S(2)}, u32[]{:S(2)}) %collective-permute-start.14) | collective-permute-done | bytes 49184 | tf_op jit(solution)/shard_map/ppermute | solution.py:381
  65.9 0.5 collective-permute-done.12
  66.4 17.5 %all_to_all.5 = f32[8,96,128]{2,1,0:T(8,128)S(1)} all-to-all(f32[8,96,128]{2,1,0:T(8,128)S(1)} %broadcast_in_dim.3), channel_id=1, replica_groups={{0,32,64,96,128,160,192,224},{1,33,65,97,129,161,193,225},{2,34,66,98,1..., dimensions={0} | all-to-all | bytes 786432 | tf_op jit(solution)/shard_map/all_to_all | solution.py:399
  83.9 4.5 %collective-permute-start.15 = (f32[96,128]{1,0:T(8,128)S(1)}, f32[96,128]{1,0:T(8,128)S(1)}, u32[]{:S(2)}, u32[]{:S(2)}) collective-permute-start(f32[96,128]{1,0:T(8,128)S(1)} %reduce_sum.9.mine_ref), channel_id=1, source_target_pairs={{0,1},{1,0},{2,3},{3,2},{4,5},{5,4},{6,7},{7,6},{8,9},{9,8},{10,11... | collective-permute-start | bytes 147464 | tf_op jit(solution)/shard_map/ppermute | solution.py:381
  88.5 0.9 collective-permute-done.15.yours_ref
  89.3 12.8 %last.1 = (f32[26,128,128]{2,1,0:T(8,128)}, f32[128,128]{1,0:T(8,128)}) custom-call(s32[1]{0:T(128)} %bitcast.core_ref, f32[96,128]{1,0:T(8,128)S(1)} %reduce_sum.9.mine_ref, f32[96,128]{1,0:T(8,128)S(1)} %collective-permute-done.15.yours_ref, f32[26,128,128]{2,1,0:T(8,128)S(1)} %get-tuple-element.29.image_ref), custom_call_target="tpu_custom_call" | custom-call | tf_op jit(solution)/shard_map/last/pallas_call | solution.py:339
  (18 shorter events, 0.1 us)
Async XLA Ops:
  0.6 23.0 %copy-start.1 = (f32[26,128]{1,0:T(8,128)S(1)}, f32[26,128]{1,0:T(8,128)}, u32[]{:S(2)}) copy-start(f32[26,128]{1,0:T(8,128)} %degree_ref.3) | copy-start | bytes 39940
  0.6 23.0 %copy-start.3 = (s32[38]{0:T(128)S(1)}, s32[38]{0:T(128)}, u32[]{:S(2)}) copy-start(s32[38]{0:T(128)} %sends_ref.3) | copy-start | bytes 460
  0.7 23.0 %copy-start = (f32[26,128,128]{2,1,0:T(8,128)S(1)}, f32[26,128,128]{2,1,0:T(8,128)}, u32[]{:S(2)}) copy-start(f32[26,128,128]{2,1,0:T(8,128)} %current_ref.1) | copy-start | bytes 5111812
  0.7 23.0 %copy-start.2 = (s32[26,11]{0,1:T(8,128)S(1)}, s32[26,11]{0,1:T(8,128)}, u32[]{:S(2)}) copy-start(s32[26,11]{0,1:T(8,128)} %param.7) | copy-start | bytes 3436
  3.5 20.2 %collective-permute-start = (bf16[13,128,128]{2,1,0:T(8,128)(2,1)}, bf16[13,128,128]{2,1,0:T(8,128)(2,1)S(1)}, u32[]{:S(2)}, u32[]{:S(2)}) collective-permute-start(bf16[13,128,128]{2,1,0:T(8,128)(2,1)} %get-tuple-element.16), channel_id=1, source_target_pairs={{0,8},{8,16},{16,24},{24,32},{32,40},{40,48},{48,56},{56,64},{64,7... | collective-permute-start | bytes 1277960 | tf_op jit(solution)/shard_map/ppermute | solution.py:358
  5.7 18.0 %collective-permute-start.1 = (bf16[13,128,128]{2,1,0:T(8,128)(2,1)}, bf16[13,128,128]{2,1,0:T(8,128)(2,1)S(1)}, u32[]{:S(2)}, u32[]{:S(2)}) collective-permute-start(bf16[13,128,128]{2,1,0:T(8,128)(2,1)} %get-tuple-element.17), channel_id=1, source_target_pairs={{0,248},{8,0},{16,8},{24,16},{32,24},{40,32},{48,40},{56,48},{64,5... | collective-permute-start | bytes 1277960 | tf_op jit(solution)/shard_map/ppermute | solution.py:358
  12.5 6.9 %collective-permute-start.2 = (bf16[6,128,128]{2,1,0:T(8,128)(2,1)}, bf16[6,128,128]{2,1,0:T(8,128)(2,1)S(1)}, u32[]{:S(2)}, u32[]{:S(2)}) collective-permute-start(bf16[6,128,128]{2,1,0:T(8,128)(2,1)} %get-tuple-element.18), channel_id=1, source_target_pairs={{0,1},{1,2},{2,3},{3,4},{4,5},{5,6},{6,7},{8,9},{9,10},{10,11},{11... | collective-permute-start | bytes 589832 | tf_op jit(solution)/shard_map/ppermute | solution.py:358
  16.5 7.2 %collective-permute-start.3 = (bf16[6,128,128]{2,1,0:T(8,128)(2,1)}, bf16[6,128,128]{2,1,0:T(8,128)(2,1)S(1)}, u32[]{:S(2)}, u32[]{:S(2)}) collective-permute-start(bf16[6,128,128]{2,1,0:T(8,128)(2,1)} %get-tuple-element.19), channel_id=1, source_target_pairs={{1,0},{2,1},{3,2},{4,3},{5,4},{6,5},{7,6},{9,8},{10,9},{11,10},{12... | collective-permute-start | bytes 589832 | tf_op jit(solution)/shard_map/ppermute | solution.py:358
  28.7 15.4 %collective-permute-start.4 = (bf16[13,128,128]{2,1,0:T(8,128)(2,1)S(1)}, bf16[13,128,128]{2,1,0:T(8,128)(2,1)S(1)}, u32[]{:S(2)}, u32[]{:S(2)}) collective-permute-start(bf16[13,128,128]{2,1,0:T(8,128)(2,1)S(1)} %get-tuple-element.22), channel_id=1, source_target_pairs={{0,8},{8,16},{16,24},{24,32},{32,40},{40,48},{48,56},{56,64},{64,7... | collective-permute-start | bytes 1277960 | tf_op jit(solution)/shard_map/ppermute | solution.py:358
  28.8 15.3 %collective-permute-start.5 = (bf16[13,128,128]{2,1,0:T(8,128)(2,1)S(1)}, bf16[13,128,128]{2,1,0:T(8,128)(2,1)S(1)}, u32[]{:S(2)}, u32[]{:S(2)}) collective-permute-start(bf16[13,128,128]{2,1,0:T(8,128)(2,1)S(1)} %get-tuple-element.23), channel_id=1, source_target_pairs={{0,248},{8,0},{16,8},{24,16},{32,24},{40,32},{48,40},{56,48},{64,5... | collective-permute-start | bytes 1277960 | tf_op jit(solution)/shard_map/ppermute | solution.py:358
  35.2 4.5 %collective-permute-start.6 = (bf16[6,128,128]{2,1,0:T(8,128)(2,1)S(1)}, bf16[6,128,128]{2,1,0:T(8,128)(2,1)S(1)}, u32[]{:S(2)}, u32[]{:S(2)}) collective-permute-start(bf16[6,128,128]{2,1,0:T(8,128)(2,1)S(1)} %get-tuple-element.24), channel_id=1, source_target_pairs={{0,1},{1,2},{2,3},{3,4},{4,5},{5,6},{6,7},{8,9},{9,10},{10,11},{11... | collective-permute-start | bytes 589832 | tf_op jit(solution)/shard_map/ppermute | solution.py:358
  37.1 7.0 %collective-permute-start.7 = (bf16[6,128,128]{2,1,0:T(8,128)(2,1)S(1)}, bf16[6,128,128]{2,1,0:T(8,128)(2,1)S(1)}, u32[]{:S(2)}, u32[]{:S(2)}) collective-permute-start(bf16[6,128,128]{2,1,0:T(8,128)(2,1)S(1)} %get-tuple-element.25), channel_id=1, source_target_pairs={{1,0},{2,1},{3,2},{4,3},{5,4},{6,5},{7,6},{9,8},{10,9},{11,10},{12... | collective-permute-start | bytes 589832 | tf_op jit(solution)/shard_map/ppermute | solution.py:358
  48.2 1.3 %collective-permute-start.8 = (f32[96,128]{1,0:T(8,128)S(1)}, f32[96,128]{1,0:T(8,128)S(1)}, u32[]{:S(2)}, u32[]{:S(2)}) collective-permute-start(f32[96,128]{1,0:T(8,128)S(1)} %get-tuple-element.28), channel_id=1, source_target_pairs={{0,1},{1,0},{2,3},{3,2},{4,5},{5,4},{6,7},{7,6},{8,9},{9,8},{10,11... | collective-permute-start | bytes 147464 | tf_op jit(solution)/shard_map/ppermute | solution.py:381
  49.5 9.1 %collective-permute-start.11 = (f32[96,128]{1,0:T(8,128)S(1)}, f32[96,128]{1,0:T(8,128)S(1)}, u32[]{:S(2)}, u32[]{:S(2)}) collective-permute-start(f32[96,128]{1,0:T(8,128)S(1)} %add.21), channel_id=1, source_target_pairs={{0,4},{1,5},{2,6},{3,7},{4,0},{5,1},{6,2},{7,3},{8,12},{9,13},{10,... | collective-permute-start | bytes 147464 | tf_op jit(solution)/shard_map/ppermute | solution.py:381
  57.2 2.9 %collective-permute-start.10 = (f32[96,128]{1,0:T(8,128)S(1)}, f32[96,128]{1,0:T(8,128)S(1)}, u32[]{:S(2)}, u32[]{:S(2)}) collective-permute-start(f32[96,128]{1,0:T(8,128)S(1)} %add.21), channel_id=1, source_target_pairs={{0,6},{1,7},{2,0},{3,1},{4,2},{5,3},{6,4},{7,5},{8,14},{9,15},{10,... | collective-permute-start | bytes 147464 | tf_op jit(solution)/shard_map/ppermute | solution.py:381
  57.2 4.2 %collective-permute-start.9 = (f32[96,128]{1,0:T(8,128)S(1)}, f32[96,128]{1,0:T(8,128)S(1)}, u32[]{:S(2)}, u32[]{:S(2)}) collective-permute-start(f32[96,128]{1,0:T(8,128)S(1)} %add.21), channel_id=1, source_target_pairs={{0,2},{1,3},{2,4},{3,5},{4,6},{5,7},{6,0},{7,1},{8,10},{9,11},{10,... | collective-permute-start | bytes 147464 | tf_op jit(solution)/shard_map/ppermute | solution.py:381
  61.3 4.6 %collective-permute-start.14 = (f32[96,128]{1,0:T(8,128)S(1)}, f32[96,128]{1,0:T(8,128)S(1)}, u32[]{:S(2)}, u32[]{:S(2)}) collective-permute-start(f32[96,128]{1,0:T(8,128)S(1)} %add_add_fusion.1), channel_id=1, source_target_pairs={{0,16},{1,17},{2,18},{3,19},{4,20},{5,21},{6,22},{7,23},{8,24},{9,... | collective-permute-start | bytes 147464 | tf_op jit(solution)/shard_map/ppermute | solution.py:381
  61.4 4.5 %collective-permute-start.13 = (f32[96,128]{1,0:T(8,128)S(1)}, f32[96,128]{1,0:T(8,128)S(1)}, u32[]{:S(2)}, u32[]{:S(2)}) collective-permute-start(f32[96,128]{1,0:T(8,128)S(1)} %add_add_fusion.1), channel_id=1, source_target_pairs={{0,24},{1,25},{2,26},{3,27},{4,28},{5,29},{6,30},{7,31},{8,0},{9,1... | collective-permute-start | bytes 147464 | tf_op jit(solution)/shard_map/ppermute | solution.py:381
  61.7 4.7 %collective-permute-start.12 = (f32[96,128]{1,0:T(8,128)S(1)}, f32[96,128]{1,0:T(8,128)S(1)}, u32[]{:S(2)}, u32[]{:S(2)}) collective-permute-start(f32[96,128]{1,0:T(8,128)S(1)} %add_add_fusion.1), channel_id=1, source_target_pairs={{0,8},{1,9},{2,10},{3,11},{4,12},{5,13},{6,14},{7,15},{8,16},{9,17... | collective-permute-start | bytes 147464 | tf_op jit(solution)/shard_map/ppermute | solution.py:381
  83.9 5.4 %collective-permute-start.15 = (f32[96,128]{1,0:T(8,128)S(1)}, f32[96,128]{1,0:T(8,128)S(1)}, u32[]{:S(2)}, u32[]{:S(2)}) collective-permute-start(f32[96,128]{1,0:T(8,128)S(1)} %reduce_sum.9.mine_ref), channel_id=1, source_target_pairs={{0,1},{1,0},{2,3},{3,2},{4,5},{5,4},{6,7},{7,6},{8,9},{9,8},{10,11... | collective-permute-start | bytes 147464 | tf_op jit(solution)/shard_map/ppermute | solution.py:381

commit v5 on v4

--- a/solution.py
+++ b/solution.py
@@ -9,8 +9,7 @@
 
 AXES = ("group", "dom")
 F32, BF16 = jnp.float32, jnp.bfloat16
-PANEL = 16
-LIMIT1 = 36
+PANEL, GROUP = 16, 2
 ANY = pl.BlockSpec(memory_space=pl.ANY)
 SMEM = pl.BlockSpec(memory_space=pltpu.SMEM)
 VMEM = pl.BlockSpec(memory_space=pltpu.VMEM)
@@ -101,40 +100,33 @@
     put_sends(out_refs, sends_ref, operand_ref)
 
 
-def chunk_bounds(slots, group):
-    steps = slots // group
-    return sorted({0, steps // 6, steps // 3, 2 * steps // 3, steps})
-
-
-def product_kernel(sending, columns_ref, sends_ref, count_ref, core_ref, degree_ref, current_ref,
-                   blocks_hbm, halo0, halo1, halo2, halo3, *refs):
-    ext_ref, scale_ref, next_ref, parts_ref, wide_ref, side_ref, sems = refs[-7:]
-    if sending:
-        image_ref, gram_ref, blocks_ref, *out_refs = refs[:-7]
-    else:
-        other_ref, image_ref, mine_ref, yours_ref = refs[:-7]
-        blocks_ref = blocks_hbm
-    slots, per_row = blocks_ref.shape[:2]
-    group = parts_ref.shape[1] // image_ref.shape[1]
-    count = count_ref[0]
-    bounds = chunk_bounds(slots, group)
-    copies = []
-    if sending:
-        for i, (low, high) in enumerate(zip(bounds, bounds[1:])):
-            chunk = pl.ds(low * group, (high - low) * group)
-            copies.append(pltpu.make_async_copy(blocks_hbm.at[chunk], blocks_ref.at[chunk], sems.at[i]))
-            copies[-1].start()
+def hold_kernel(blocks_hbm, degree_ref, blocks_ref, scale_ref, sem):
+    copy = pltpu.make_async_copy(blocks_hbm, blocks_ref, sem)
+    copy.start()
     for s, scale in enumerate(scale_blocks(degree_ref)):
         scale_ref[s] = scale
-        ext_ref[s] = (scale * current_ref[s]).astype(BF16)
+    copy.wait()
+
+
+def product_kernel(sending, columns_ref, sends_ref, count_ref, core_ref, scale_ref, current_ref,
+                   blocks_ref, halo0, halo1, halo2, halo3, *refs):
+    if sending:
+        image_ref, *out_refs, ext_ref, next_ref = refs
+    else:
+        other_ref, image_ref, mine_ref, yours_ref, ext_ref, parts_ref, wide_ref, side_ref = refs
+    slots, per_row = blocks_ref.shape[:2]
+    count = count_ref[0]
+    for s in range(slots):
+        ext_ref[s] = (scale_ref[s] * current_ref[s]).astype(BF16)
     base = slots
     for piece in (halo0, halo1, halo2, halo3):
         size = piece.shape[0]
         ext_ref[base:base + size] = piece[...]
         base += size
-    wide_ref[...] = jnp.zeros_like(wide_ref)
-    side_ref[...] = jnp.zeros_like(side_ref)
-    parts_ref[...] = jnp.zeros_like(parts_ref)
+    if not sending:
+        wide_ref[...] = jnp.zeros_like(wide_ref)
+        side_ref[...] = jnp.zeros_like(side_ref)
+        parts_ref[...] = jnp.zeros_like(parts_ref)
 
     def row(s):
         left = jnp.concatenate([blocks_ref[s, k] for k in range(per_row)], axis=1)
@@ -143,35 +135,45 @@
         return jnp.where(s < count, image, 0.0)
 
     def rows(step, carry):
-        add_gram([parts_ref[i] for i in range(3)], wide_ref, side_ref)
-        first = step * group
-        images = [row(first + i) for i in range(group)]
+        if not sending:
+            add_gram([parts_ref[i] for i in range(3)], wide_ref, side_ref)
+        first = step * GROUP
+        images = [row(first + i) for i in range(GROUP)]
         for i, image in enumerate(images):
             image_ref[first + i] = image
             if sending:
                 next_ref[first + i] = (scale_ref[first + i] * image).astype(BF16)
-        for i, part in enumerate(split3(jnp.concatenate(images, axis=0))):
-            parts_ref[i] = part
+        if not sending:
+            for i, part in enumerate(split3(jnp.concatenate(images, axis=0))):
+                parts_ref[i] = part
         return carry
-    steps = (count + group - 1) // group
-    for i, (low, high) in enumerate(zip(bounds, bounds[1:])):
-        if sending:
-            copies[i].wait()
-        lax.fori_loop(low, jnp.minimum(high, steps), rows, 0)
-    add_gram([parts_ref[i] for i in range(3)], wide_ref, side_ref)
+    steps = (count + GROUP - 1) // GROUP
+    lax.fori_loop(0, steps, rows, 0)
 
     def dead(s, carry):
         image_ref[s] = jnp.zeros(image_ref.shape[1:], F32)
         return carry
-    lax.fori_loop(steps * group, slots, dead, 0)
-    gram = pack_gram(finish_gram(wide_ref, side_ref))
+    lax.fori_loop(steps * GROUP, slots, dead, 0)
     if sending:
-        gram_ref[...] = gram
         put_sends(out_refs, sends_ref, next_ref)
     else:
+        add_gram([parts_ref[i] for i in range(3)], wide_ref, side_ref)
+        gram = pack_gram(finish_gram(wide_ref, side_ref))
         other, low_core = other_ref[...], core_ref[0] == 0
         mine_ref[...] = jnp.where(low_core, other, gram)
         yours_ref[...] = jnp.where(low_core, gram, other)
+
+
+def gram_kernel(count_ref, image_ref, gram_ref, wide_ref, side_ref):
+    wide_ref[...] = jnp.zeros_like(wide_ref)
+    side_ref[...] = jnp.zeros_like(side_ref)
+
+    def rows(step, carry):
+        images = [image_ref[step * GROUP + i] for i in range(GROUP)]
+        add_gram(split3(jnp.concatenate(images, axis=0)), wide_ref, side_ref)
+        return carry
+    lax.fori_loop(0, (count_ref[0] + GROUP - 1) // GROUP, rows, 0)
+    gram_ref[...] = pack_gram(finish_gram(wide_ref, side_ref))
 
 
 def gather_rows(rows, sublane):
@@ -248,17 +250,17 @@
     return both[:, :width] + both[:, width:]
 
 
-def last_kernel(denominator, core_ref, mine_ref, yours_ref, image_ref, basis_hbm, factor_ref,
-                work_ref, weights_ref, basis_ref, out_sems):
+def factor_kernel(denominator, gram_ref, work_ref):
+    start_factor(unpack_gram(gram_ref[...]), denominator, work_ref)
+
+
+def last_kernel(core_ref, mine_ref, yours_ref, image_ref, basis_hbm, factor_ref,
+                weights_ref, basis_ref, out_sems):
     slots, nodes, width = image_ref.shape
     low_core = core_ref[0] == 0
-    mine, yours = mine_ref[...], yours_ref[...]
-    start_factor(unpack_gram(jnp.where(low_core, mine, yours)), denominator, work_ref)
-    first = work_ref[:, width:]
-    turned = first.T
-    second = dot_full(dot_full(first, unpack_gram(jnp.where(low_core, yours, mine))), turned)
-    rows, columns = start_factor(second, denominator, work_ref)
-    wide_weights(dot_full(turned, work_ref[:, width:].T), weights_ref)
+    both = jnp.where(low_core, yours_ref[...], mine_ref[...])
+    first = jnp.where(low_core, mine_ref[:, width:], yours_ref[:, width:])
+    wide_weights(both[:, width:].T, weights_ref)
     half = slots // 2
 
     def out_copy(part):
@@ -271,7 +273,10 @@
     for part in range(2):
         lax.fori_loop(part * half, (part + 1) * half, apply, 0, unroll=half)
         out_copy(part).start()
-    factor_ref[...] = jnp.where(rows <= columns, work_ref[:, :width], 0.0).T
+    rows = lax.broadcasted_iota(jnp.int32, (width, width), 0)
+    columns = lax.broadcasted_iota(jnp.int32, (width, width), 1)
+    joint = jnp.where(rows <= columns, both[:, :width], 0.0).T
+    factor_ref[...] = jnp.where(rows >= columns, dot_full(first, joint), 0.0)
     for part in range(2):
         out_copy(part).wait()
 
@@ -303,46 +308,81 @@
     )(sends, degree, start)
 
 
-def product(columns, sends, count, core, degree, current, blocks, halos, other):
+def hold(blocks, degree, slots, nodes):
+    size = blocks.size * blocks.dtype.itemsize
+    return pl.pallas_call(
+        hold_kernel,
+        out_shape=[spread(blocks.shape, BF16), spread((slots, nodes, nodes), F32)],
+        in_specs=[ANY, VMEM],
+        out_specs=[VMEM, VMEM],
+        scratch_shapes=[pltpu.SemaphoreType.DMA(())],
+        compiler_params=params(36),
+        cost_estimate=pl.CostEstimate(flops=0, bytes_accessed=2 * size, transcendentals=0),
+        name="hold",
+    )(blocks, degree)
+
+
+def product(columns, sends, count, core, scale, current, blocks, halos, other):
     slots, nodes, width = current.shape
     sizes = [h.shape[0] for h in halos]
     sending = other is None
-    group = 2
     packed = spread((3 * width // 4, width), F32)
-    out_shape = [spread(current.shape, F32), packed]
+    scratch = [pltpu.VMEM((slots + sum(sizes), nodes, width), BF16)]
     if sending:
-        out_shape += [spread(blocks.shape, BF16)]
-        out_shape += [spread(h.shape, BF16) for h in halos]
+        out_shape = [spread(h.shape, BF16) for h in halos]
+        scratch += [pltpu.VMEM(current.shape, BF16)]
     else:
-        out_shape += [packed]
+        out_shape = [packed, packed]
+        scratch += [pltpu.VMEM((3, GROUP * nodes, width), BF16)] + gram_scratch(width)
     return pl.pallas_call(
         functools.partial(product_kernel, sending),
-        out_shape=out_shape,
-        in_specs=[SMEM] * 4 + [VMEM] * 2 + [ANY if sending else VMEM] + [VMEM] * (4 if sending else 5),
-        out_specs=[VMEM] * len(out_shape),
-        scratch_shapes=[
-            pltpu.VMEM((slots + sum(sizes), nodes, width), BF16),
-            pltpu.VMEM(current.shape, F32),
-            pltpu.VMEM(current.shape if sending else (1, 16, width), BF16),
-            pltpu.VMEM((3, group * nodes, width), BF16),
-            pltpu.VMEM((width, 2 * width), F32),
-            pltpu.VMEM((width, width), F32),
-            pltpu.SemaphoreType.DMA((len(chunk_bounds(slots, group)),)),
-        ],
-        compiler_params=params(LIMIT1 if sending else 28),
+        out_shape=[spread(current.shape, F32)] + out_shape,
+        in_specs=[SMEM] * 4 + [VMEM] * (7 if sending else 8),
+        out_specs=[VMEM] * (1 + len(out_shape)),
+        scratch_shapes=scratch,
+        compiler_params=params(28),
         name="product",
-    )(columns, sends, count, core, degree, current, blocks, *halos, *([] if sending else [other]))
-
-
-def last(core, mine, yours, image, denominator):
+    )(columns, sends, count, core, scale, current, blocks, *halos, *([] if sending else [other]))
+
+
+def gram_scratch(width):
+    return [pltpu.VMEM((width, 2 * width), F32), pltpu.VMEM((width, width), F32)]
+
+
+def gram(count, image):
+    width = image.shape[2]
+    return pl.pallas_call(
+        gram_kernel,
+        out_shape=spread((3 * width // 4, width), F32),
+        in_specs=[SMEM, VMEM],
+        out_specs=VMEM,
+        scratch_shapes=gram_scratch(width),
+        compiler_params=params(16),
+        cost_estimate=pl.CostEstimate(flops=2 * image.size * width, bytes_accessed=image.size * 4, transcendentals=0),
+        name="gram",
+    )(count, image)
+
+
+def factor(packed, denominator):
+    width = packed.shape[1]
+    return pl.pallas_call(
+        functools.partial(factor_kernel, denominator),
+        out_shape=spread((width, 2 * width), F32),
+        in_specs=[VMEM],
+        out_specs=VMEM,
+        compiler_params=params(16),
+        name="factor",
+    )(packed)
+
+
+def last(core, mine, yours, image):
     slots, nodes, width = image.shape
     return pl.pallas_call(
-        functools.partial(last_kernel, denominator),
+        last_kernel,
         out_shape=[spread(image.shape, F32), spread((width, width), F32)],
         in_specs=[SMEM, VMEM, VMEM, VMEM],
         out_specs=[ANY, VMEM],
         scratch_shapes=[
-            pltpu.VMEM((width, 2 * width), F32),
             pltpu.VMEM((2 * width, 2 * width), BF16),
             pltpu.VMEM(image.shape, F32),
             pltpu.SemaphoreType.DMA((2,)),
@@ -403,8 +443,7 @@
     value = mine + neighbours(yours, 3, 1)
     value = sum_ring(value, 2)
     value = sum_ring(value, 1)
-    value = sum_far(value)
-    return value, neighbours(value, 3, 1)
+    return sum_far(value)
 
 
 def body(blocks, columns, sends, active_row_count, degree, start):
@@ -412,11 +451,15 @@
     denominator = lax.axis_size("group") * lax.axis_size("dom") * slots * nodes
     sizes = (slots // 2, slots // 2, slots // 4, slots // 4)
     core = lax.rem(lax.axis_index("dom"), 2).reshape(1)
-    table = (columns.T, sends, active_row_count, core, degree)
-    sent = prep(sends, degree, start, sizes)
-    image, first_gram, blocks, *sent = product(*table, start, blocks, exchange(sent), None)
-    image, mine, yours = product(*table, image, blocks, exchange(sent), first_gram)
-    return last(core, *summed(mine, yours), image, denominator)
+    table = (columns.T, sends, active_row_count, core)
+    halo = exchange(prep(sends, degree, start, sizes))
+    held, scale = hold(blocks, degree, slots, nodes)
+    image, *sent = product(*table, scale, start, held, halo, None)
+    halo = exchange(sent)
+    first_gram = gram(active_row_count, image)
+    image, mine, yours = product(*table, scale, image, held, halo, first_gram)
+    work = factor(summed(mine, yours), denominator)
+    return tuple(last(core, work, neighbours(work, 3, 1), image))
 
 
 def solution(mesh):

time: 103 us -> 93.8 us (0.911)
  Pallas kernels: 24.7 us -> 20.9 us
  waiting for transfers between devices: 17.2 us -> 14.4 us
  blocking collectives: 17.5 us -> 15.5 us
    ppermute x8, waiting for transfers between devices: 9.2 us -> 4.65 us  [shift(): return lax.ppermute(shard, axis, route)]
    pallas_call x3 -> x6, Pallas kernels: 21.9 us -> 18.2 us  [the longest x2 5.79 us: product(): pl.pallas_call(functools.partial(product_kernel, sending), out_shape=[spr...]
    ppermute x8, starting transfers between devices: 25.7 us -> 28.4 us  [shift(): return lax.ppermute(shard, axis, route)]
    ppermute x8, starting transfers between devices: 15.5 us -> 13 us  [neighbours(): return lax.ppermute(value, AXES, route)]
    all_to_all x1, blocking collectives: 17.5 us -> 15.5 us  [sum_far(): lax.all_to_all(copies, AXES, 0, 0, axis_index_groups=groups, tiled=True)]
    ppermute x8, waiting for transfers between devices: 8.02 us -> 9.76 us  [neighbours(): return lax.ppermute(value, AXES, route)]
  transfers between devices with their start and end apart: 16 -> 16, of which waited for: 10 -> 8; matrix products, arithmetic and copies ran while one was open for 0% -> 0% of each run, Pallas kernels for 0% -> 5%
where the time goes in v5:
time: 93.8 us; the launch traced here: 94.1 us
  starting transfers between devices  41.4 us (44%)
  Pallas kernels  20.9 us (22%)
  blocking collectives  15.5 us (17%)
  waiting for transfers between devices  14.4 us (15%)
  between operations  1.63 us (2%)
    ppermute x8, starting transfers between devices, shift(): return lax.ppermute(shard, axis, route)  28.4 us
    all_to_all x1, blocking collectives, sum_far(): lax.all_to_all(copies, AXES, 0, 0, axis_index_groups=groups, tiled=True)  15.5 us
    ppermute x8, starting transfers between devices, neighbours(): return lax.ppermute(value, AXES, route)  13 us
    ppermute x8, waiting for transfers between devices, neighbours(): return lax.ppermute(value, AXES, route)  9.76 us
    pallas_call x2, Pallas kernels, product(): pl.pallas_call(functools.partial(product_kernel, sending), out_shape=[spr...  5.79 us
    pallas_call x1, Pallas kernels, factor(): pl.pallas_call(functools.partial(factor_kernel, denominator), out_shape=s...  5.09 us
    ppermute x8, waiting for transfers between devices, shift(): return lax.ppermute(shard, axis, route)  4.65 us
    pallas_call x1, Pallas kernels, hold(): pl.pallas_call(hold_kernel, out_shape=[spread(blocks.shape, BF16), spread...  3.79 us
  transfers between devices with their start and end apart: 16, of which 8 were waited for; matrix products, arithmetic and copies ran while one was open for 0% of the time, Pallas kernels for 5%

profile of v5, /device:TPU:1, one launch (start us, length us, event | category | flops | bytes accessed | tf_op | source)
XLA Modules:
  0.0 94.1 jit_solution(2064605433080945033)
XLA Ops:
  0.6 2.7 %prep.1 = (bf16[13,128,128]{2,1,0:T(8,128)(2,1)}, bf16[13,128,128]{2,1,0:T(8,128)(2,1)}, bf16[6,128,128]{2,1,0:T(8,128)(2,1)}, bf16[6,128,128]{2,1,0:T(8,128)(2,1)}) custom-call(s32[38]{0:T(128)} %sends_ref.3, f32[26,128]{1,0:T(8,128)} %degree_hbm.1, f32[26,128,128]{2,1,0:T(8,128)} %current_ref.1), custom_call_target="tpu_custom_call" | custom-call | tf_op jit(solution)/shard_map/prep/pallas_call | solution.py:294
  3.4 2.2 %collective-permute-start = (bf16[13,128,128]{2,1,0:T(8,128)(2,1)}, bf16[13,128,128]{2,1,0:T(8,128)(2,1)S(1)}, u32[]{:S(2)}, u32[]{:S(2)}) collective-permute-start(bf16[13,128,128]{2,1,0:T(8,128)(2,1)} %get-tuple-element.18), channel_id=1, source_target_pairs={{0,8},{8,16},{16,24},{24,32},{32,40},{40,48},{48,56},{56,64},{64,7... | collective-permute-start | bytes 1277960 | tf_op jit(solution)/shard_map/ppermute | solution.py:398
  5.6 6.8 %collective-permute-start.1 = (bf16[13,128,128]{2,1,0:T(8,128)(2,1)}, bf16[13,128,128]{2,1,0:T(8,128)(2,1)S(1)}, u32[]{:S(2)}, u32[]{:S(2)}) collective-permute-start(bf16[13,128,128]{2,1,0:T(8,128)(2,1)} %get-tuple-element.19), channel_id=1, source_target_pairs={{0,248},{8,0},{16,8},{24,16},{32,24},{40,32},{48,40},{56,48},{64,5... | collective-permute-start | bytes 1277960 | tf_op jit(solution)/shard_map/ppermute | solution.py:398
  12.4 3.9 %collective-permute-start.2 = (bf16[6,128,128]{2,1,0:T(8,128)(2,1)}, bf16[6,128,128]{2,1,0:T(8,128)(2,1)S(1)}, u32[]{:S(2)}, u32[]{:S(2)}) collective-permute-start(bf16[6,128,128]{2,1,0:T(8,128)(2,1)} %get-tuple-element.20), channel_id=1, source_target_pairs={{0,1},{1,2},{2,3},{3,4},{4,5},{5,6},{6,7},{8,9},{9,10},{10,11},{11... | collective-permute-start | bytes 589832 | tf_op jit(solution)/shard_map/ppermute | solution.py:398
  16.4 1.9 %collective-permute-start.3 = (bf16[6,128,128]{2,1,0:T(8,128)(2,1)}, bf16[6,128,128]{2,1,0:T(8,128)(2,1)S(1)}, u32[]{:S(2)}, u32[]{:S(2)}) collective-permute-start(bf16[6,128,128]{2,1,0:T(8,128)(2,1)} %get-tuple-element.21), channel_id=1, source_target_pairs={{1,0},{2,1},{3,2},{4,3},{5,4},{6,5},{7,6},{9,8},{10,9},{11,10},{12... | collective-permute-start | bytes 589832 | tf_op jit(solution)/shard_map/ppermute | solution.py:398
  19.0 0.0 copy-start.2
  19.0 3.8 %hold.1 = (bf16[26,11,128,128]{3,2,1,0:T(8,128)(2,1)S(1)}, f32[26,128,128]{2,1,0:T(8,128)S(1)}) custom-call(bf16[26,11,128,128]{3,2,1,0:T(8,128)(2,1)} %blocks_hbm.1, f32[26,128]{1,0:T(8,128)S(1)} %copy-done.1), custom_call_target="tpu_custom_call" | custom-call | bytes 18743296 | tf_op jit(solution)/shard_map/hold/pallas_call | solution.py:313
  22.8 0.8 collective-permute-done.3.halo3
  23.6 2.6 %product.2 = (f32[26,128,128]{2,1,0:T(8,128)S(1)}, bf16[13,128,128]{2,1,0:T(8,128)(2,1)S(1)}, bf16[13,128,128]{2,1,0:T(8,128)(2,1)S(1)}, bf16[6,128,128]{2,1,0:T(8,128)(2,1)S(1)}, bf16[6,128,128]{2,1,0:T(8,128)(2,1)S(1)}) custom-call(s32[11,26]{1,0:T(8,128)S(1)} %bitcast.2, s32[38]{0:T(128)S(1)} %copy-done.3, s32[1]{0:T(128)S(6)} %copy.8.count_ref, ...), custom_call_target="tpu_custom_call" | custom-call | tf_op jit(solution)/shard_map/product/pallas_call | solution.py:337
  26.2 0.1 collective-permute-start.4
  26.3 4.8 %collective-permute-start.5 = (bf16[13,128,128]{2,1,0:T(8,128)(2,1)S(1)}, bf16[13,128,128]{2,1,0:T(8,128)(2,1)S(1)}, u32[]{:S(2)}, u32[]{:S(2)}) collective-permute-start(bf16[13,128,128]{2,1,0:T(8,128)(2,1)S(1)} %get-tuple-element.24), channel_id=1, source_target_pairs={{0,248},{8,0},{16,8},{24,16},{32,24},{40,32},{48,40},{56,48},{64,5... | collective-permute-start | bytes 1277960 | tf_op jit(solution)/shard_map/ppermute | solution.py:398
  31.1 6.7 %collective-permute-start.6 = (bf16[6,128,128]{2,1,0:T(8,128)(2,1)S(1)}, bf16[6,128,128]{2,1,0:T(8,128)(2,1)S(1)}, u32[]{:S(2)}, u32[]{:S(2)}) collective-permute-start(bf16[6,128,128]{2,1,0:T(8,128)(2,1)S(1)} %get-tuple-element.25), channel_id=1, source_target_pairs={{0,1},{1,2},{2,3},{3,4},{4,5},{5,6},{6,7},{8,9},{9,10},{10,11},{11... | collective-permute-start | bytes 589832 | tf_op jit(solution)/shard_map/ppermute | solution.py:398
  37.8 1.9 %collective-permute-start.7 = (bf16[6,128,128]{2,1,0:T(8,128)(2,1)S(1)}, bf16[6,128,128]{2,1,0:T(8,128)(2,1)S(1)}, u32[]{:S(2)}, u32[]{:S(2)}) collective-permute-start(bf16[6,128,128]{2,1,0:T(8,128)(2,1)S(1)} %get-tuple-element.26), channel_id=1, source_target_pairs={{1,0},{2,1},{3,2},{4,3},{5,4},{6,5},{7,6},{9,8},{10,9},{11,10},{12... | collective-permute-start | bytes 589832 | tf_op jit(solution)/shard_map/ppermute | solution.py:398
  39.8 1.2 %gram.1.refs_0_ = f32[96,128]{1,0:T(8,128)S(1)} custom-call(s32[1]{0:T(128)S(6)} %copy.8.count_ref, f32[26,128,128]{2,1,0:T(8,128)S(1)} %get-tuple-element.22.image_ref.current_ref), custom_call_target="tpu_custom_call" | custom-call | flops 109051904 | bytes 1703936 | tf_op jit(solution)/shard_map/gram/pallas_call | solution.py:354
  40.9 3.9 %collective-permute-done.7.halo3 = bf16[6,128,128]{2,1,0:T(8,128)(2,1)S(1)} collective-permute-done((bf16[6,128,128]{2,1,0:T(8,128)(2,1)S(1)}, bf16[6,128,128]{2,1,0:T(8,128)(2,1)S(1)}, u32[]{:S(2)}, u32[]{:S(2)}) %collective-permute-start.7) | collective-permute-done | bytes 196640 | tf_op jit(solution)/shard_map/ppermute | solution.py:398
  44.8 3.2 %product.3 = (f32[26,128,128]{2,1,0:T(8,128)S(1)}, f32[96,128]{1,0:T(8,128)S(1)}, f32[96,128]{1,0:T(8,128)S(1)}) custom-call(s32[11,26]{1,0:T(8,128)S(1)} %bitcast.3, s32[38]{0:T(128)S(1)} %copy-done.3, s32[1]{0:T(128)S(6)} %copy.8.count_ref, s32[1]{0:T(128)} %bitcast.core_ref, f32[26,128,128]{2,1,0:T(8,128)S(1)} %get-tuple-element.16.scale_ref, ...), custom_call_target="tpu_custom_call" | custom-call | tf_op jit(solution)/shard_map/product/pallas_call | solution.py:337
  48.0 0.1 collective-permute-start.8
  48.1 1.2 %collective-permute-done.8 = f32[96,128]{1,0:T(8,128)S(1)} collective-permute-done((f32[96,128]{1,0:T(8,128)S(1)}, f32[96,128]{1,0:T(8,128)S(1)}, u32[]{:S(2)}, u32[]{:S(2)}) %collective-permute-start.8) | collective-permute-done | bytes 49184 | tf_op jit(solution)/shard_map/ppermute | solution.py:421
  49.3 0.2 collective-permute-start.11
  49.6 5.9 %collective-permute-start.10 = (f32[96,128]{1,0:T(8,128)S(1)}, f32[96,128]{1,0:T(8,128)S(1)}, u32[]{:S(2)}, u32[]{:S(2)}) collective-permute-start(f32[96,128]{1,0:T(8,128)S(1)} %add.21), channel_id=1, source_target_pairs={{0,6},{1,7},{2,0},{3,1},{4,2},{5,3},{6,4},{7,5},{8,14},{9,15},{10,... | collective-permute-start | bytes 147464 | tf_op jit(solution)/shard_map/ppermute | solution.py:421
  55.5 1.2 %collective-permute-done.10 = f32[96,128]{1,0:T(8,128)S(1)} collective-permute-done((f32[96,128]{1,0:T(8,128)S(1)}, f32[96,128]{1,0:T(8,128)S(1)}, u32[]{:S(2)}, u32[]{:S(2)}) %collective-permute-start.10) | collective-permute-done | bytes 49184 | tf_op jit(solution)/shard_map/ppermute | solution.py:421
  56.7 3.0 %collective-permute-done.9 = f32[96,128]{1,0:T(8,128)S(1)} collective-permute-done((f32[96,128]{1,0:T(8,128)S(1)}, f32[96,128]{1,0:T(8,128)S(1)}, u32[]{:S(2)}, u32[]{:S(2)}) %collective-permute-start.9) | collective-permute-done | bytes 49184 | tf_op jit(solution)/shard_map/ppermute | solution.py:421
  59.7 0.1 collective-permute-start.14
  59.8 0.1 collective-permute-start.13
  59.8 1.5 %collective-permute-start.12 = (f32[96,128]{1,0:T(8,128)S(1)}, f32[96,128]{1,0:T(8,128)S(1)}, u32[]{:S(2)}, u32[]{:S(2)}) collective-permute-start(f32[96,128]{1,0:T(8,128)S(1)} %add_add_fusion.1), channel_id=1, source_target_pairs={{0,8},{1,9},{2,10},{3,11},{4,12},{5,13},{6,14},{7,15},{8,16},{9,17... | collective-permute-start | bytes 147464 | tf_op jit(solution)/shard_map/ppermute | solution.py:421
  61.3 2.9 %collective-permute-done.14 = f32[96,128]{1,0:T(8,128)S(1)} collective-permute-done((f32[96,128]{1,0:T(8,128)S(1)}, f32[96,128]{1,0:T(8,128)S(1)}, u32[]{:S(2)}, u32[]{:S(2)}) %collective-permute-start.14) | collective-permute-done | bytes 49184 | tf_op jit(solution)/shard_map/ppermute | solution.py:421
  64.2 0.5 collective-permute-done.12
  64.8 15.5 %all_to_all.5 = f32[8,96,128]{2,1,0:T(8,128)S(1)} all-to-all(f32[8,96,128]{2,1,0:T(8,128)S(1)} %broadcast_in_dim.3), channel_id=1, replica_groups={{0,32,64,96,128,160,192,224},{1,33,65,97,129,161,193,225},{2,34,66,98,1..., dimensions={0} | all-to-all | bytes 786432 | tf_op jit(solution)/shard_map/all_to_all | solution.py:439
  80.3 5.1 %factor.1.mine_ref = f32[128,256]{1,0:T(8,128)S(1)} custom-call(f32[96,128]{1,0:T(8,128)S(1)} %reduce_sum.9.gram_ref), custom_call_target="tpu_custom_call" | custom-call | tf_op jit(solution)/shard_map/factor/pallas_call | solution.py:368
  85.4 5.1 %collective-permute-start.15 = (f32[128,256]{1,0:T(8,128)S(1)}, f32[128,256]{1,0:T(8,128)S(1)}, u32[]{:S(2)}, u32[]{:S(2)}) collective-permute-start(f32[128,256]{1,0:T(8,128)S(1)} %factor.1.mine_ref), channel_id=1, source_target_pairs={{0,1},{1,0},{2,3},{3,2},{4,5},{5,4},{6,7},{7,6},{8,9},{9,8},{10,11... | collective-permute-start | bytes 393224 | tf_op jit(solution)/shard_map/ppermute | solution.py:421
  90.6 1.0 %collective-permute-done.15.yours_ref = f32[128,256]{1,0:T(8,128)S(1)} collective-permute-done((f32[128,256]{1,0:T(8,128)S(1)}, f32[128,256]{1,0:T(8,128)S(1)}, u32[]{:S(2)}, u32[]{:S(2)}) %collective-permute-start.15) | collective-permute-done | bytes 131104 | tf_op jit(solution)/shard_map/ppermute | solution.py:421
  91.6 2.3 %last.1 = (f32[26,128,128]{2,1,0:T(8,128)}, f32[128,128]{1,0:T(8,128)}) custom-call(s32[1]{0:T(128)} %bitcast.core_ref, f32[128,256]{1,0:T(8,128)S(1)} %factor.1.mine_ref, f32[128,256]{1,0:T(8,128)S(1)} %collective-permute-done.15.yours_ref, f32[26,128,128]{2,1,0:T(8,128)S(1)} %get-tuple-element.29.image_ref), custom_call_target="tpu_custom_call" | custom-call | tf_op jit(solution)/shard_map/last/pallas_call | solution.py:380
  (21 shorter events, 0.1 us)
Async XLA Ops:
  0.6 18.3 %copy-start.1 = (f32[26,128]{1,0:T(8,128)S(1)}, f32[26,128]{1,0:T(8,128)}, u32[]{:S(2)}) copy-start(f32[26,128]{1,0:T(8,128)} %degree_hbm.1) | copy-start | bytes 39940
  3.4 20.2 %collective-permute-start = (bf16[13,128,128]{2,1,0:T(8,128)(2,1)}, bf16[13,128,128]{2,1,0:T(8,128)(2,1)S(1)}, u32[]{:S(2)}, u32[]{:S(2)}) collective-permute-start(bf16[13,128,128]{2,1,0:T(8,128)(2,1)} %get-tuple-element.18), channel_id=1, source_target_pairs={{0,8},{8,16},{16,24},{24,32},{32,40},{40,48},{48,56},{56,64},{64,7... | collective-permute-start | bytes 1277960 | tf_op jit(solution)/shard_map/ppermute | solution.py:398
  5.6 18.0 %collective-permute-start.1 = (bf16[13,128,128]{2,1,0:T(8,128)(2,1)}, bf16[13,128,128]{2,1,0:T(8,128)(2,1)S(1)}, u32[]{:S(2)}, u32[]{:S(2)}) collective-permute-start(bf16[13,128,128]{2,1,0:T(8,128)(2,1)} %get-tuple-element.19), channel_id=1, source_target_pairs={{0,248},{8,0},{16,8},{24,16},{32,24},{40,32},{48,40},{56,48},{64,5... | collective-permute-start | bytes 1277960 | tf_op jit(solution)/shard_map/ppermute | solution.py:398
  12.4 10.4 %collective-permute-start.2 = (bf16[6,128,128]{2,1,0:T(8,128)(2,1)}, bf16[6,128,128]{2,1,0:T(8,128)(2,1)S(1)}, u32[]{:S(2)}, u32[]{:S(2)}) collective-permute-start(bf16[6,128,128]{2,1,0:T(8,128)(2,1)} %get-tuple-element.20), channel_id=1, source_target_pairs={{0,1},{1,2},{2,3},{3,4},{4,5},{5,6},{6,7},{8,9},{9,10},{10,11},{11... | collective-permute-start | bytes 589832 | tf_op jit(solution)/shard_map/ppermute | solution.py:398
  16.4 7.2 %collective-permute-start.3 = (bf16[6,128,128]{2,1,0:T(8,128)(2,1)}, bf16[6,128,128]{2,1,0:T(8,128)(2,1)S(1)}, u32[]{:S(2)}, u32[]{:S(2)}) collective-permute-start(bf16[6,128,128]{2,1,0:T(8,128)(2,1)} %get-tuple-element.21), channel_id=1, source_target_pairs={{1,0},{2,1},{3,2},{4,3},{5,4},{6,5},{7,6},{9,8},{10,9},{11,10},{12... | collective-permute-start | bytes 589832 | tf_op jit(solution)/shard_map/ppermute | solution.py:398
  18.9 4.6 %copy-start = (f32[26,128,128]{2,1,0:T(8,128)S(1)}, f32[26,128,128]{2,1,0:T(8,128)}, u32[]{:S(2)}) copy-start(f32[26,128,128]{2,1,0:T(8,128)} %current_ref.1) | copy-start | bytes 5111812
  19.0 4.6 %copy-start.2 = (s32[26,11]{0,1:T(8,128)S(1)}, s32[26,11]{0,1:T(8,128)}, u32[]{:S(2)}) copy-start(s32[26,11]{0,1:T(8,128)} %param.7) | copy-start | bytes 3436
  19.0 4.6 %copy-start.3 = (s32[38]{0:T(128)S(1)}, s32[38]{0:T(128)}, u32[]{:S(2)}) copy-start(s32[38]{0:T(128)} %sends_ref.3) | copy-start | bytes 460
  26.2 18.6 %collective-permute-start.4 = (bf16[13,128,128]{2,1,0:T(8,128)(2,1)S(1)}, bf16[13,128,128]{2,1,0:T(8,128)(2,1)S(1)}, u32[]{:S(2)}, u32[]{:S(2)}) collective-permute-start(bf16[13,128,128]{2,1,0:T(8,128)(2,1)S(1)} %get-tuple-element.23), channel_id=1, source_target_pairs={{0,8},{8,16},{16,24},{24,32},{32,40},{40,48},{48,56},{56,64},{64,7... | collective-permute-start | bytes 1277960 | tf_op jit(solution)/shard_map/ppermute | solution.py:398
  26.3 18.5 %collective-permute-start.5 = (bf16[13,128,128]{2,1,0:T(8,128)(2,1)S(1)}, bf16[13,128,128]{2,1,0:T(8,128)(2,1)S(1)}, u32[]{:S(2)}, u32[]{:S(2)}) collective-permute-start(bf16[13,128,128]{2,1,0:T(8,128)(2,1)S(1)} %get-tuple-element.24), channel_id=1, source_target_pairs={{0,248},{8,0},{16,8},{24,16},{32,24},{40,32},{48,40},{56,48},{64,5... | collective-permute-start | bytes 1277960 | tf_op jit(solution)/shard_map/ppermute | solution.py:398
  31.1 9.9 %collective-permute-start.6 = (bf16[6,128,128]{2,1,0:T(8,128)(2,1)S(1)}, bf16[6,128,128]{2,1,0:T(8,128)(2,1)S(1)}, u32[]{:S(2)}, u32[]{:S(2)}) collective-permute-start(bf16[6,128,128]{2,1,0:T(8,128)(2,1)S(1)} %get-tuple-element.25), channel_id=1, source_target_pairs={{0,1},{1,2},{2,3},{3,4},{4,5},{5,6},{6,7},{8,9},{9,10},{10,11},{11... | collective-permute-start | bytes 589832 | tf_op jit(solution)/shard_map/ppermute | solution.py:398
  37.8 7.0 %collective-permute-start.7 = (bf16[6,128,128]{2,1,0:T(8,128)(2,1)S(1)}, bf16[6,128,128]{2,1,0:T(8,128)(2,1)S(1)}, u32[]{:S(2)}, u32[]{:S(2)}) collective-permute-start(bf16[6,128,128]{2,1,0:T(8,128)(2,1)S(1)} %get-tuple-element.26), channel_id=1, source_target_pairs={{1,0},{2,1},{3,2},{4,3},{5,4},{6,5},{7,6},{9,8},{10,9},{11,10},{12... | collective-permute-start | bytes 589832 | tf_op jit(solution)/shard_map/ppermute | solution.py:398
  48.0 1.3 %collective-permute-start.8 = (f32[96,128]{1,0:T(8,128)S(1)}, f32[96,128]{1,0:T(8,128)S(1)}, u32[]{:S(2)}, u32[]{:S(2)}) collective-permute-start(f32[96,128]{1,0:T(8,128)S(1)} %get-tuple-element.28), channel_id=1, source_target_pairs={{0,1},{1,0},{2,3},{3,2},{4,5},{5,4},{6,7},{7,6},{8,9},{9,8},{10,11... | collective-permute-start | bytes 147464 | tf_op jit(solution)/shard_map/ppermute | solution.py:421
  49.3 6.2 %collective-permute-start.11 = (f32[96,128]{1,0:T(8,128)S(1)}, f32[96,128]{1,0:T(8,128)S(1)}, u32[]{:S(2)}, u32[]{:S(2)}) collective-permute-start(f32[96,128]{1,0:T(8,128)S(1)} %add.21), channel_id=1, source_target_pairs={{0,4},{1,5},{2,6},{3,7},{4,0},{5,1},{6,2},{7,3},{8,12},{9,13},{10,... | collective-permute-start | bytes 147464 | tf_op jit(solution)/shard_map/ppermute | solution.py:421
  49.6 7.1 %collective-permute-start.10 = (f32[96,128]{1,0:T(8,128)S(1)}, f32[96,128]{1,0:T(8,128)S(1)}, u32[]{:S(2)}, u32[]{:S(2)}) collective-permute-start(f32[96,128]{1,0:T(8,128)S(1)} %add.21), channel_id=1, source_target_pairs={{0,6},{1,7},{2,0},{3,1},{4,2},{5,3},{6,4},{7,5},{8,14},{9,15},{10,... | collective-permute-start | bytes 147464 | tf_op jit(solution)/shard_map/ppermute | solution.py:421
  55.5 4.2 %collective-permute-start.9 = (f32[96,128]{1,0:T(8,128)S(1)}, f32[96,128]{1,0:T(8,128)S(1)}, u32[]{:S(2)}, u32[]{:S(2)}) collective-permute-start(f32[96,128]{1,0:T(8,128)S(1)} %add.21), channel_id=1, source_target_pairs={{0,2},{1,3},{2,4},{3,5},{4,6},{5,7},{6,0},{7,1},{8,10},{9,11},{10,... | collective-permute-start | bytes 147464 | tf_op jit(solution)/shard_map/ppermute | solution.py:421
  59.7 4.6 %collective-permute-start.14 = (f32[96,128]{1,0:T(8,128)S(1)}, f32[96,128]{1,0:T(8,128)S(1)}, u32[]{:S(2)}, u32[]{:S(2)}) collective-permute-start(f32[96,128]{1,0:T(8,128)S(1)} %add_add_fusion.1), channel_id=1, source_target_pairs={{0,16},{1,17},{2,18},{3,19},{4,20},{5,21},{6,22},{7,23},{8,24},{9,... | collective-permute-start | bytes 147464 | tf_op jit(solution)/shard_map/ppermute | solution.py:421
  59.8 4.5 %collective-permute-start.13 = (f32[96,128]{1,0:T(8,128)S(1)}, f32[96,128]{1,0:T(8,128)S(1)}, u32[]{:S(2)}, u32[]{:S(2)}) collective-permute-start(f32[96,128]{1,0:T(8,128)S(1)} %add_add_fusion.1), channel_id=1, source_target_pairs={{0,24},{1,25},{2,26},{3,27},{4,28},{5,29},{6,30},{7,31},{8,0},{9,1... | collective-permute-start | bytes 147464 | tf_op jit(solution)/shard_map/ppermute | solution.py:421
  59.8 4.9 %collective-permute-start.12 = (f32[96,128]{1,0:T(8,128)S(1)}, f32[96,128]{1,0:T(8,128)S(1)}, u32[]{:S(2)}, u32[]{:S(2)}) collective-permute-start(f32[96,128]{1,0:T(8,128)S(1)} %add_add_fusion.1), channel_id=1, source_target_pairs={{0,8},{1,9},{2,10},{3,11},{4,12},{5,13},{6,14},{7,15},{8,16},{9,17... | collective-permute-start | bytes 147464 | tf_op jit(solution)/shard_map/ppermute | solution.py:421
  85.4 6.1 %collective-permute-start.15 = (f32[128,256]{1,0:T(8,128)S(1)}, f32[128,256]{1,0:T(8,128)S(1)}, u32[]{:S(2)}, u32[]{:S(2)}) collective-permute-start(f32[128,256]{1,0:T(8,128)S(1)} %factor.1.mine_ref), channel_id=1, source_target_pairs={{0,1},{1,0},{2,3},{3,2},{4,5},{5,4},{6,7},{7,6},{8,9},{9,8},{10,11... | collective-permute-start | bytes 393224 | tf_op jit(solution)/shard_map/ppermute | solution.py:421

commit v6 on v5

--- a/solution.py
+++ b/solution.py
@@ -9,7 +9,7 @@
 
 AXES = ("group", "dom")
 F32, BF16 = jnp.float32, jnp.bfloat16
-PANEL, GROUP = 16, 2
+PANEL, SUB, GROUP = 16, 8, 13
 ANY = pl.BlockSpec(memory_space=pl.ANY)
 SMEM = pl.BlockSpec(memory_space=pltpu.SMEM)
 VMEM = pl.BlockSpec(memory_space=pltpu.VMEM)
@@ -113,7 +113,7 @@
     if sending:
         image_ref, *out_refs, ext_ref, next_ref = refs
     else:
-        other_ref, image_ref, mine_ref, yours_ref, ext_ref, parts_ref, wide_ref, side_ref = refs
+        other_ref, image_ref, mine_ref, yours_ref, ext_ref, wide_ref, side_ref = refs
     slots, per_row = blocks_ref.shape[:2]
     count = count_ref[0]
     for s in range(slots):
@@ -126,7 +126,6 @@
     if not sending:
         wide_ref[...] = jnp.zeros_like(wide_ref)
         side_ref[...] = jnp.zeros_like(side_ref)
-        parts_ref[...] = jnp.zeros_like(parts_ref)
 
     def row(s):
         left = jnp.concatenate([blocks_ref[s, k] for k in range(per_row)], axis=1)
@@ -135,8 +134,6 @@
         return jnp.where(s < count, image, 0.0)
 
     def rows(step, carry):
-        if not sending:
-            add_gram([parts_ref[i] for i in range(3)], wide_ref, side_ref)
         first = step * GROUP
         images = [row(first + i) for i in range(GROUP)]
         for i, image in enumerate(images):
@@ -144,8 +141,7 @@
             if sending:
                 next_ref[first + i] = (scale_ref[first + i] * image).astype(BF16)
         if not sending:
-            for i, part in enumerate(split3(jnp.concatenate(images, axis=0))):
-                parts_ref[i] = part
+            add_gram(split3(jnp.concatenate(images, axis=0)), wide_ref, side_ref)
         return carry
     steps = (count + GROUP - 1) // GROUP
     lax.fori_loop(0, steps, rows, 0)
@@ -157,7 +153,6 @@
     if sending:
         put_sends(out_refs, sends_ref, next_ref)
     else:
-        add_gram([parts_ref[i] for i in range(3)], wide_ref, side_ref)
         gram = pack_gram(finish_gram(wide_ref, side_ref))
         other, low_core = other_ref[...], core_ref[0] == 0
         mine_ref[...] = jnp.where(low_core, other, gram)
@@ -187,6 +182,25 @@
     return jnp.concatenate(pieces, axis=0)
 
 
+def pair_step(entry, main, side, j, part):
+    a, b = entry[j, j], entry[j, j + 1]
+    det = a * entry[j + 1, j + 1] - b * b
+    first = lax.rsqrt(a)
+    second = first * lax.rsqrt(det)
+    later = [k for k in part if k > j + 1]
+    one = {k: entry[j, k] * first for k in later}
+    two = {k: (a * entry[j + 1, k] - b * entry[j, k]) * second for k in later}
+    for i in later:
+        for k in later:
+            if k >= i:
+                entry[i, k] = entry[i, k] - one[i] * one[k] - two[i] * two[k]
+    for rows in (main, side):
+        rows[j + 1] = (a * rows[j + 1] - b * rows[j]) * second
+        rows[j] = rows[j] * first
+        for i in later:
+            rows[i] = rows[i] - one[i] * rows[j] - two[i] * rows[j + 1]
+
+
 def factorize(work_ref):
     size = work_ref.shape[0]
     step, lanes = PANEL, 8
@@ -195,18 +209,17 @@
         rows = work_ref[top:top + step, :]
         main = [jnp.broadcast_to(rows[i:i + 1, :size], (lanes, size)) for i in range(step)]
         side = [jnp.broadcast_to(rows[i:i + 1, size:], (lanes, size)) for i in range(step)]
-        entry = [[jnp.broadcast_to(main[i][:, top + k:top + k + 1], (lanes, size)) if k >= i else None
-                  for k in range(step)] for i in range(step)]
-        for j in range(step):
-            inv = lax.rsqrt(entry[j][j])
-            main[j] = main[j] * inv
-            side[j] = side[j] * inv
-            scaled = [entry[j][k] * inv if k > j else None for k in range(step)]
-            for i in range(j + 1, step):
-                for k in range(i, step):
-                    entry[i][k] = entry[i][k] - scaled[i] * scaled[k]
-                main[i] = main[i] - scaled[i] * main[j]
-                side[i] = side[i] - scaled[i] * side[j]
+        for begin in range(0, step, SUB):
+            part = range(begin, begin + SUB)
+            entry = {(i, k): jnp.broadcast_to(main[i][:, top + k:top + k + 1], (lanes, size))
+                     for i in part for k in part if k >= i}
+            for j in part[::2]:
+                pair_step(entry, main, side, j, part)
+            for i in range(begin + SUB, step):
+                for j in part:
+                    factor = jnp.broadcast_to(main[j][:, top + i:top + i + 1], (lanes, size))
+                    main[i] = main[i] - factor * main[j]
+                    side[i] = side[i] - factor * side[j]
         both = jnp.concatenate([gather_rows(main, sublane), gather_rows(side, sublane)], axis=1)
         work_ref[top:top + step, :] = both
         if top + step < size:
@@ -214,18 +227,24 @@
             a, b, c = h[:, :size], m[:, :size], l[:, :size]
             left = jnp.concatenate([a, a, b, b, a, c], axis=0)
             right = jnp.concatenate([h, m, h, m, l, h], axis=0)
-            update = dot_rows(left, right)
-            work_ref[top + step:, :] -= update[top + step:, :]
-
-
-def start_factor(gram, denominator, work_ref):
+            turned, near = left.T, top + step
+            work_ref[near:near + step, :] -= dot(turned[near:near + step], right)
+            if near + step < size:
+                work_ref[near + step:, :] -= dot(turned[near + step:], right)
+
+
+def start_factor(gram, work_ref):
     size = work_ref.shape[0]
-    rows = lax.broadcasted_iota(jnp.int32, (size, size), 0)
-    columns = lax.broadcasted_iota(jnp.int32, (size, size), 1)
-    work_ref[:, :size] = gram * F32(1.0 / denominator)
-    work_ref[:, size:] = (rows == columns).astype(F32)
+    same = (lax.broadcasted_iota(jnp.int32, (size, size), 0)
+            == lax.broadcasted_iota(jnp.int32, (size, size), 1))
+    diagonal = jnp.where(same, gram, 0.0)
+    across = jnp.sum(diagonal, axis=0, keepdims=True)
+    down = jnp.sum(diagonal, axis=1, keepdims=True)
+    inverse_root = lax.rsqrt(across)
+    work_ref[:, :size] = gram * lax.rsqrt(down) * inverse_root
+    work_ref[:, size:] = jnp.where(same, inverse_root, 0.0)
     factorize(work_ref)
-    return rows, columns
+    return across * inverse_root
 
 
 def dot_full(a, b):
@@ -251,7 +270,8 @@
 
 
 def factor_kernel(denominator, gram_ref, work_ref):
-    start_factor(unpack_gram(gram_ref[...]), denominator, work_ref)
+    root = start_factor(unpack_gram(gram_ref[...]) * F32(1.0 / denominator), work_ref)
+    work_ref[:, :work_ref.shape[0]] *= root
 
 
 def last_kernel(core_ref, mine_ref, yours_ref, image_ref, basis_hbm, factor_ref,
@@ -333,7 +353,7 @@
         scratch += [pltpu.VMEM(current.shape, BF16)]
     else:
         out_shape = [packed, packed]
-        scratch += [pltpu.VMEM((3, GROUP * nodes, width), BF16)] + gram_scratch(width)
+        scratch += gram_scratch(width)
     return pl.pallas_call(
         functools.partial(product_kernel, sending),
         out_shape=[spread(current.shape, F32)] + out_shape,

time: 93.8 us -> 90.4 us (0.964)
  starting transfers between devices: 41.4 us -> 36.3 us
  blocking collectives: 15.5 us -> 18.2 us
  Pallas kernels: 20.9 us -> 19.9 us
    ppermute x8, starting transfers between devices: 28.4 us -> 25.4 us  [shift(): return lax.ppermute(shard, axis, route)]
    all_to_all x1, blocking collectives: 15.5 us -> 18.2 us  [sum_far(): lax.all_to_all(copies, AXES, 0, 0, axis_index_groups=groups, tiled=True)]
    ppermute x8, starting transfers between devices: 13 us -> 10.9 us  [neighbours(): return lax.ppermute(value, AXES, route)]
  transfers between devices with their start and end apart: 16 -> 16, of which waited for: 8 -> 9; matrix products, arithmetic and copies ran while one was open for 0% -> 0% of each run, Pallas kernels for 5% -> 5%
where the time goes in v6:
time: 90.4 us; the launch traced here: 90.6 us
  starting transfers between devices  36.3 us (40%)
  Pallas kernels  19.9 us (22%)
  blocking collectives  18.2 us (20%)
  waiting for transfers between devices  14.5 us (16%)
  between operations  1.63 us (2%)
    ppermute x8, starting transfers between devices, shift(): return lax.ppermute(shard, axis, route)  25.4 us
    all_to_all x1, blocking collectives, sum_far(): lax.all_to_all(copies, AXES, 0, 0, axis_index_groups=groups, tiled=True)  18.2 us
    ppermute x8, starting transfers between devices, neighbours(): return lax.ppermute(value, AXES, route)  10.9 us
    ppermute x8, waiting for transfers between devices, neighbours(): return lax.ppermute(value, AXES, route)  9.4 us
    pallas_call x2, Pallas kernels, product(): pl.pallas_call(functools.partial(product_kernel, sending), out_shape=[spr...  5.56 us
    ppermute x8, waiting for transfers between devices, shift(): return lax.ppermute(shard, axis, route)  5.1 us
    pallas_call x1, Pallas kernels, factor(): pl.pallas_call(functools.partial(factor_kernel, denominator), out_shape=s...  4.75 us
    pallas_call x1, Pallas kernels, hold(): pl.pallas_call(hold_kernel, out_shape=[spread(blocks.shape, BF16), spread...  3.79 us
  transfers between devices with their start and end apart: 16, of which 9 were waited for; matrix products, arithmetic and copies ran while one was open for 0% of the time, Pallas kernels for 5%

profile of v6, /device:TPU:1, one launch (start us, length us, event | category | flops | bytes accessed | tf_op | source)
XLA Modules:
  0.0 90.6 jit_solution(9067847457927490076)
XLA Ops:
  0.6 2.7 %prep.1 = (bf16[13,128,128]{2,1,0:T(8,128)(2,1)}, bf16[13,128,128]{2,1,0:T(8,128)(2,1)}, bf16[6,128,128]{2,1,0:T(8,128)(2,1)}, bf16[6,128,128]{2,1,0:T(8,128)(2,1)}) custom-call(s32[38]{0:T(128)} %sends_ref.3, f32[26,128]{1,0:T(8,128)} %degree_hbm.1, f32[26,128,128]{2,1,0:T(8,128)} %current_ref.1), custom_call_target="tpu_custom_call" | custom-call | tf_op jit(solution)/shard_map/prep/pallas_call | solution.py:314
  3.4 2.2 %collective-permute-start = (bf16[13,128,128]{2,1,0:T(8,128)(2,1)}, bf16[13,128,128]{2,1,0:T(8,128)(2,1)S(1)}, u32[]{:S(2)}, u32[]{:S(2)}) collective-permute-start(bf16[13,128,128]{2,1,0:T(8,128)(2,1)} %get-tuple-element.18), channel_id=1, source_target_pairs={{0,8},{8,16},{16,24},{24,32},{32,40},{40,48},{48,56},{56,64},{64,7... | collective-permute-start | bytes 1277960 | tf_op jit(solution)/shard_map/ppermute | solution.py:418
  5.6 6.8 %collective-permute-start.1 = (bf16[13,128,128]{2,1,0:T(8,128)(2,1)}, bf16[13,128,128]{2,1,0:T(8,128)(2,1)S(1)}, u32[]{:S(2)}, u32[]{:S(2)}) collective-permute-start(bf16[13,128,128]{2,1,0:T(8,128)(2,1)} %get-tuple-element.19), channel_id=1, source_target_pairs={{0,248},{8,0},{16,8},{24,16},{32,24},{40,32},{48,40},{56,48},{64,5... | collective-permute-start | bytes 1277960 | tf_op jit(solution)/shard_map/ppermute | solution.py:418
  12.4 3.9 %collective-permute-start.2 = (bf16[6,128,128]{2,1,0:T(8,128)(2,1)}, bf16[6,128,128]{2,1,0:T(8,128)(2,1)S(1)}, u32[]{:S(2)}, u32[]{:S(2)}) collective-permute-start(bf16[6,128,128]{2,1,0:T(8,128)(2,1)} %get-tuple-element.20), channel_id=1, source_target_pairs={{0,1},{1,2},{2,3},{3,4},{4,5},{5,6},{6,7},{8,9},{9,10},{10,11},{11... | collective-permute-start | bytes 589832 | tf_op jit(solution)/shard_map/ppermute | solution.py:418
  16.4 1.9 %collective-permute-start.3 = (bf16[6,128,128]{2,1,0:T(8,128)(2,1)}, bf16[6,128,128]{2,1,0:T(8,128)(2,1)S(1)}, u32[]{:S(2)}, u32[]{:S(2)}) collective-permute-start(bf16[6,128,128]{2,1,0:T(8,128)(2,1)} %get-tuple-element.21), channel_id=1, source_target_pairs={{1,0},{2,1},{3,2},{4,3},{5,4},{6,5},{7,6},{9,8},{10,9},{11,10},{12... | collective-permute-start | bytes 589832 | tf_op jit(solution)/shard_map/ppermute | solution.py:418
  19.0 3.8 %hold.1 = (bf16[26,11,128,128]{3,2,1,0:T(8,128)(2,1)S(1)}, f32[26,128,128]{2,1,0:T(8,128)S(1)}) custom-call(bf16[26,11,128,128]{3,2,1,0:T(8,128)(2,1)} %blocks_hbm.1, f32[26,128]{1,0:T(8,128)S(1)} %copy-done.1), custom_call_target="tpu_custom_call" | custom-call | bytes 18743296 | tf_op jit(solution)/shard_map/hold/pallas_call | solution.py:333
  22.8 0.8 collective-permute-done.3.halo3
  23.6 2.6 %product.2 = (f32[26,128,128]{2,1,0:T(8,128)S(1)}, bf16[13,128,128]{2,1,0:T(8,128)(2,1)S(1)}, bf16[13,128,128]{2,1,0:T(8,128)(2,1)S(1)}, bf16[6,128,128]{2,1,0:T(8,128)(2,1)S(1)}, bf16[6,128,128]{2,1,0:T(8,128)(2,1)S(1)}) custom-call(s32[11,26]{1,0:T(8,128)S(1)} %bitcast.2, s32[38]{0:T(128)S(1)} %copy-done.3, s32[1]{0:T(128)S(6)} %copy.8.count_ref, ...), custom_call_target="tpu_custom_call" | custom-call | tf_op jit(solution)/shard_map/product/pallas_call | solution.py:357
  26.2 0.1 collective-permute-start.4
  26.3 4.8 %collective-permute-start.5 = (bf16[13,128,128]{2,1,0:T(8,128)(2,1)S(1)}, bf16[13,128,128]{2,1,0:T(8,128)(2,1)S(1)}, u32[]{:S(2)}, u32[]{:S(2)}) collective-permute-start(bf16[13,128,128]{2,1,0:T(8,128)(2,1)S(1)} %get-tuple-element.24), channel_id=1, source_target_pairs={{0,248},{8,0},{16,8},{24,16},{32,24},{40,32},{48,40},{56,48},{64,5... | collective-permute-start | bytes 1277960 | tf_op jit(solution)/shard_map/ppermute | solution.py:418
  31.1 3.7 %collective-permute-start.6 = (bf16[6,128,128]{2,1,0:T(8,128)(2,1)S(1)}, bf16[6,128,128]{2,1,0:T(8,128)(2,1)S(1)}, u32[]{:S(2)}, u32[]{:S(2)}) collective-permute-start(bf16[6,128,128]{2,1,0:T(8,128)(2,1)S(1)} %get-tuple-element.25), channel_id=1, source_target_pairs={{0,1},{1,2},{2,3},{3,4},{4,5},{5,6},{6,7},{8,9},{9,10},{10,11},{11... | collective-permute-start | bytes 589832 | tf_op jit(solution)/shard_map/ppermute | solution.py:418
  34.8 1.9 %collective-permute-start.7 = (bf16[6,128,128]{2,1,0:T(8,128)(2,1)S(1)}, bf16[6,128,128]{2,1,0:T(8,128)(2,1)S(1)}, u32[]{:S(2)}, u32[]{:S(2)}) collective-permute-start(bf16[6,128,128]{2,1,0:T(8,128)(2,1)S(1)} %get-tuple-element.26), channel_id=1, source_target_pairs={{1,0},{2,1},{3,2},{4,3},{5,4},{6,5},{7,6},{9,8},{10,9},{11,10},{12... | collective-permute-start | bytes 589832 | tf_op jit(solution)/shard_map/ppermute | solution.py:418
  36.7 0.7 gram.1.refs_0_
  37.5 4.3 %collective-permute-done.7.halo3 = bf16[6,128,128]{2,1,0:T(8,128)(2,1)S(1)} collective-permute-done((bf16[6,128,128]{2,1,0:T(8,128)(2,1)S(1)}, bf16[6,128,128]{2,1,0:T(8,128)(2,1)S(1)}, u32[]{:S(2)}, u32[]{:S(2)}) %collective-permute-start.7) | collective-permute-done | bytes 196640 | tf_op jit(solution)/shard_map/ppermute | solution.py:418
  41.8 2.9 %product.3 = (f32[26,128,128]{2,1,0:T(8,128)S(1)}, f32[96,128]{1,0:T(8,128)S(1)}, f32[96,128]{1,0:T(8,128)S(1)}) custom-call(s32[11,26]{1,0:T(8,128)S(1)} %bitcast.3, s32[38]{0:T(128)S(1)} %copy-done.3, s32[1]{0:T(128)S(6)} %copy.8.count_ref, s32[1]{0:T(128)} %bitcast.core_ref, f32[26,128,128]{2,1,0:T(8,128)S(1)} %get-tuple-element.16.scale_ref, ...), custom_call_target="tpu_custom_call" | custom-call | tf_op jit(solution)/shard_map/product/pallas_call | solution.py:357
  44.7 0.1 collective-permute-start.8
  44.9 1.2 %collective-permute-done.8 = f32[96,128]{1,0:T(8,128)S(1)} collective-permute-done((f32[96,128]{1,0:T(8,128)S(1)}, f32[96,128]{1,0:T(8,128)S(1)}, u32[]{:S(2)}, u32[]{:S(2)}) %collective-permute-start.8) | collective-permute-done | bytes 49184 | tf_op jit(solution)/shard_map/ppermute | solution.py:441
  46.1 2.5 %collective-permute-start.11 = (f32[96,128]{1,0:T(8,128)S(1)}, f32[96,128]{1,0:T(8,128)S(1)}, u32[]{:S(2)}, u32[]{:S(2)}) collective-permute-start(f32[96,128]{1,0:T(8,128)S(1)} %add.21), channel_id=1, source_target_pairs={{0,4},{1,5},{2,6},{3,7},{4,0},{5,1},{6,2},{7,3},{8,12},{9,13},{10,... | collective-permute-start | bytes 147464 | tf_op jit(solution)/shard_map/ppermute | solution.py:441
  48.6 1.2 %collective-permute-start.10 = (f32[96,128]{1,0:T(8,128)S(1)}, f32[96,128]{1,0:T(8,128)S(1)}, u32[]{:S(2)}, u32[]{:S(2)}) collective-permute-start(f32[96,128]{1,0:T(8,128)S(1)} %add.21), channel_id=1, source_target_pairs={{0,6},{1,7},{2,0},{3,1},{4,2},{5,3},{6,4},{7,5},{8,14},{9,15},{10,... | collective-permute-start | bytes 147464 | tf_op jit(solution)/shard_map/ppermute | solution.py:441
  49.7 0.3 collective-permute-start.9
  50.0 0.6 collective-permute-done.11
  50.6 0.9 collective-permute-done.10
  51.5 2.4 %collective-permute-done.9 = f32[96,128]{1,0:T(8,128)S(1)} collective-permute-done((f32[96,128]{1,0:T(8,128)S(1)}, f32[96,128]{1,0:T(8,128)S(1)}, u32[]{:S(2)}, u32[]{:S(2)}) %collective-permute-start.9) | collective-permute-done | bytes 49184 | tf_op jit(solution)/shard_map/ppermute | solution.py:441
  53.9 0.3 collective-permute-start.14
  54.2 1.5 %collective-permute-start.12 = (f32[96,128]{1,0:T(8,128)S(1)}, f32[96,128]{1,0:T(8,128)S(1)}, u32[]{:S(2)}, u32[]{:S(2)}) collective-permute-start(f32[96,128]{1,0:T(8,128)S(1)} %add_add_fusion.1), channel_id=1, source_target_pairs={{0,8},{1,9},{2,10},{3,11},{4,12},{5,13},{6,14},{7,15},{8,16},{9,17... | collective-permute-start | bytes 147464 | tf_op jit(solution)/shard_map/ppermute | solution.py:441
  55.7 2.9 %collective-permute-done.14 = f32[96,128]{1,0:T(8,128)S(1)} collective-permute-done((f32[96,128]{1,0:T(8,128)S(1)}, f32[96,128]{1,0:T(8,128)S(1)}, u32[]{:S(2)}, u32[]{:S(2)}) %collective-permute-start.14) | collective-permute-done | bytes 49184 | tf_op jit(solution)/shard_map/ppermute | solution.py:441
  58.6 0.5 collective-permute-done.12
  59.2 18.2 %all_to_all.5 = f32[8,96,128]{2,1,0:T(8,128)S(1)} all-to-all(f32[8,96,128]{2,1,0:T(8,128)S(1)} %broadcast_in_dim.3), channel_id=1, replica_groups={{0,32,64,96,128,160,192,224},{1,33,65,97,129,161,193,225},{2,34,66,98,1..., dimensions={0} | all-to-all | bytes 786432 | tf_op jit(solution)/shard_map/all_to_all | solution.py:459
  77.4 4.8 %factor.1.mine_ref = f32[128,256]{1,0:T(8,128)S(1)} custom-call(f32[96,128]{1,0:T(8,128)S(1)} %reduce_sum.9.gram_ref), custom_call_target="tpu_custom_call" | custom-call | tf_op jit(solution)/shard_map/factor/pallas_call | solution.py:388
  82.1 5.0 %collective-permute-start.15 = (f32[128,256]{1,0:T(8,128)S(1)}, f32[128,256]{1,0:T(8,128)S(1)}, u32[]{:S(2)}, u32[]{:S(2)}) collective-permute-start(f32[128,256]{1,0:T(8,128)S(1)} %factor.1.mine_ref), channel_id=1, source_target_pairs={{0,1},{1,0},{2,3},{3,2},{4,5},{5,4},{6,7},{7,6},{8,9},{9,8},{10,11... | collective-permute-start | bytes 393224 | tf_op jit(solution)/shard_map/ppermute | solution.py:441
  87.1 1.0 %collective-permute-done.15.yours_ref = f32[128,256]{1,0:T(8,128)S(1)} collective-permute-done((f32[128,256]{1,0:T(8,128)S(1)}, f32[128,256]{1,0:T(8,128)S(1)}, u32[]{:S(2)}, u32[]{:S(2)}) %collective-permute-start.15) | collective-permute-done | bytes 131104 | tf_op jit(solution)/shard_map/ppermute | solution.py:441
  88.1 2.3 %last.1 = (f32[26,128,128]{2,1,0:T(8,128)}, f32[128,128]{1,0:T(8,128)}) custom-call(s32[1]{0:T(128)} %bitcast.core_ref, f32[128,256]{1,0:T(8,128)S(1)} %factor.1.mine_ref, f32[128,256]{1,0:T(8,128)S(1)} %collective-permute-done.15.yours_ref, f32[26,128,128]{2,1,0:T(8,128)S(1)} %get-tuple-element.29.image_ref), custom_call_target="tpu_custom_call" | custom-call | tf_op jit(solution)/shard_map/last/pallas_call | solution.py:400
  (21 shorter events, 0.2 us)
Async XLA Ops:
  0.6 18.3 %copy-start.1 = (f32[26,128]{1,0:T(8,128)S(1)}, f32[26,128]{1,0:T(8,128)}, u32[]{:S(2)}) copy-start(f32[26,128]{1,0:T(8,128)} %degree_hbm.1) | copy-start | bytes 39940
  3.4 20.2 %collective-permute-start = (bf16[13,128,128]{2,1,0:T(8,128)(2,1)}, bf16[13,128,128]{2,1,0:T(8,128)(2,1)S(1)}, u32[]{:S(2)}, u32[]{:S(2)}) collective-permute-start(bf16[13,128,128]{2,1,0:T(8,128)(2,1)} %get-tuple-element.18), channel_id=1, source_target_pairs={{0,8},{8,16},{16,24},{24,32},{32,40},{40,48},{48,56},{56,64},{64,7... | collective-permute-start | bytes 1277960 | tf_op jit(solution)/shard_map/ppermute | solution.py:418
  5.6 18.0 %collective-permute-start.1 = (bf16[13,128,128]{2,1,0:T(8,128)(2,1)}, bf16[13,128,128]{2,1,0:T(8,128)(2,1)S(1)}, u32[]{:S(2)}, u32[]{:S(2)}) collective-permute-start(bf16[13,128,128]{2,1,0:T(8,128)(2,1)} %get-tuple-element.19), channel_id=1, source_target_pairs={{0,248},{8,0},{16,8},{24,16},{32,24},{40,32},{48,40},{56,48},{64,5... | collective-permute-start | bytes 1277960 | tf_op jit(solution)/shard_map/ppermute | solution.py:418
  12.4 10.4 %collective-permute-start.2 = (bf16[6,128,128]{2,1,0:T(8,128)(2,1)}, bf16[6,128,128]{2,1,0:T(8,128)(2,1)S(1)}, u32[]{:S(2)}, u32[]{:S(2)}) collective-permute-start(bf16[6,128,128]{2,1,0:T(8,128)(2,1)} %get-tuple-element.20), channel_id=1, source_target_pairs={{0,1},{1,2},{2,3},{3,4},{4,5},{5,6},{6,7},{8,9},{9,10},{10,11},{11... | collective-permute-start | bytes 589832 | tf_op jit(solution)/shard_map/ppermute | solution.py:418
  16.4 7.2 %collective-permute-start.3 = (bf16[6,128,128]{2,1,0:T(8,128)(2,1)}, bf16[6,128,128]{2,1,0:T(8,128)(2,1)S(1)}, u32[]{:S(2)}, u32[]{:S(2)}) collective-permute-start(bf16[6,128,128]{2,1,0:T(8,128)(2,1)} %get-tuple-element.21), channel_id=1, source_target_pairs={{1,0},{2,1},{3,2},{4,3},{5,4},{6,5},{7,6},{9,8},{10,9},{11,10},{12... | collective-permute-start | bytes 589832 | tf_op jit(solution)/shard_map/ppermute | solution.py:418
  18.9 4.6 %copy-start = (f32[26,128,128]{2,1,0:T(8,128)S(1)}, f32[26,128,128]{2,1,0:T(8,128)}, u32[]{:S(2)}) copy-start(f32[26,128,128]{2,1,0:T(8,128)} %current_ref.1) | copy-start | bytes 5111812
  19.0 4.6 %copy-start.2 = (s32[26,11]{0,1:T(8,128)S(1)}, s32[26,11]{0,1:T(8,128)}, u32[]{:S(2)}) copy-start(s32[26,11]{0,1:T(8,128)} %param.7) | copy-start | bytes 3436
  19.0 4.6 %copy-start.3 = (s32[38]{0:T(128)S(1)}, s32[38]{0:T(128)}, u32[]{:S(2)}) copy-start(s32[38]{0:T(128)} %sends_ref.3) | copy-start | bytes 460
  26.2 15.6 %collective-permute-start.4 = (bf16[13,128,128]{2,1,0:T(8,128)(2,1)S(1)}, bf16[13,128,128]{2,1,0:T(8,128)(2,1)S(1)}, u32[]{:S(2)}, u32[]{:S(2)}) collective-permute-start(bf16[13,128,128]{2,1,0:T(8,128)(2,1)S(1)} %get-tuple-element.23), channel_id=1, source_target_pairs={{0,8},{8,16},{16,24},{24,32},{32,40},{40,48},{48,56},{56,64},{64,7... | collective-permute-start | bytes 1277960 | tf_op jit(solution)/shard_map/ppermute | solution.py:418
  26.3 15.5 %collective-permute-start.5 = (bf16[13,128,128]{2,1,0:T(8,128)(2,1)S(1)}, bf16[13,128,128]{2,1,0:T(8,128)(2,1)S(1)}, u32[]{:S(2)}, u32[]{:S(2)}) collective-permute-start(bf16[13,128,128]{2,1,0:T(8,128)(2,1)S(1)} %get-tuple-element.24), channel_id=1, source_target_pairs={{0,248},{8,0},{16,8},{24,16},{32,24},{40,32},{48,40},{56,48},{64,5... | collective-permute-start | bytes 1277960 | tf_op jit(solution)/shard_map/ppermute | solution.py:418
  31.1 6.4 %collective-permute-start.6 = (bf16[6,128,128]{2,1,0:T(8,128)(2,1)S(1)}, bf16[6,128,128]{2,1,0:T(8,128)(2,1)S(1)}, u32[]{:S(2)}, u32[]{:S(2)}) collective-permute-start(bf16[6,128,128]{2,1,0:T(8,128)(2,1)S(1)} %get-tuple-element.25), channel_id=1, source_target_pairs={{0,1},{1,2},{2,3},{3,4},{4,5},{5,6},{6,7},{8,9},{9,10},{10,11},{11... | collective-permute-start | bytes 589832 | tf_op jit(solution)/shard_map/ppermute | solution.py:418
  34.8 7.0 %collective-permute-start.7 = (bf16[6,128,128]{2,1,0:T(8,128)(2,1)S(1)}, bf16[6,128,128]{2,1,0:T(8,128)(2,1)S(1)}, u32[]{:S(2)}, u32[]{:S(2)}) collective-permute-start(bf16[6,128,128]{2,1,0:T(8,128)(2,1)S(1)} %get-tuple-element.26), channel_id=1, source_target_pairs={{1,0},{2,1},{3,2},{4,3},{5,4},{6,5},{7,6},{9,8},{10,9},{11,10},{12... | collective-permute-start | bytes 589832 | tf_op jit(solution)/shard_map/ppermute | solution.py:418
  44.7 1.3 %collective-permute-start.8 = (f32[96,128]{1,0:T(8,128)S(1)}, f32[96,128]{1,0:T(8,128)S(1)}, u32[]{:S(2)}, u32[]{:S(2)}) collective-permute-start(f32[96,128]{1,0:T(8,128)S(1)} %get-tuple-element.28), channel_id=1, source_target_pairs={{0,1},{1,0},{2,3},{3,2},{4,5},{5,4},{6,7},{7,6},{8,9},{9,8},{10,11... | collective-permute-start | bytes 147464 | tf_op jit(solution)/shard_map/ppermute | solution.py:441
  46.1 4.6 %collective-permute-start.11 = (f32[96,128]{1,0:T(8,128)S(1)}, f32[96,128]{1,0:T(8,128)S(1)}, u32[]{:S(2)}, u32[]{:S(2)}) collective-permute-start(f32[96,128]{1,0:T(8,128)S(1)} %add.21), channel_id=1, source_target_pairs={{0,4},{1,5},{2,6},{3,7},{4,0},{5,1},{6,2},{7,3},{8,12},{9,13},{10,... | collective-permute-start | bytes 147464 | tf_op jit(solution)/shard_map/ppermute | solution.py:441
  48.6 2.9 %collective-permute-start.10 = (f32[96,128]{1,0:T(8,128)S(1)}, f32[96,128]{1,0:T(8,128)S(1)}, u32[]{:S(2)}, u32[]{:S(2)}) collective-permute-start(f32[96,128]{1,0:T(8,128)S(1)} %add.21), channel_id=1, source_target_pairs={{0,6},{1,7},{2,0},{3,1},{4,2},{5,3},{6,4},{7,5},{8,14},{9,15},{10,... | collective-permute-start | bytes 147464 | tf_op jit(solution)/shard_map/ppermute | solution.py:441
  49.7 4.2 %collective-permute-start.9 = (f32[96,128]{1,0:T(8,128)S(1)}, f32[96,128]{1,0:T(8,128)S(1)}, u32[]{:S(2)}, u32[]{:S(2)}) collective-permute-start(f32[96,128]{1,0:T(8,128)S(1)} %add.21), channel_id=1, source_target_pairs={{0,2},{1,3},{2,4},{3,5},{4,6},{5,7},{6,0},{7,1},{8,10},{9,11},{10,... | collective-permute-start | bytes 147464 | tf_op jit(solution)/shard_map/ppermute | solution.py:441
  53.9 4.7 %collective-permute-start.14 = (f32[96,128]{1,0:T(8,128)S(1)}, f32[96,128]{1,0:T(8,128)S(1)}, u32[]{:S(2)}, u32[]{:S(2)}) collective-permute-start(f32[96,128]{1,0:T(8,128)S(1)} %add_add_fusion.1), channel_id=1, source_target_pairs={{0,16},{1,17},{2,18},{3,19},{4,20},{5,21},{6,22},{7,23},{8,24},{9,... | collective-permute-start | bytes 147464 | tf_op jit(solution)/shard_map/ppermute | solution.py:441
  54.2 4.5 %collective-permute-start.13 = (f32[96,128]{1,0:T(8,128)S(1)}, f32[96,128]{1,0:T(8,128)S(1)}, u32[]{:S(2)}, u32[]{:S(2)}) collective-permute-start(f32[96,128]{1,0:T(8,128)S(1)} %add_add_fusion.1), channel_id=1, source_target_pairs={{0,24},{1,25},{2,26},{3,27},{4,28},{5,29},{6,30},{7,31},{8,0},{9,1... | collective-permute-start | bytes 147464 | tf_op jit(solution)/shard_map/ppermute | solution.py:441
  54.2 4.9 %collective-permute-start.12 = (f32[96,128]{1,0:T(8,128)S(1)}, f32[96,128]{1,0:T(8,128)S(1)}, u32[]{:S(2)}, u32[]{:S(2)}) collective-permute-start(f32[96,128]{1,0:T(8,128)S(1)} %add_add_fusion.1), channel_id=1, source_target_pairs={{0,8},{1,9},{2,10},{3,11},{4,12},{5,13},{6,14},{7,15},{8,16},{9,17... | collective-permute-start | bytes 147464 | tf_op jit(solution)/shard_map/ppermute | solution.py:441
  82.1 6.0 %collective-permute-start.15 = (f32[128,256]{1,0:T(8,128)S(1)}, f32[128,256]{1,0:T(8,128)S(1)}, u32[]{:S(2)}, u32[]{:S(2)}) collective-permute-start(f32[128,256]{1,0:T(8,128)S(1)} %factor.1.mine_ref), channel_id=1, source_target_pairs={{0,1},{1,0},{2,3},{3,2},{4,5},{5,4},{6,7},{7,6},{8,9},{9,8},{10,11... | collective-permute-start | bytes 393224 | tf_op jit(solution)/shard_map/ppermute | solution.py:441

commit v7 on v6

--- a/solution.py
+++ b/solution.py
@@ -51,22 +51,33 @@
     return wide_ref[:, :width] + (cross + cross.T)
 
 
+def lane_masks(rows, size):
+    lane = lax.broadcasted_iota(jnp.int32, (rows, size), 1)
+    return lane < size // 2, lane % (size // 2) < size // 4
+
+
 def pack_gram(gram):
-    half, quarter = gram.shape[0] // 2, gram.shape[0] // 4
-    left = lax.broadcasted_iota(jnp.int32, (half, gram.shape[1]), 1) < half
+    size = gram.shape[0]
+    half, quarter, eighth = size // 2, size // 4, size // 8
+    left, first = lane_masks(half, size)
     low = gram[half:]
     blocks = jnp.where(left, gram[:half], low)
+    upper, lower = blocks[:quarter], blocks[quarter:]
+    diagonal = jnp.where(first[:quarter], upper, lower)
+    below = jnp.where(first[:eighth], lower[:eighth], pltpu.roll(lower[eighth:], quarter, 1))
     corner = jnp.where(left[:quarter], low[:quarter], pltpu.roll(low[quarter:], half, 1))
-    return jnp.concatenate([blocks, corner], axis=0)
+    return jnp.concatenate([diagonal, below, corner], axis=0)
 
 
 def unpack_gram(packed):
     size = packed.shape[1]
-    half = size // 2
-    left = lax.broadcasted_iota(jnp.int32, (half, size), 1) < half
-    corner = jnp.concatenate([packed[half:], pltpu.roll(packed[half:], half, 1)], axis=0)
-    low = jnp.where(left, corner, packed[:half])
-    full = jnp.concatenate([packed[:half], low], axis=0)
+    half, quarter, eighth = size // 2, size // 4, size // 8
+    left, first = lane_masks(half, size)
+    diagonal, below, corner = packed[:quarter], packed[quarter:quarter + eighth], packed[quarter + eighth:]
+    below = jnp.concatenate([below, pltpu.roll(below, size - quarter, 1)], axis=0)
+    blocks = jnp.concatenate([diagonal, jnp.where(first[:quarter], below, diagonal)], axis=0)
+    corner = jnp.concatenate([corner, pltpu.roll(corner, half, 1)], axis=0)
+    full = jnp.concatenate([blocks, jnp.where(left, corner, blocks)], axis=0)
     rows = lax.broadcasted_iota(jnp.int32, (size, size), 0)
     columns = lax.broadcasted_iota(jnp.int32, (size, size), 1)
     return jnp.where(rows > columns, full, 0.0) + jnp.where(rows >= columns, full, 0.0).T
@@ -346,7 +357,7 @@
     slots, nodes, width = current.shape
     sizes = [h.shape[0] for h in halos]
     sending = other is None
-    packed = spread((3 * width // 4, width), F32)
+    packed = spread((5 * width // 8, width), F32)
     scratch = [pltpu.VMEM((slots + sum(sizes), nodes, width), BF16)]
     if sending:
         out_shape = [spread(h.shape, BF16) for h in halos]
@@ -373,7 +384,7 @@
     width = image.shape[2]
     return pl.pallas_call(
         gram_kernel,
-        out_shape=spread((3 * width // 4, width), F32),
+        out_shape=spread((5 * width // 8, width), F32),
         in_specs=[SMEM, VMEM],
         out_specs=VMEM,
         scratch_shapes=gram_scratch(width),

time: 90.4 us -> 90.4 us (level); the launches traced: 90.6 us -> 89.5 us
  blocking collectives: 18.2 us -> 16.1 us
    all_to_all x1, blocking collectives: 18.2 us -> 16.1 us  [sum_far(): lax.all_to_all(copies, AXES, 0, 0, axis_index_groups=groups, tiled=True)]
    ppermute x8, starting transfers between devices: 25.4 us -> 26.7 us  [shift(): return lax.ppermute(shard, axis, route)]
where the time goes in v7:
time: 90.4 us; the launch traced here: 89.5 us
  starting transfers between devices  37.1 us (41%)
  Pallas kernels  19.9 us (22%)
  blocking collectives  16.1 us (18%)
  waiting for transfers between devices  14.6 us (16%)
  between operations  1.64 us (2%)
    ppermute x8, starting transfers between devices, shift(): return lax.ppermute(shard, axis, route)  26.7 us
    all_to_all x1, blocking collectives, sum_far(): lax.all_to_all(copies, AXES, 0, 0, axis_index_groups=groups, tiled=True)  16.1 us
    ppermute x8, starting transfers between devices, neighbours(): return lax.ppermute(value, AXES, route)  10.4 us
    ppermute x8, waiting for transfers between devices, neighbours(): return lax.ppermute(value, AXES, route)  9.49 us
    pallas_call x2, Pallas kernels, product(): pl.pallas_call(functools.partial(product_kernel, sending), out_shape=[spr...  5.57 us
    ppermute x8, waiting for transfers between devices, shift(): return lax.ppermute(shard, axis, route)  5.09 us
    pallas_call x1, Pallas kernels, factor(): pl.pallas_call(functools.partial(factor_kernel, denominator), out_shape=s...  4.77 us
    pallas_call x1, Pallas kernels, hold(): pl.pallas_call(hold_kernel, out_shape=[spread(blocks.shape, BF16), spread...  3.79 us
  transfers between devices with their start and end apart: 16, of which 9 were waited for; matrix products, arithmetic and copies ran while one was open for 0% of the time, Pallas kernels for 5%

profile of v7, /device:TPU:1, one launch (start us, length us, event | category | flops | bytes accessed | tf_op | source)
XLA Modules:
  0.0 89.5 jit_solution(8105360380907799572)
XLA Ops:
  0.6 2.7 %prep.1 = (bf16[13,128,128]{2,1,0:T(8,128)(2,1)}, bf16[13,128,128]{2,1,0:T(8,128)(2,1)}, bf16[6,128,128]{2,1,0:T(8,128)(2,1)}, bf16[6,128,128]{2,1,0:T(8,128)(2,1)}) custom-call(s32[38]{0:T(128)} %sends_ref.3, f32[26,128]{1,0:T(8,128)} %degree_hbm.1, f32[26,128,128]{2,1,0:T(8,128)} %current_ref.1), custom_call_target="tpu_custom_call" | custom-call | tf_op jit(solution)/shard_map/prep/pallas_call | solution.py:325
  3.4 2.2 %collective-permute-start = (bf16[13,128,128]{2,1,0:T(8,128)(2,1)}, bf16[13,128,128]{2,1,0:T(8,128)(2,1)S(1)}, u32[]{:S(2)}, u32[]{:S(2)}) collective-permute-start(bf16[13,128,128]{2,1,0:T(8,128)(2,1)} %get-tuple-element.18), channel_id=1, source_target_pairs={{0,8},{8,16},{16,24},{24,32},{32,40},{40,48},{48,56},{56,64},{64,7... | collective-permute-start | bytes 1277960 | tf_op jit(solution)/shard_map/ppermute | solution.py:429
  5.6 6.8 %collective-permute-start.1 = (bf16[13,128,128]{2,1,0:T(8,128)(2,1)}, bf16[13,128,128]{2,1,0:T(8,128)(2,1)S(1)}, u32[]{:S(2)}, u32[]{:S(2)}) collective-permute-start(bf16[13,128,128]{2,1,0:T(8,128)(2,1)} %get-tuple-element.19), channel_id=1, source_target_pairs={{0,248},{8,0},{16,8},{24,16},{32,24},{40,32},{48,40},{56,48},{64,5... | collective-permute-start | bytes 1277960 | tf_op jit(solution)/shard_map/ppermute | solution.py:429
  12.4 3.9 %collective-permute-start.2 = (bf16[6,128,128]{2,1,0:T(8,128)(2,1)}, bf16[6,128,128]{2,1,0:T(8,128)(2,1)S(1)}, u32[]{:S(2)}, u32[]{:S(2)}) collective-permute-start(bf16[6,128,128]{2,1,0:T(8,128)(2,1)} %get-tuple-element.20), channel_id=1, source_target_pairs={{0,1},{1,2},{2,3},{3,4},{4,5},{5,6},{6,7},{8,9},{9,10},{10,11},{11... | collective-permute-start | bytes 589832 | tf_op jit(solution)/shard_map/ppermute | solution.py:429
  16.4 1.9 %collective-permute-start.3 = (bf16[6,128,128]{2,1,0:T(8,128)(2,1)}, bf16[6,128,128]{2,1,0:T(8,128)(2,1)S(1)}, u32[]{:S(2)}, u32[]{:S(2)}) collective-permute-start(bf16[6,128,128]{2,1,0:T(8,128)(2,1)} %get-tuple-element.21), channel_id=1, source_target_pairs={{1,0},{2,1},{3,2},{4,3},{5,4},{6,5},{7,6},{9,8},{10,9},{11,10},{12... | collective-permute-start | bytes 589832 | tf_op jit(solution)/shard_map/ppermute | solution.py:429
  19.0 3.8 %hold.1 = (bf16[26,11,128,128]{3,2,1,0:T(8,128)(2,1)S(1)}, f32[26,128,128]{2,1,0:T(8,128)S(1)}) custom-call(bf16[26,11,128,128]{3,2,1,0:T(8,128)(2,1)} %blocks_hbm.1, f32[26,128]{1,0:T(8,128)S(1)} %copy-done.1), custom_call_target="tpu_custom_call" | custom-call | bytes 18743296 | tf_op jit(solution)/shard_map/hold/pallas_call | solution.py:344
  22.8 0.8 collective-permute-done.3.halo3
  23.6 2.6 %product.2 = (f32[26,128,128]{2,1,0:T(8,128)S(1)}, bf16[13,128,128]{2,1,0:T(8,128)(2,1)S(1)}, bf16[13,128,128]{2,1,0:T(8,128)(2,1)S(1)}, bf16[6,128,128]{2,1,0:T(8,128)(2,1)S(1)}, bf16[6,128,128]{2,1,0:T(8,128)(2,1)S(1)}) custom-call(s32[11,26]{1,0:T(8,128)S(1)} %bitcast.2, s32[38]{0:T(128)S(1)} %copy-done.3, s32[1]{0:T(128)S(6)} %copy.8.count_ref, ...), custom_call_target="tpu_custom_call" | custom-call | tf_op jit(solution)/shard_map/product/pallas_call | solution.py:368
  26.2 0.1 collective-permute-start.4
  26.3 4.8 %collective-permute-start.5 = (bf16[13,128,128]{2,1,0:T(8,128)(2,1)S(1)}, bf16[13,128,128]{2,1,0:T(8,128)(2,1)S(1)}, u32[]{:S(2)}, u32[]{:S(2)}) collective-permute-start(bf16[13,128,128]{2,1,0:T(8,128)(2,1)S(1)} %get-tuple-element.24), channel_id=1, source_target_pairs={{0,248},{8,0},{16,8},{24,16},{32,24},{40,32},{48,40},{56,48},{64,5... | collective-permute-start | bytes 1277960 | tf_op jit(solution)/shard_map/ppermute | solution.py:429
  31.1 5.0 %collective-permute-start.6 = (bf16[6,128,128]{2,1,0:T(8,128)(2,1)S(1)}, bf16[6,128,128]{2,1,0:T(8,128)(2,1)S(1)}, u32[]{:S(2)}, u32[]{:S(2)}) collective-permute-start(bf16[6,128,128]{2,1,0:T(8,128)(2,1)S(1)} %get-tuple-element.25), channel_id=1, source_target_pairs={{0,1},{1,2},{2,3},{3,4},{4,5},{5,6},{6,7},{8,9},{9,10},{10,11},{11... | collective-permute-start | bytes 589832 | tf_op jit(solution)/shard_map/ppermute | solution.py:429
  36.1 1.9 %collective-permute-start.7 = (bf16[6,128,128]{2,1,0:T(8,128)(2,1)S(1)}, bf16[6,128,128]{2,1,0:T(8,128)(2,1)S(1)}, u32[]{:S(2)}, u32[]{:S(2)}) collective-permute-start(bf16[6,128,128]{2,1,0:T(8,128)(2,1)S(1)} %get-tuple-element.26), channel_id=1, source_target_pairs={{1,0},{2,1},{3,2},{4,3},{5,4},{6,5},{7,6},{9,8},{10,9},{11,10},{12... | collective-permute-start | bytes 589832 | tf_op jit(solution)/shard_map/ppermute | solution.py:429
  38.1 0.7 gram.1.refs_0_
  38.8 4.3 %collective-permute-done.7.halo3 = bf16[6,128,128]{2,1,0:T(8,128)(2,1)S(1)} collective-permute-done((bf16[6,128,128]{2,1,0:T(8,128)(2,1)S(1)}, bf16[6,128,128]{2,1,0:T(8,128)(2,1)S(1)}, u32[]{:S(2)}, u32[]{:S(2)}) %collective-permute-start.7) | collective-permute-done | bytes 196640 | tf_op jit(solution)/shard_map/ppermute | solution.py:429
  43.1 2.9 %product.3 = (f32[26,128,128]{2,1,0:T(8,128)S(1)}, f32[80,128]{1,0:T(8,128)S(1)}, f32[80,128]{1,0:T(8,128)S(1)}) custom-call(s32[11,26]{1,0:T(8,128)S(1)} %bitcast.3, s32[38]{0:T(128)S(1)} %copy-done.3, s32[1]{0:T(128)S(6)} %copy.8.count_ref, s32[1]{0:T(128)} %bitcast.core_ref, f32[26,128,128]{2,1,0:T(8,128)S(1)} %get-tuple-element.16.scale_ref, ...), custom_call_target="tpu_custom_call" | custom-call | tf_op jit(solution)/shard_map/product/pallas_call | solution.py:368
  46.1 0.1 collective-permute-start.8
  46.2 1.2 %collective-permute-done.8 = f32[80,128]{1,0:T(8,128)S(1)} collective-permute-done((f32[80,128]{1,0:T(8,128)S(1)}, f32[80,128]{1,0:T(8,128)S(1)}, u32[]{:S(2)}, u32[]{:S(2)}) %collective-permute-start.8) | collective-permute-done | bytes 40992 | tf_op jit(solution)/shard_map/ppermute | solution.py:452
  47.4 1.1 %collective-permute-start.11 = (f32[80,128]{1,0:T(8,128)S(1)}, f32[80,128]{1,0:T(8,128)S(1)}, u32[]{:S(2)}, u32[]{:S(2)}) collective-permute-start(f32[80,128]{1,0:T(8,128)S(1)} %add.21), channel_id=1, source_target_pairs={{0,4},{1,5},{2,6},{3,7},{4,0},{5,1},{6,2},{7,3},{8,12},{9,13},{10,... | collective-permute-start | bytes 122888 | tf_op jit(solution)/shard_map/ppermute | solution.py:452
  48.5 2.6 %collective-permute-start.10 = (f32[80,128]{1,0:T(8,128)S(1)}, f32[80,128]{1,0:T(8,128)S(1)}, u32[]{:S(2)}, u32[]{:S(2)}) collective-permute-start(f32[80,128]{1,0:T(8,128)S(1)} %add.21), channel_id=1, source_target_pairs={{0,6},{1,7},{2,0},{3,1},{4,2},{5,3},{6,4},{7,5},{8,14},{9,15},{10,... | collective-permute-start | bytes 122888 | tf_op jit(solution)/shard_map/ppermute | solution.py:452
  51.1 0.6 collective-permute-done.11
  51.8 0.5 collective-permute-done.10
  52.2 3.0 %collective-permute-done.9 = f32[80,128]{1,0:T(8,128)S(1)} collective-permute-done((f32[80,128]{1,0:T(8,128)S(1)}, f32[80,128]{1,0:T(8,128)S(1)}, u32[]{:S(2)}, u32[]{:S(2)}) %collective-permute-start.9) | collective-permute-done | bytes 40992 | tf_op jit(solution)/shard_map/ppermute | solution.py:452
  55.2 0.3 collective-permute-start.14
  55.5 0.1 collective-permute-start.13
  55.6 1.5 %collective-permute-start.12 = (f32[80,128]{1,0:T(8,128)S(1)}, f32[80,128]{1,0:T(8,128)S(1)}, u32[]{:S(2)}, u32[]{:S(2)}) collective-permute-start(f32[80,128]{1,0:T(8,128)S(1)} %add_add_fusion.1), channel_id=1, source_target_pairs={{0,8},{1,9},{2,10},{3,11},{4,12},{5,13},{6,14},{7,15},{8,16},{9,17... | collective-permute-start | bytes 122888 | tf_op jit(solution)/shard_map/ppermute | solution.py:452
  57.0 2.8 %collective-permute-done.14 = f32[80,128]{1,0:T(8,128)S(1)} collective-permute-done((f32[80,128]{1,0:T(8,128)S(1)}, f32[80,128]{1,0:T(8,128)S(1)}, u32[]{:S(2)}, u32[]{:S(2)}) %collective-permute-start.14) | collective-permute-done | bytes 40992 | tf_op jit(solution)/shard_map/ppermute | solution.py:452
  59.8 0.4 collective-permute-done.12
  60.3 16.1 %all_to_all.5 = f32[8,80,128]{2,1,0:T(8,128)S(1)} all-to-all(f32[8,80,128]{2,1,0:T(8,128)S(1)} %broadcast_in_dim.3), channel_id=1, replica_groups={{0,32,64,96,128,160,192,224},{1,33,65,97,129,161,193,225},{2,34,66,98,1..., dimensions={0} | all-to-all | bytes 655360 | tf_op jit(solution)/shard_map/all_to_all | solution.py:470
  76.4 4.8 %factor.1.mine_ref = f32[128,256]{1,0:T(8,128)S(1)} custom-call(f32[80,128]{1,0:T(8,128)S(1)} %reduce_sum.9.gram_ref), custom_call_target="tpu_custom_call" | custom-call | tf_op jit(solution)/shard_map/factor/pallas_call | solution.py:399
  81.2 4.8 %collective-permute-start.15 = (f32[128,256]{1,0:T(8,128)S(1)}, f32[128,256]{1,0:T(8,128)S(1)}, u32[]{:S(2)}, u32[]{:S(2)}) collective-permute-start(f32[128,256]{1,0:T(8,128)S(1)} %factor.1.mine_ref), channel_id=1, source_target_pairs={{0,1},{1,0},{2,3},{3,2},{4,5},{5,4},{6,7},{7,6},{8,9},{9,8},{10,11... | collective-permute-start | bytes 393224 | tf_op jit(solution)/shard_map/ppermute | solution.py:452
  86.0 1.0 %collective-permute-done.15.yours_ref = f32[128,256]{1,0:T(8,128)S(1)} collective-permute-done((f32[128,256]{1,0:T(8,128)S(1)}, f32[128,256]{1,0:T(8,128)S(1)}, u32[]{:S(2)}, u32[]{:S(2)}) %collective-permute-start.15) | collective-permute-done | bytes 131104 | tf_op jit(solution)/shard_map/ppermute | solution.py:452
  87.0 2.3 %last.1 = (f32[26,128,128]{2,1,0:T(8,128)}, f32[128,128]{1,0:T(8,128)}) custom-call(s32[1]{0:T(128)} %bitcast.core_ref, f32[128,256]{1,0:T(8,128)S(1)} %factor.1.mine_ref, f32[128,256]{1,0:T(8,128)S(1)} %collective-permute-done.15.yours_ref, f32[26,128,128]{2,1,0:T(8,128)S(1)} %get-tuple-element.29.image_ref), custom_call_target="tpu_custom_call" | custom-call | tf_op jit(solution)/shard_map/last/pallas_call | solution.py:411
  (21 shorter events, 0.1 us)
Async XLA Ops:
  0.6 18.3 %copy-start.1 = (f32[26,128]{1,0:T(8,128)S(1)}, f32[26,128]{1,0:T(8,128)}, u32[]{:S(2)}) copy-start(f32[26,128]{1,0:T(8,128)} %degree_hbm.1) | copy-start | bytes 39940
  3.4 20.2 %collective-permute-start = (bf16[13,128,128]{2,1,0:T(8,128)(2,1)}, bf16[13,128,128]{2,1,0:T(8,128)(2,1)S(1)}, u32[]{:S(2)}, u32[]{:S(2)}) collective-permute-start(bf16[13,128,128]{2,1,0:T(8,128)(2,1)} %get-tuple-element.18), channel_id=1, source_target_pairs={{0,8},{8,16},{16,24},{24,32},{32,40},{40,48},{48,56},{56,64},{64,7... | collective-permute-start | bytes 1277960 | tf_op jit(solution)/shard_map/ppermute | solution.py:429
  5.6 18.0 %collective-permute-start.1 = (bf16[13,128,128]{2,1,0:T(8,128)(2,1)}, bf16[13,128,128]{2,1,0:T(8,128)(2,1)S(1)}, u32[]{:S(2)}, u32[]{:S(2)}) collective-permute-start(bf16[13,128,128]{2,1,0:T(8,128)(2,1)} %get-tuple-element.19), channel_id=1, source_target_pairs={{0,248},{8,0},{16,8},{24,16},{32,24},{40,32},{48,40},{56,48},{64,5... | collective-permute-start | bytes 1277960 | tf_op jit(solution)/shard_map/ppermute | solution.py:429
  12.4 10.4 %collective-permute-start.2 = (bf16[6,128,128]{2,1,0:T(8,128)(2,1)}, bf16[6,128,128]{2,1,0:T(8,128)(2,1)S(1)}, u32[]{:S(2)}, u32[]{:S(2)}) collective-permute-start(bf16[6,128,128]{2,1,0:T(8,128)(2,1)} %get-tuple-element.20), channel_id=1, source_target_pairs={{0,1},{1,2},{2,3},{3,4},{4,5},{5,6},{6,7},{8,9},{9,10},{10,11},{11... | collective-permute-start | bytes 589832 | tf_op jit(solution)/shard_map/ppermute | solution.py:429
  16.4 7.2 %collective-permute-start.3 = (bf16[6,128,128]{2,1,0:T(8,128)(2,1)}, bf16[6,128,128]{2,1,0:T(8,128)(2,1)S(1)}, u32[]{:S(2)}, u32[]{:S(2)}) collective-permute-start(bf16[6,128,128]{2,1,0:T(8,128)(2,1)} %get-tuple-element.21), channel_id=1, source_target_pairs={{1,0},{2,1},{3,2},{4,3},{5,4},{6,5},{7,6},{9,8},{10,9},{11,10},{12... | collective-permute-start | bytes 589832 | tf_op jit(solution)/shard_map/ppermute | solution.py:429
  18.9 4.6 %copy-start = (f32[26,128,128]{2,1,0:T(8,128)S(1)}, f32[26,128,128]{2,1,0:T(8,128)}, u32[]{:S(2)}) copy-start(f32[26,128,128]{2,1,0:T(8,128)} %current_ref.1) | copy-start | bytes 5111812
  19.0 4.6 %copy-start.2 = (s32[26,11]{0,1:T(8,128)S(1)}, s32[26,11]{0,1:T(8,128)}, u32[]{:S(2)}) copy-start(s32[26,11]{0,1:T(8,128)} %param.7) | copy-start | bytes 3436
  19.0 4.6 %copy-start.3 = (s32[38]{0:T(128)S(1)}, s32[38]{0:T(128)}, u32[]{:S(2)}) copy-start(s32[38]{0:T(128)} %sends_ref.3) | copy-start | bytes 460
  26.2 16.9 %collective-permute-start.4 = (bf16[13,128,128]{2,1,0:T(8,128)(2,1)S(1)}, bf16[13,128,128]{2,1,0:T(8,128)(2,1)S(1)}, u32[]{:S(2)}, u32[]{:S(2)}) collective-permute-start(bf16[13,128,128]{2,1,0:T(8,128)(2,1)S(1)} %get-tuple-element.23), channel_id=1, source_target_pairs={{0,8},{8,16},{16,24},{24,32},{32,40},{40,48},{48,56},{56,64},{64,7... | collective-permute-start | bytes 1277960 | tf_op jit(solution)/shard_map/ppermute | solution.py:429
  26.3 16.8 %collective-permute-start.5 = (bf16[13,128,128]{2,1,0:T(8,128)(2,1)S(1)}, bf16[13,128,128]{2,1,0:T(8,128)(2,1)S(1)}, u32[]{:S(2)}, u32[]{:S(2)}) collective-permute-start(bf16[13,128,128]{2,1,0:T(8,128)(2,1)S(1)} %get-tuple-element.24), channel_id=1, source_target_pairs={{0,248},{8,0},{16,8},{24,16},{32,24},{40,32},{48,40},{56,48},{64,5... | collective-permute-start | bytes 1277960 | tf_op jit(solution)/shard_map/ppermute | solution.py:429
  31.1 7.7 %collective-permute-start.6 = (bf16[6,128,128]{2,1,0:T(8,128)(2,1)S(1)}, bf16[6,128,128]{2,1,0:T(8,128)(2,1)S(1)}, u32[]{:S(2)}, u32[]{:S(2)}) collective-permute-start(bf16[6,128,128]{2,1,0:T(8,128)(2,1)S(1)} %get-tuple-element.25), channel_id=1, source_target_pairs={{0,1},{1,2},{2,3},{3,4},{4,5},{5,6},{6,7},{8,9},{9,10},{10,11},{11... | collective-permute-start | bytes 589832 | tf_op jit(solution)/shard_map/ppermute | solution.py:429
  36.1 7.0 %collective-permute-start.7 = (bf16[6,128,128]{2,1,0:T(8,128)(2,1)S(1)}, bf16[6,128,128]{2,1,0:T(8,128)(2,1)S(1)}, u32[]{:S(2)}, u32[]{:S(2)}) collective-permute-start(bf16[6,128,128]{2,1,0:T(8,128)(2,1)S(1)} %get-tuple-element.26), channel_id=1, source_target_pairs={{1,0},{2,1},{3,2},{4,3},{5,4},{6,5},{7,6},{9,8},{10,9},{11,10},{12... | collective-permute-start | bytes 589832 | tf_op jit(solution)/shard_map/ppermute | solution.py:429
  46.1 1.3 %collective-permute-start.8 = (f32[80,128]{1,0:T(8,128)S(1)}, f32[80,128]{1,0:T(8,128)S(1)}, u32[]{:S(2)}, u32[]{:S(2)}) collective-permute-start(f32[80,128]{1,0:T(8,128)S(1)} %get-tuple-element.28), channel_id=1, source_target_pairs={{0,1},{1,0},{2,3},{3,2},{4,5},{5,4},{6,7},{7,6},{8,9},{9,8},{10,11... | collective-permute-start | bytes 122888 | tf_op jit(solution)/shard_map/ppermute | solution.py:452
  47.4 4.4 %collective-permute-start.11 = (f32[80,128]{1,0:T(8,128)S(1)}, f32[80,128]{1,0:T(8,128)S(1)}, u32[]{:S(2)}, u32[]{:S(2)}) collective-permute-start(f32[80,128]{1,0:T(8,128)S(1)} %add.21), channel_id=1, source_target_pairs={{0,4},{1,5},{2,6},{3,7},{4,0},{5,1},{6,2},{7,3},{8,12},{9,13},{10,... | collective-permute-start | bytes 122888 | tf_op jit(solution)/shard_map/ppermute | solution.py:452
  48.5 3.7 %collective-permute-start.10 = (f32[80,128]{1,0:T(8,128)S(1)}, f32[80,128]{1,0:T(8,128)S(1)}, u32[]{:S(2)}, u32[]{:S(2)}) collective-permute-start(f32[80,128]{1,0:T(8,128)S(1)} %add.21), channel_id=1, source_target_pairs={{0,6},{1,7},{2,0},{3,1},{4,2},{5,3},{6,4},{7,5},{8,14},{9,15},{10,... | collective-permute-start | bytes 122888 | tf_op jit(solution)/shard_map/ppermute | solution.py:452
  51.1 4.1 %collective-permute-start.9 = (f32[80,128]{1,0:T(8,128)S(1)}, f32[80,128]{1,0:T(8,128)S(1)}, u32[]{:S(2)}, u32[]{:S(2)}) collective-permute-start(f32[80,128]{1,0:T(8,128)S(1)} %add.21), channel_id=1, source_target_pairs={{0,2},{1,3},{2,4},{3,5},{4,6},{5,7},{6,0},{7,1},{8,10},{9,11},{10,... | collective-permute-start | bytes 122888 | tf_op jit(solution)/shard_map/ppermute | solution.py:452
  55.2 4.6 %collective-permute-start.14 = (f32[80,128]{1,0:T(8,128)S(1)}, f32[80,128]{1,0:T(8,128)S(1)}, u32[]{:S(2)}, u32[]{:S(2)}) collective-permute-start(f32[80,128]{1,0:T(8,128)S(1)} %add_add_fusion.1), channel_id=1, source_target_pairs={{0,16},{1,17},{2,18},{3,19},{4,20},{5,21},{6,22},{7,23},{8,24},{9,... | collective-permute-start | bytes 122888 | tf_op jit(solution)/shard_map/ppermute | solution.py:452
  55.5 4.4 %collective-permute-start.13 = (f32[80,128]{1,0:T(8,128)S(1)}, f32[80,128]{1,0:T(8,128)S(1)}, u32[]{:S(2)}, u32[]{:S(2)}) collective-permute-start(f32[80,128]{1,0:T(8,128)S(1)} %add_add_fusion.1), channel_id=1, source_target_pairs={{0,24},{1,25},{2,26},{3,27},{4,28},{5,29},{6,30},{7,31},{8,0},{9,1... | collective-permute-start | bytes 122888 | tf_op jit(solution)/shard_map/ppermute | solution.py:452
  55.6 4.7 %collective-permute-start.12 = (f32[80,128]{1,0:T(8,128)S(1)}, f32[80,128]{1,0:T(8,128)S(1)}, u32[]{:S(2)}, u32[]{:S(2)}) collective-permute-start(f32[80,128]{1,0:T(8,128)S(1)} %add_add_fusion.1), channel_id=1, source_target_pairs={{0,8},{1,9},{2,10},{3,11},{4,12},{5,13},{6,14},{7,15},{8,16},{9,17... | collective-permute-start | bytes 122888 | tf_op jit(solution)/shard_map/ppermute | solution.py:452
  81.2 5.8 %collective-permute-start.15 = (f32[128,256]{1,0:T(8,128)S(1)}, f32[128,256]{1,0:T(8,128)S(1)}, u32[]{:S(2)}, u32[]{:S(2)}) collective-permute-start(f32[128,256]{1,0:T(8,128)S(1)} %factor.1.mine_ref), channel_id=1, source_target_pairs={{0,1},{1,0},{2,3},{3,2},{4,5},{5,4},{6,7},{7,6},{8,9},{9,8},{10,11... | collective-permute-start | bytes 393224 | tf_op jit(solution)/shard_map/ppermute | solution.py:452

commit v8 on v7

--- a/solution.py
+++ b/solution.py
@@ -461,13 +461,15 @@
 
 
 def sum_far(value):
-    extents = place()
-    depth, stride = extents[0], math.prod(extents[1:])
+    depth = place()[0]
     if depth == 1:
         return value
-    groups = [[z * stride + i for z in range(depth)] for i in range(stride)]
-    copies = jnp.broadcast_to(value, (depth,) + value.shape)
-    return lax.all_to_all(copies, AXES, 0, 0, axis_index_groups=groups, tiled=True).sum(0)
+    stride = math.prod(place()[1:])
+    value = value + lax.ppermute(value, AXES, [(i, i ^ stride) for i in range(depth * stride)])
+    order = sorted(range(2, depth, 2), key=lambda k: min(k, depth - k))
+    for piece in [neighbours(value, 0, k) for k in order]:
+        value = value + piece
+    return value
 
 
 def summed(mine, yours):

time: 90.4 us -> 89.9 us (level); the launches traced: 89.5 us -> 90.6 us
  blocking collectives: 16.1 us -> 0 us
  waiting for transfers between devices: 14.6 us -> 21.6 us
  starting transfers between devices: 37.1 us -> 43.7 us
  Pallas kernels: 19.9 us -> 23.6 us
    all_to_all x1 -> x0, blocking collectives: 16.1 us -> none  [sum_far(): lax.all_to_all(copies, AXES, 0, 0, axis_index_groups=groups, tiled=True)]
    ppermute x8 -> x11, starting transfers between devices: 10.4 us -> 18.8 us  [neighbours(): return lax.ppermute(value, AXES, route)]
    ppermute x8 -> x11, waiting for transfers between devices: 9.49 us -> 14.3 us  [neighbours(): return lax.ppermute(value, AXES, route)]
    pallas_call x2, Pallas kernels: 5.57 us -> 8.66 us  [product(): pl.pallas_call(functools.partial(product_kernel, sending), out_shape=[spr...]
    ppermute x0 -> x1, waiting for transfers between devices: none -> 2.84 us  [sum_far(): lax.ppermute(value, AXES, [(i, i ^ stride) for i in range(depth * stride)])]
    ppermute x8, starting transfers between devices: 26.7 us -> 24.8 us  [shift(): return lax.ppermute(shard, axis, route)]
  transfers between devices with their start and end apart: 16 -> 20, of which waited for: 9 -> 11; matrix products, arithmetic and copies ran while one was open for 0% -> 0% of each run, Pallas kernels for 5% -> 6%
where the time goes in v8:
time: 89.9 us; the launch traced here: 90.6 us
  starting transfers between devices  43.7 us (49%)
  Pallas kernels  23.6 us (26%)
  waiting for transfers between devices  21.6 us (24%)
  between operations  1.64 us (2%)
    ppermute x8, starting transfers between devices, shift(): return lax.ppermute(shard, axis, route)  24.8 us
    ppermute x11, starting transfers between devices, neighbours(): return lax.ppermute(value, AXES, route)  18.8 us
    ppermute x11, waiting for transfers between devices, neighbours(): return lax.ppermute(value, AXES, route)  14.3 us
    pallas_call x2, Pallas kernels, product(): pl.pallas_call(functools.partial(product_kernel, sending), out_shape=[spr...  8.66 us
    pallas_call x1, Pallas kernels, factor(): pl.pallas_call(functools.partial(factor_kernel, denominator), out_shape=s...  4.77 us
    ppermute x8, waiting for transfers between devices, shift(): return lax.ppermute(shard, axis, route)  4.54 us
    pallas_call x1, Pallas kernels, hold(): pl.pallas_call(hold_kernel, out_shape=[spread(blocks.shape, BF16), spread...  3.79 us
    ppermute x1, waiting for transfers between devices, sum_far(): lax.ppermute(value, AXES, [(i, i ^ stride) for i in range(depth * stride)])  2.84 us
  transfers between devices with their start and end apart: 20, of which 11 were waited for; matrix products, arithmetic and copies ran while one was open for 0% of the time, Pallas kernels for 6%

profile of v8, /device:TPU:1, one launch (start us, length us, event | category | flops | bytes accessed | tf_op | source)
XLA Modules:
  0.0 90.6 jit_solution(16719861667930489450)
XLA Ops:
  0.6 2.7 %prep.1 = (bf16[13,128,128]{2,1,0:T(8,128)(2,1)}, bf16[13,128,128]{2,1,0:T(8,128)(2,1)}, bf16[6,128,128]{2,1,0:T(8,128)(2,1)}, bf16[6,128,128]{2,1,0:T(8,128)(2,1)}) custom-call(s32[38]{0:T(128)} %sends_ref.3, f32[26,128]{1,0:T(8,128)} %degree_hbm.1, f32[26,128,128]{2,1,0:T(8,128)} %current_ref.1), custom_call_target="tpu_custom_call" | custom-call | tf_op jit(solution)/shard_map/prep/pallas_call | solution.py:325
  3.4 2.2 %collective-permute-start = (bf16[13,128,128]{2,1,0:T(8,128)(2,1)}, bf16[13,128,128]{2,1,0:T(8,128)(2,1)S(1)}, u32[]{:S(2)}, u32[]{:S(2)}) collective-permute-start(bf16[13,128,128]{2,1,0:T(8,128)(2,1)} %get-tuple-element.18), channel_id=1, source_target_pairs={{0,8},{8,16},{16,24},{24,32},{32,40},{40,48},{48,56},{56,64},{64,7... | collective-permute-start | bytes 1277960 | tf_op jit(solution)/shard_map/ppermute | solution.py:429
  5.6 6.8 %collective-permute-start.1 = (bf16[13,128,128]{2,1,0:T(8,128)(2,1)}, bf16[13,128,128]{2,1,0:T(8,128)(2,1)S(1)}, u32[]{:S(2)}, u32[]{:S(2)}) collective-permute-start(bf16[13,128,128]{2,1,0:T(8,128)(2,1)} %get-tuple-element.19), channel_id=1, source_target_pairs={{0,248},{8,0},{16,8},{24,16},{32,24},{40,32},{48,40},{56,48},{64,5... | collective-permute-start | bytes 1277960 | tf_op jit(solution)/shard_map/ppermute | solution.py:429
  12.4 3.9 %collective-permute-start.2 = (bf16[6,128,128]{2,1,0:T(8,128)(2,1)}, bf16[6,128,128]{2,1,0:T(8,128)(2,1)S(1)}, u32[]{:S(2)}, u32[]{:S(2)}) collective-permute-start(bf16[6,128,128]{2,1,0:T(8,128)(2,1)} %get-tuple-element.20), channel_id=1, source_target_pairs={{0,1},{1,2},{2,3},{3,4},{4,5},{5,6},{6,7},{8,9},{9,10},{10,11},{11... | collective-permute-start | bytes 589832 | tf_op jit(solution)/shard_map/ppermute | solution.py:429
  16.4 1.9 %collective-permute-start.3 = (bf16[6,128,128]{2,1,0:T(8,128)(2,1)}, bf16[6,128,128]{2,1,0:T(8,128)(2,1)S(1)}, u32[]{:S(2)}, u32[]{:S(2)}) collective-permute-start(bf16[6,128,128]{2,1,0:T(8,128)(2,1)} %get-tuple-element.21), channel_id=1, source_target_pairs={{1,0},{2,1},{3,2},{4,3},{5,4},{6,5},{7,6},{9,8},{10,9},{11,10},{12... | collective-permute-start | bytes 589832 | tf_op jit(solution)/shard_map/ppermute | solution.py:429
  19.0 3.8 %hold.1 = (bf16[26,11,128,128]{3,2,1,0:T(8,128)(2,1)S(1)}, f32[26,128,128]{2,1,0:T(8,128)S(1)}) custom-call(bf16[26,11,128,128]{3,2,1,0:T(8,128)(2,1)} %blocks_hbm.1, f32[26,128]{1,0:T(8,128)S(1)} %copy-done.1), custom_call_target="tpu_custom_call" | custom-call | bytes 18743296 | tf_op jit(solution)/shard_map/hold/pallas_call | solution.py:344
  22.8 0.8 collective-permute-done.3.halo3
  23.6 4.0 %product.2 = (f32[26,128,128]{2,1,0:T(8,128)S(1)}, bf16[13,128,128]{2,1,0:T(8,128)(2,1)S(1)}, bf16[13,128,128]{2,1,0:T(8,128)(2,1)S(1)}, bf16[6,128,128]{2,1,0:T(8,128)(2,1)S(1)}, bf16[6,128,128]{2,1,0:T(8,128)(2,1)S(1)}) custom-call(s32[11,26]{1,0:T(8,128)S(1)} %bitcast.2, s32[38]{0:T(128)S(1)} %copy-done.3, s32[1]{0:T(128)S(6)} %copy.8.count_ref, ...), custom_call_target="tpu_custom_call" | custom-call | tf_op jit(solution)/shard_map/product/pallas_call | solution.py:368
  27.7 4.8 %collective-permute-start.5 = (bf16[13,128,128]{2,1,0:T(8,128)(2,1)S(1)}, bf16[13,128,128]{2,1,0:T(8,128)(2,1)S(1)}, u32[]{:S(2)}, u32[]{:S(2)}) collective-permute-start(bf16[13,128,128]{2,1,0:T(8,128)(2,1)S(1)} %get-tuple-element.24), channel_id=1, source_target_pairs={{0,248},{8,0},{16,8},{24,16},{32,24},{40,32},{48,40},{56,48},{64,5... | collective-permute-start | bytes 1277960 | tf_op jit(solution)/shard_map/ppermute | solution.py:429
  32.5 3.2 %collective-permute-start.6 = (bf16[6,128,128]{2,1,0:T(8,128)(2,1)S(1)}, bf16[6,128,128]{2,1,0:T(8,128)(2,1)S(1)}, u32[]{:S(2)}, u32[]{:S(2)}) collective-permute-start(bf16[6,128,128]{2,1,0:T(8,128)(2,1)S(1)} %get-tuple-element.25), channel_id=1, source_target_pairs={{0,1},{1,2},{2,3},{3,4},{4,5},{5,6},{6,7},{8,9},{9,10},{10,11},{11... | collective-permute-start | bytes 589832 | tf_op jit(solution)/shard_map/ppermute | solution.py:429
  35.6 1.9 %collective-permute-start.7 = (bf16[6,128,128]{2,1,0:T(8,128)(2,1)S(1)}, bf16[6,128,128]{2,1,0:T(8,128)(2,1)S(1)}, u32[]{:S(2)}, u32[]{:S(2)}) collective-permute-start(bf16[6,128,128]{2,1,0:T(8,128)(2,1)S(1)} %get-tuple-element.26), channel_id=1, source_target_pairs={{1,0},{2,1},{3,2},{4,3},{5,4},{6,5},{7,6},{9,8},{10,9},{11,10},{12... | collective-permute-start | bytes 589832 | tf_op jit(solution)/shard_map/ppermute | solution.py:429
  37.6 1.3 %gram.1.refs_0_ = f32[80,128]{1,0:T(8,128)S(1)} custom-call(s32[1]{0:T(128)S(6)} %copy.8.count_ref, f32[26,128,128]{2,1,0:T(8,128)S(1)} %get-tuple-element.22.image_ref.current_ref), custom_call_target="tpu_custom_call" | custom-call | flops 109051904 | bytes 1703936 | tf_op jit(solution)/shard_map/gram/pallas_call | solution.py:385
  38.9 3.8 %collective-permute-done.7.halo3 = bf16[6,128,128]{2,1,0:T(8,128)(2,1)S(1)} collective-permute-done((bf16[6,128,128]{2,1,0:T(8,128)(2,1)S(1)}, bf16[6,128,128]{2,1,0:T(8,128)(2,1)S(1)}, u32[]{:S(2)}, u32[]{:S(2)}) %collective-permute-start.7) | collective-permute-done | bytes 196640 | tf_op jit(solution)/shard_map/ppermute | solution.py:429
  42.6 4.7 %product.3 = (f32[26,128,128]{2,1,0:T(8,128)S(1)}, f32[80,128]{1,0:T(8,128)S(1)}, f32[80,128]{1,0:T(8,128)S(1)}) custom-call(s32[11,26]{1,0:T(8,128)S(1)} %bitcast.3, s32[38]{0:T(128)S(1)} %copy-done.3, s32[1]{0:T(128)S(6)} %copy.8.count_ref, s32[1]{0:T(128)} %bitcast.core_ref, f32[26,128,128]{2,1,0:T(8,128)S(1)} %get-tuple-element.16.scale_ref, ...), custom_call_target="tpu_custom_call" | custom-call | tf_op jit(solution)/shard_map/product/pallas_call | solution.py:368
  47.4 1.2 %collective-permute-done.8 = f32[80,128]{1,0:T(8,128)S(1)} collective-permute-done((f32[80,128]{1,0:T(8,128)S(1)}, f32[80,128]{1,0:T(8,128)S(1)}, u32[]{:S(2)}, u32[]{:S(2)}) %collective-permute-start.8) | collective-permute-done | bytes 40992 | tf_op jit(solution)/shard_map/ppermute | solution.py:452
  48.6 1.0 %collective-permute-start.10 = (f32[80,128]{1,0:T(8,128)S(1)}, f32[80,128]{1,0:T(8,128)S(1)}, u32[]{:S(2)}, u32[]{:S(2)}) collective-permute-start(f32[80,128]{1,0:T(8,128)S(1)} %add.33), channel_id=1, source_target_pairs={{0,6},{1,7},{2,0},{3,1},{4,2},{5,3},{6,4},{7,5},{8,14},{9,15},{10,... | collective-permute-start | bytes 122888 | tf_op jit(solution)/shard_map/ppermute | solution.py:452
  49.6 0.5 collective-permute-start.9
  50.2 2.8 %collective-permute-done.11 = f32[80,128]{1,0:T(8,128)S(1)} collective-permute-done((f32[80,128]{1,0:T(8,128)S(1)}, f32[80,128]{1,0:T(8,128)S(1)}, u32[]{:S(2)}, u32[]{:S(2)}) %collective-permute-start.11) | collective-permute-done | bytes 40992 | tf_op jit(solution)/shard_map/ppermute | solution.py:452
  53.0 1.1 %collective-permute-done.9 = f32[80,128]{1,0:T(8,128)S(1)} collective-permute-done((f32[80,128]{1,0:T(8,128)S(1)}, f32[80,128]{1,0:T(8,128)S(1)}, u32[]{:S(2)}, u32[]{:S(2)}) %collective-permute-start.9) | collective-permute-done | bytes 40992 | tf_op jit(solution)/shard_map/ppermute | solution.py:452
  54.0 0.3 collective-permute-start.14
  54.6 1.3 %collective-permute-start.12 = (f32[80,128]{1,0:T(8,128)S(1)}, f32[80,128]{1,0:T(8,128)S(1)}, u32[]{:S(2)}, u32[]{:S(2)}) collective-permute-start(f32[80,128]{1,0:T(8,128)S(1)} %add_add_fusion.2), channel_id=1, source_target_pairs={{0,8},{1,9},{2,10},{3,11},{4,12},{5,13},{6,14},{7,15},{8,16},{9,17... | collective-permute-start | bytes 122888 | tf_op jit(solution)/shard_map/ppermute | solution.py:452
  55.9 2.8 %collective-permute-done.14 = f32[80,128]{1,0:T(8,128)S(1)} collective-permute-done((f32[80,128]{1,0:T(8,128)S(1)}, f32[80,128]{1,0:T(8,128)S(1)}, u32[]{:S(2)}, u32[]{:S(2)}) %collective-permute-start.14) | collective-permute-done | bytes 40992 | tf_op jit(solution)/shard_map/ppermute | solution.py:452
  58.7 0.4 collective-permute-done.12
  59.2 2.8 %collective-permute-done.15 = f32[80,128]{1,0:T(8,128)S(1)} collective-permute-done((f32[80,128]{1,0:T(8,128)S(1)}, f32[80,128]{1,0:T(8,128)S(1)}, u32[]{:S(2)}, u32[]{:S(2)}) %collective-permute-start.15) | collective-permute-done | bytes 40992 | tf_op jit(solution)/shard_map/ppermute | solution.py:468
  62.1 3.8 %collective-permute-start.18 = (f32[80,128]{1,0:T(8,128)S(1)}, f32[80,128]{1,0:T(8,128)S(1)}, u32[]{:S(2)}, u32[]{:S(2)}) collective-permute-start(f32[80,128]{1,0:T(8,128)S(1)} %add.40), channel_id=1, source_target_pairs={{0,128},{1,129},{2,130},{3,131},{4,132},{5,133},{6,134},{7,135},{8... | collective-permute-start | bytes 122888 | tf_op jit(solution)/shard_map/ppermute | solution.py:452
  65.9 5.4 %collective-permute-start.17 = (f32[80,128]{1,0:T(8,128)S(1)}, f32[80,128]{1,0:T(8,128)S(1)}, u32[]{:S(2)}, u32[]{:S(2)}) collective-permute-start(f32[80,128]{1,0:T(8,128)S(1)} %add.40), channel_id=1, source_target_pairs={{0,192},{1,193},{2,194},{3,195},{4,196},{5,197},{6,198},{7,199},{8... | collective-permute-start | bytes 122888 | tf_op jit(solution)/shard_map/ppermute | solution.py:452
  71.2 1.4 %collective-permute-done.17 = f32[80,128]{1,0:T(8,128)S(1)} collective-permute-done((f32[80,128]{1,0:T(8,128)S(1)}, f32[80,128]{1,0:T(8,128)S(1)}, u32[]{:S(2)}, u32[]{:S(2)}) %collective-permute-start.17) | collective-permute-done | bytes 40992 | tf_op jit(solution)/shard_map/ppermute | solution.py:452
  72.6 3.6 %collective-permute-done.16 = f32[80,128]{1,0:T(8,128)S(1)} collective-permute-done((f32[80,128]{1,0:T(8,128)S(1)}, f32[80,128]{1,0:T(8,128)S(1)}, u32[]{:S(2)}, u32[]{:S(2)}) %collective-permute-start.16) | collective-permute-done | bytes 40992 | tf_op jit(solution)/shard_map/ppermute | solution.py:452
  76.2 4.8 %factor.1.mine_ref = f32[128,256]{1,0:T(8,128)S(1)} custom-call(f32[80,128]{1,0:T(8,128)S(1)} %add_add_fusion.gram_ref), custom_call_target="tpu_custom_call" | custom-call | tf_op jit(solution)/shard_map/factor/pallas_call | solution.py:399
  81.0 6.2 %collective-permute-start.19 = (f32[128,256]{1,0:T(8,128)S(1)}, f32[128,256]{1,0:T(8,128)S(1)}, u32[]{:S(2)}, u32[]{:S(2)}) collective-permute-start(f32[128,256]{1,0:T(8,128)S(1)} %factor.1.mine_ref), channel_id=1, source_target_pairs={{0,1},{1,0},{2,3},{3,2},{4,5},{5,4},{6,7},{7,6},{8,9},{9,8},{10,11... | collective-permute-start | bytes 393224 | tf_op jit(solution)/shard_map/ppermute | solution.py:452
  87.1 1.0 %collective-permute-done.19.yours_ref = f32[128,256]{1,0:T(8,128)S(1)} collective-permute-done((f32[128,256]{1,0:T(8,128)S(1)}, f32[128,256]{1,0:T(8,128)S(1)}, u32[]{:S(2)}, u32[]{:S(2)}) %collective-permute-start.19) | collective-permute-done | bytes 131104 | tf_op jit(solution)/shard_map/ppermute | solution.py:452
  88.1 2.3 %last.1 = (f32[26,128,128]{2,1,0:T(8,128)}, f32[128,128]{1,0:T(8,128)}) custom-call(s32[1]{0:T(128)} %bitcast.core_ref, f32[128,256]{1,0:T(8,128)S(1)} %factor.1.mine_ref, f32[128,256]{1,0:T(8,128)S(1)} %collective-permute-done.19.yours_ref, f32[26,128,128]{2,1,0:T(8,128)S(1)} %get-tuple-element.29.image_ref), custom_call_target="tpu_custom_call" | custom-call | tf_op jit(solution)/shard_map/last/pallas_call | solution.py:411
  (28 shorter events, 0.6 us)
Async XLA Ops:
  0.6 18.3 %copy-start.1 = (f32[26,128]{1,0:T(8,128)S(1)}, f32[26,128]{1,0:T(8,128)}, u32[]{:S(2)}) copy-start(f32[26,128]{1,0:T(8,128)} %degree_hbm.1) | copy-start | bytes 39940
  3.4 20.2 %collective-permute-start = (bf16[13,128,128]{2,1,0:T(8,128)(2,1)}, bf16[13,128,128]{2,1,0:T(8,128)(2,1)S(1)}, u32[]{:S(2)}, u32[]{:S(2)}) collective-permute-start(bf16[13,128,128]{2,1,0:T(8,128)(2,1)} %get-tuple-element.18), channel_id=1, source_target_pairs={{0,8},{8,16},{16,24},{24,32},{32,40},{40,48},{48,56},{56,64},{64,7... | collective-permute-start | bytes 1277960 | tf_op jit(solution)/shard_map/ppermute | solution.py:429
  5.6 18.0 %collective-permute-start.1 = (bf16[13,128,128]{2,1,0:T(8,128)(2,1)}, bf16[13,128,128]{2,1,0:T(8,128)(2,1)S(1)}, u32[]{:S(2)}, u32[]{:S(2)}) collective-permute-start(bf16[13,128,128]{2,1,0:T(8,128)(2,1)} %get-tuple-element.19), channel_id=1, source_target_pairs={{0,248},{8,0},{16,8},{24,16},{32,24},{40,32},{48,40},{56,48},{64,5... | collective-permute-start | bytes 1277960 | tf_op jit(solution)/shard_map/ppermute | solution.py:429
  12.4 10.4 %collective-permute-start.2 = (bf16[6,128,128]{2,1,0:T(8,128)(2,1)}, bf16[6,128,128]{2,1,0:T(8,128)(2,1)S(1)}, u32[]{:S(2)}, u32[]{:S(2)}) collective-permute-start(bf16[6,128,128]{2,1,0:T(8,128)(2,1)} %get-tuple-element.20), channel_id=1, source_target_pairs={{0,1},{1,2},{2,3},{3,4},{4,5},{5,6},{6,7},{8,9},{9,10},{10,11},{11... | collective-permute-start | bytes 589832 | tf_op jit(solution)/shard_map/ppermute | solution.py:429
  16.4 7.2 %collective-permute-start.3 = (bf16[6,128,128]{2,1,0:T(8,128)(2,1)}, bf16[6,128,128]{2,1,0:T(8,128)(2,1)S(1)}, u32[]{:S(2)}, u32[]{:S(2)}) collective-permute-start(bf16[6,128,128]{2,1,0:T(8,128)(2,1)} %get-tuple-element.21), channel_id=1, source_target_pairs={{1,0},{2,1},{3,2},{4,3},{5,4},{6,5},{7,6},{9,8},{10,9},{11,10},{12... | collective-permute-start | bytes 589832 | tf_op jit(solution)/shard_map/ppermute | solution.py:429
  19.0 4.6 %copy-start = (f32[26,128,128]{2,1,0:T(8,128)S(1)}, f32[26,128,128]{2,1,0:T(8,128)}, u32[]{:S(2)}) copy-start(f32[26,128,128]{2,1,0:T(8,128)} %current_ref.1) | copy-start | bytes 5111812
  19.0 4.6 %copy-start.2 = (s32[26,11]{0,1:T(8,128)S(1)}, s32[26,11]{0,1:T(8,128)}, u32[]{:S(2)}) copy-start(s32[26,11]{0,1:T(8,128)} %param.7) | copy-start | bytes 3436
  19.0 4.6 %copy-start.3 = (s32[38]{0:T(128)S(1)}, s32[38]{0:T(128)}, u32[]{:S(2)}) copy-start(s32[38]{0:T(128)} %sends_ref.3) | copy-start | bytes 460
  27.6 15.0 %collective-permute-start.4 = (bf16[13,128,128]{2,1,0:T(8,128)(2,1)S(1)}, bf16[13,128,128]{2,1,0:T(8,128)(2,1)S(1)}, u32[]{:S(2)}, u32[]{:S(2)}) collective-permute-start(bf16[13,128,128]{2,1,0:T(8,128)(2,1)S(1)} %get-tuple-element.23), channel_id=1, source_target_pairs={{0,8},{8,16},{16,24},{24,32},{32,40},{40,48},{48,56},{56,64},{64,7... | collective-permute-start | bytes 1277960 | tf_op jit(solution)/shard_map/ppermute | solution.py:429
  27.7 14.9 %collective-permute-start.5 = (bf16[13,128,128]{2,1,0:T(8,128)(2,1)S(1)}, bf16[13,128,128]{2,1,0:T(8,128)(2,1)S(1)}, u32[]{:S(2)}, u32[]{:S(2)}) collective-permute-start(bf16[13,128,128]{2,1,0:T(8,128)(2,1)S(1)} %get-tuple-element.24), channel_id=1, source_target_pairs={{0,248},{8,0},{16,8},{24,16},{32,24},{40,32},{48,40},{56,48},{64,5... | collective-permute-start | bytes 1277960 | tf_op jit(solution)/shard_map/ppermute | solution.py:429
  32.5 6.4 %collective-permute-start.6 = (bf16[6,128,128]{2,1,0:T(8,128)(2,1)S(1)}, bf16[6,128,128]{2,1,0:T(8,128)(2,1)S(1)}, u32[]{:S(2)}, u32[]{:S(2)}) collective-permute-start(bf16[6,128,128]{2,1,0:T(8,128)(2,1)S(1)} %get-tuple-element.25), channel_id=1, source_target_pairs={{0,1},{1,2},{2,3},{3,4},{4,5},{5,6},{6,7},{8,9},{9,10},{10,11},{11... | collective-permute-start | bytes 589832 | tf_op jit(solution)/shard_map/ppermute | solution.py:429
  35.6 7.0 %collective-permute-start.7 = (bf16[6,128,128]{2,1,0:T(8,128)(2,1)S(1)}, bf16[6,128,128]{2,1,0:T(8,128)(2,1)S(1)}, u32[]{:S(2)}, u32[]{:S(2)}) collective-permute-start(bf16[6,128,128]{2,1,0:T(8,128)(2,1)S(1)} %get-tuple-element.26), channel_id=1, source_target_pairs={{1,0},{2,1},{3,2},{4,3},{5,4},{6,5},{7,6},{9,8},{10,9},{11,10},{12... | collective-permute-start | bytes 589832 | tf_op jit(solution)/shard_map/ppermute | solution.py:429
  47.3 1.3 %collective-permute-start.8 = (f32[80,128]{1,0:T(8,128)S(1)}, f32[80,128]{1,0:T(8,128)S(1)}, u32[]{:S(2)}, u32[]{:S(2)}) collective-permute-start(f32[80,128]{1,0:T(8,128)S(1)} %get-tuple-element.28), channel_id=1, source_target_pairs={{0,1},{1,0},{2,3},{3,2},{4,5},{5,4},{6,7},{7,6},{8,9},{9,8},{10,11... | collective-permute-start | bytes 122888 | tf_op jit(solution)/shard_map/ppermute | solution.py:452
  48.6 4.4 %collective-permute-start.11 = (f32[80,128]{1,0:T(8,128)S(1)}, f32[80,128]{1,0:T(8,128)S(1)}, u32[]{:S(2)}, u32[]{:S(2)}) collective-permute-start(f32[80,128]{1,0:T(8,128)S(1)} %add.33), channel_id=1, source_target_pairs={{0,4},{1,5},{2,6},{3,7},{4,0},{5,1},{6,2},{7,3},{8,12},{9,13},{10,... | collective-permute-start | bytes 122888 | tf_op jit(solution)/shard_map/ppermute | solution.py:452
  48.6 4.4 %collective-permute-start.10 = (f32[80,128]{1,0:T(8,128)S(1)}, f32[80,128]{1,0:T(8,128)S(1)}, u32[]{:S(2)}, u32[]{:S(2)}) collective-permute-start(f32[80,128]{1,0:T(8,128)S(1)} %add.33), channel_id=1, source_target_pairs={{0,6},{1,7},{2,0},{3,1},{4,2},{5,3},{6,4},{7,5},{8,14},{9,15},{10,... | collective-permute-start | bytes 122888 | tf_op jit(solution)/shard_map/ppermute | solution.py:452
  49.6 4.4 %collective-permute-start.9 = (f32[80,128]{1,0:T(8,128)S(1)}, f32[80,128]{1,0:T(8,128)S(1)}, u32[]{:S(2)}, u32[]{:S(2)}) collective-permute-start(f32[80,128]{1,0:T(8,128)S(1)} %add.33), channel_id=1, source_target_pairs={{0,2},{1,3},{2,4},{3,5},{4,6},{5,7},{6,0},{7,1},{8,10},{9,11},{10,... | collective-permute-start | bytes 122888 | tf_op jit(solution)/shard_map/ppermute | solution.py:452
  54.0 4.6 %collective-permute-start.14 = (f32[80,128]{1,0:T(8,128)S(1)}, f32[80,128]{1,0:T(8,128)S(1)}, u32[]{:S(2)}, u32[]{:S(2)}) collective-permute-start(f32[80,128]{1,0:T(8,128)S(1)} %add_add_fusion.2), channel_id=1, source_target_pairs={{0,16},{1,17},{2,18},{3,19},{4,20},{5,21},{6,22},{7,23},{8,24},{9,... | collective-permute-start | bytes 122888 | tf_op jit(solution)/shard_map/ppermute | solution.py:452
  54.3 4.4 %collective-permute-start.13 = (f32[80,128]{1,0:T(8,128)S(1)}, f32[80,128]{1,0:T(8,128)S(1)}, u32[]{:S(2)}, u32[]{:S(2)}) collective-permute-start(f32[80,128]{1,0:T(8,128)S(1)} %add_add_fusion.2), channel_id=1, source_target_pairs={{0,24},{1,25},{2,26},{3,27},{4,28},{5,29},{6,30},{7,31},{8,0},{9,1... | collective-permute-start | bytes 122888 | tf_op jit(solution)/shard_map/ppermute | solution.py:452
  54.6 4.5 %collective-permute-start.12 = (f32[80,128]{1,0:T(8,128)S(1)}, f32[80,128]{1,0:T(8,128)S(1)}, u32[]{:S(2)}, u32[]{:S(2)}) collective-permute-start(f32[80,128]{1,0:T(8,128)S(1)} %add_add_fusion.2), channel_id=1, source_target_pairs={{0,8},{1,9},{2,10},{3,11},{4,12},{5,13},{6,14},{7,15},{8,16},{9,17... | collective-permute-start | bytes 122888 | tf_op jit(solution)/shard_map/ppermute | solution.py:452
  59.1 2.9 %collective-permute-start.15 = (f32[80,128]{1,0:T(8,128)S(1)}, f32[80,128]{1,0:T(8,128)S(1)}, u32[]{:S(2)}, u32[]{:S(2)}) collective-permute-start(f32[80,128]{1,0:T(8,128)S(1)} %add_add_fusion.1), channel_id=1, source_target_pairs={{0,32},{1,33},{2,34},{3,35},{4,36},{5,37},{6,38},{7,39},{8,40},{9,... | collective-permute-start | bytes 122888 | tf_op jit(solution)/shard_map/ppermute | solution.py:468
  62.1 9.1 %collective-permute-start.18 = (f32[80,128]{1,0:T(8,128)S(1)}, f32[80,128]{1,0:T(8,128)S(1)}, u32[]{:S(2)}, u32[]{:S(2)}) collective-permute-start(f32[80,128]{1,0:T(8,128)S(1)} %add.40), channel_id=1, source_target_pairs={{0,128},{1,129},{2,130},{3,131},{4,132},{5,133},{6,134},{7,135},{8... | collective-permute-start | bytes 122888 | tf_op jit(solution)/shard_map/ppermute | solution.py:452
  65.9 6.7 %collective-permute-start.17 = (f32[80,128]{1,0:T(8,128)S(1)}, f32[80,128]{1,0:T(8,128)S(1)}, u32[]{:S(2)}, u32[]{:S(2)}) collective-permute-start(f32[80,128]{1,0:T(8,128)S(1)} %add.40), channel_id=1, source_target_pairs={{0,192},{1,193},{2,194},{3,195},{4,196},{5,197},{6,198},{7,199},{8... | collective-permute-start | bytes 122888 | tf_op jit(solution)/shard_map/ppermute | solution.py:452
  71.2 5.0 %collective-permute-start.16 = (f32[80,128]{1,0:T(8,128)S(1)}, f32[80,128]{1,0:T(8,128)S(1)}, u32[]{:S(2)}, u32[]{:S(2)}) collective-permute-start(f32[80,128]{1,0:T(8,128)S(1)} %add.40), channel_id=1, source_target_pairs={{0,64},{1,65},{2,66},{3,67},{4,68},{5,69},{6,70},{7,71},{8,72},{9,... | collective-permute-start | bytes 122888 | tf_op jit(solution)/shard_map/ppermute | solution.py:452
  81.0 7.1 %collective-permute-start.19 = (f32[128,256]{1,0:T(8,128)S(1)}, f32[128,256]{1,0:T(8,128)S(1)}, u32[]{:S(2)}, u32[]{:S(2)}) collective-permute-start(f32[128,256]{1,0:T(8,128)S(1)} %factor.1.mine_ref), channel_id=1, source_target_pairs={{0,1},{1,0},{2,3},{3,2},{4,5},{5,4},{6,7},{7,6},{8,9},{9,8},{10,11... | collective-permute-start | bytes 393224 | tf_op jit(solution)/shard_map/ppermute | solution.py:452
